TPU v7x, 32 devices: a whole 2x2x4 slice. The times are simulated.
32 devices in a mesh: coil: 4 (over x, core), tile: 8 (over z, y).
Axes of the slice: x: 2, y: 2, z: 4, core: 2. Of those that a mesh axis runs over, the one named last changes fastest.
Arguments:
- image_p: float32 [2, 128, 128, 128], P(None, 'tile', 'coil'), may hold values from -6 to 6
- image_x: float32 [2, 128, 128, 128], P(None, 'tile', 'coil'), may hold values from -6 to 6
- image_r: float32 [2, 128, 128, 128], P(None, 'tile', 'coil'), may hold values from -6 to 6
- sensitivity: float32 [4, 2, 128, 128, 128], P('coil', None, 'tile'), may hold values from -5 to 5
- kb_weights: float32 [256, 3, 4, 128], P('tile'), may hold values from -3 to 3
- block_owner: int32 [256], P('tile'), may hold values from 0 to 7, as said below
- owner_list: int32 [3, 8, 8, 16], P(None, 'tile'), may hold values from -1 to 124, as said below
Outputs:
- next_x: float32 [2, 128, 128, 128], P(None, 'tile', 'coil')
- next_r: float32 [2, 128, 128, 128], P(None, 'tile', 'coil')
- next_p: float32 [2, 128, 128, 128], P(None, 'tile', 'coil')
Inputs may be any that keep to these rules, and one draw needn't show every extreme that they name: `block_owner`: of the 32 blocks handled by one index of tile (blocks h * 32 to h * 32 + 31), at most 16 have any one owner; in every draw each such device has exactly 16 blocks of one common owner. owner_list[:, o, h, k] holds the offsets (kx, ky within tile o, kz) of the block of rank k among the blocks of device h whose owner is o, in the order of their slots; all three are -1 where there is no such block. Offsets place the whole box inside the grid and inside tile o.
All inputs are finite; a program needn't handle non-finite values.
Results may differ from a plain program's by a relative error of at most 0.0002.
Values sent between devices are 32-bit elements; how exact they have to be, the bound alone decides.
No kernel may reach another device: no remote copies, remote signals or barrier semaphores. Data moves between devices by JAX's collectives and lax.ppermute only.
A program may use at most 256 MiB of HBM per device.

v0:
```python
import functools
import math

import jax
import jax.numpy as jnp
import ml_dtypes
import numpy as np
from jax import lax
from jax.experimental import pallas as pl
from jax.experimental.pallas import tpu as pltpu
from jax.sharding import PartitionSpec as P

LANES = 128
VMEM = 24 * 1024 * 1024


def halves(values):
    high = values.astype(jnp.bfloat16)
    low = (values - high.astype(jnp.float32)).astype(jnp.bfloat16)
    return high, low


def dot_bf16(left, right, dims):
    return lax.dot_general(left, right, (dims, ((), ())), preferred_element_type=jnp.float32)


def dot_left(table, values, dims=((1,), (0,))):
    high, low = halves(values)
    return (
        dot_bf16(table[0], high, dims)
        + dot_bf16(table[0], low, dims)
        + dot_bf16(table[1], high, dims)
    )


def dot_right(values, table, dims=((1,), (0,))):
    high, low = halves(values)
    return (
        dot_bf16(high, table[0], dims)
        + dot_bf16(low, table[0], dims)
        + dot_bf16(high, table[1], dims)
    )


def fourier_tables(length):
    cells = np.arange(length)
    angle = 2.0 * math.pi / length * (cells[:, None] * cells[None, :] % length)
    cos_t = np.cos(angle) / math.sqrt(length)
    sin_t = np.sin(angle) / math.sqrt(length)
    found = []
    for sign in (1.0, -1.0):
        whole = np.block([[cos_t, -sign * sin_t], [sign * sin_t, cos_t]])
        high = whole.astype(ml_dtypes.bfloat16)
        low = (whole - high.astype(np.float64)).astype(ml_dtypes.bfloat16)
        found += [high, low]
    return jnp.asarray(np.stack(found))


def band_of_lane(planes, chunk):
    return lax.broadcasted_iota(jnp.int32, (4, LANES), 1) // planes % chunk


def in_window(band, first, chunk):
    past = band - first
    if chunk == 4:
        here = past >= 0
        return here, jnp.logical_not(here)
    here = jnp.logical_and(past >= 0, past < 4)
    return here, past < 4 - chunk


def call(kernel, outs, scratch, operands, smem, flops, name, hbm=(), limit=VMEM):
    specs = [pl.BlockSpec(memory_space=pltpu.SMEM)] * smem
    specs += [pl.BlockSpec(memory_space=pltpu.VMEM)] * (len(operands) - smem)
    for at in hbm:
        specs[at] = pl.BlockSpec(memory_space=pltpu.HBM)
    moved = sum(math.prod(a.shape) * a.dtype.itemsize for a in operands)
    return pl.pallas_call(
        kernel,
        out_shape=[jax.ShapeDtypeStruct(shape, jnp.float32) for shape in outs],
        in_specs=specs,
        out_specs=[pl.BlockSpec(memory_space=pltpu.VMEM)] * len(outs),
        scratch_shapes=[
            pltpu.VMEM(shape, jnp.float32) if isinstance(shape, tuple) else shape
            for shape in scratch
        ],
        compiler_params=pltpu.CompilerParams(vmem_limit_bytes=limit),
        cost_estimate=pl.CostEstimate(flops=flops, bytes_accessed=moved, transcendentals=0),
        name=name,
    )(*operands)


def z_of_coil(p_ref, s_ref, out_ref, rows, table):
    _, planes, part, length = p_ref.shape
    batch = min(planes, 256 // part)
    for base in range(0, planes, batch):
        bands = []
        for plane in range(base, base + batch):
            s_re = s_ref[0, plane, rows, :]
            s_im = s_ref[1, plane, rows, :]
            p_re = p_ref[0, plane]
            p_im = p_ref[1, plane]
            bands.append(
                jnp.concatenate([s_re * p_re - s_im * p_im, s_re * p_im + s_im * p_re], axis=1)
            )
        done = dot_right(jnp.concatenate(bands, axis=0), table)
        for ri in range(2):
            half = done[:, ri * length : (ri + 1) * length]
            out_ref[ri, base : base + batch] = half.reshape(batch, part, length)


def quarter(starts, at, part):
    return pl.ds(pl.multiple_of(starts[at], part), part)


def coil_z_kernel(starts, *refs, quarters, sends):
    count = len(quarters)
    p_refs = refs[:count]
    s_ref, table_ref = refs[count : count + 2]
    outs = refs[count + 2 :]
    part = p_refs[0].shape[2]
    table = (table_ref[0], table_ref[1])
    for at in range(count):
        z_of_coil(p_refs[at], s_ref, outs[at], quarter(starts, quarters[at], part), table)
    chips = sends + 1
    for by in range(1, chips):
        hop = chips - by
        for half in range(2):
            rows = quarter(starts, half * chips + hop, part)
            to = quarter(starts, 2 * chips + half, part)
            for ri in range(2):
                outs[count + by - 1][ri, :, to, :] = s_ref[ri, :, rows, :]


def coil_z(starts, pieces, quarters, smap, tables, sends=0):
    _, planes, part, length = pieces[0].shape
    count = len(pieces)
    return call(
        functools.partial(coil_z_kernel, quarters=quarters, sends=sends),
        [pieces[0].shape] * count + [(2, planes, 2 * part, length)] * sends,
        [],
        [starts, *pieces, smap, tables],
        1,
        count * planes * part * 24 * length * length,
        "coil_z",
    )


def cut_boxes(info, grid, cos_ref, sin_ref, shift_ref, out_ref, gbuf, planes, chunk, slots):
    handlers = out_ref.shape[0]
    band = band_of_lane(planes, chunk)

    def cut(handler, carry):
        base = pl.multiple_of(handler * LANES, LANES)
        for slot in range(slots):
            block = handler * slots + slot
            here, after = in_window(band, info[1, block], chunk)
            first = grid[pl.ds(info[0, block], 4), :]
            second = grid[pl.ds(info[0, block] + LANES, 4), :]
            if chunk > 4:
                second = jnp.where(after, second, 0.0)
            gbuf[pl.ds(base + slot, 4, stride=slots), :] = jnp.where(here, first, second)
        return carry

    lax.fori_loop(0, handlers, cut, 0)
    high, low = halves(shift_ref[...])
    table = jnp.concatenate(
        [
            jnp.concatenate([high, high], axis=1),
            jnp.concatenate([low, jnp.zeros_like(low)], axis=1),
        ],
        axis=0,
    )
    for handler in range(handlers):
        rows = slice(handler * slots, (handler + 1) * slots)
        cos_b = jnp.concatenate([cos_ref[rows, :]] * 4, axis=0)
        sin_b = jnp.concatenate([sin_ref[rows, :]] * 4, axis=0)
        cells = gbuf[handler * LANES : (handler + 1) * LANES, :]
        turned = cells * cos_b + pltpu.roll(cells, LANES // 2, 1) * sin_b
        both = dot_bf16(table, jnp.concatenate(halves(turned), axis=1), ((1,), (1,)))
        out_ref[handler] = both[:32] + both[32:]


def forward_kernel(info, starts, *refs, done, pieces, planes, part, length, chunk, slots):
    t_refs = refs[:done]
    p_refs = refs[done:pieces]
    s_ref, table_ref, cos_ref, sin_ref, shift_ref = refs[pieces : pieces + 5]
    out_ref, natural, ybuf, grid, gbuf, late = refs[pieces + 5 :]
    rows = length * planes
    table = (table_ref[0], table_ref[1])
    for at in range(done, pieces):
        z_of_coil(p_refs[at - done], s_ref, late.at[at - done], quarter(starts, at, part), table)
    for at in range(pieces):
        to = quarter(starts, at, part)
        source = t_refs[at] if at < done else late.at[at - done]
        for ri in range(2):
            natural[ri, :, to, :] = source[ri]
    table = (table_ref[2], table_ref[3])
    for pair in range(planes // 2):
        columns = [
            jnp.concatenate([natural[0, plane], natural[1, plane]], axis=0)
            for plane in (2 * pair, 2 * pair + 1)
        ]
        both = dot_left(table, jnp.concatenate(columns, axis=1))
        for inner in range(2):
            for ri in range(2):
                ybuf[pl.ds(ri * rows + 2 * pair + inner, length, stride=planes), :] = both[
                    ri * length : (ri + 1) * length, inner * LANES : (inner + 1) * LANES
                ]
    for band in range(length // chunk):
        re = ybuf[band * 64 : (band + 1) * 64, :]
        im = ybuf[rows + band * 64 : rows + (band + 1) * 64, :]
        grid[band * length : (band + 1) * length, :] = jnp.concatenate([re, im], axis=0).T
    cut_boxes(info, grid, cos_ref, sin_ref, shift_ref, out_ref, gbuf, planes, chunk, slots)


def forward(info, starts, done, rest, smap, tables, phases, shift, chunk, slots):
    _, planes, part, length = done[0].shape
    pieces = len(done) + len(rest)
    handlers = info.shape[1] // slots
    kernel = functools.partial(
        forward_kernel, done=len(done), pieces=pieces, planes=planes, part=part, length=length,
        chunk=chunk, slots=slots,
    )
    return call(
        kernel,
        [(handlers, 32, LANES)],
        [
            (2, planes, length, length),
            (2 * length * planes, length),
            (length * (length // chunk + 1), LANES),
            (handlers * LANES, LANES),
            (len(rest), 2, planes, part, length),
        ],
        [info, starts, *done, *rest, smap, tables, *phases, shift],
        2,
        48 * planes * length**3,
        "forward",
    )[0]


def regrid_kernel(parts_ref, matrix_ref, out_ref, held, done_sem):
    total = parts_ref[0]
    for at in range(1, parts_ref.shape[0]):
        total = total + parts_ref[at]
    along = lax.broadcasted_iota(jnp.int32, (8, LANES), 0) % 4
    sums = [jnp.zeros((8, LANES), jnp.float32) for _ in range(4)]
    for source in range(4):
        for d_z in range(4):
            value = total[8 * source : 8 * source + 8]
            if d_z:
                value = pltpu.roll(value, LANES - 32 * d_z, 1)
            for d_x in range(4):
                moved = value
                if d_x:
                    moved = jnp.where(
                        along + d_x < 4, pltpu.roll(value, 8 - d_x, 0), pltpu.roll(value, 4 - d_x, 0)
                    )
                for e in range(4):
                    at = 8 * (((e * 4 + source) * 4 + d_z) * 4 + d_x)
                    sums[e] = sums[e] + matrix_ref[at : at + 8] * moved
    done = jnp.concatenate(sums, axis=0)
    for at in range(held.shape[0]):
        held[at] = done
    copy = pltpu.make_async_copy(held, out_ref, done_sem)
    copy.start()
    copy.wait()


def regrid(parts, matrix, copies):
    shape = (copies,) + parts.shape[1:]
    return pl.pallas_call(
        regrid_kernel,
        out_shape=jax.ShapeDtypeStruct(shape, jnp.float32),
        in_specs=[pl.BlockSpec(memory_space=pltpu.VMEM)] * 2,
        out_specs=pl.BlockSpec(memory_space=pltpu.HBM),
        scratch_shapes=[pltpu.VMEM(shape, jnp.float32), pltpu.SemaphoreType.DMA],
        compiler_params=pltpu.CompilerParams(vmem_limit_bytes=VMEM // 2),
        cost_estimate=pl.CostEstimate(flops=10**7, bytes_accessed=10**6, transcendentals=0),
        name="regrid",
    )(parts, matrix)


def place_boxes(info, chip, u_ref, cos_ref, sin_ref, shift_ref, outs, gbufs, planes, chunk, slots):
    chips = len(outs)
    handlers = u_ref.shape[0] // chips
    high, low = halves(shift_ref[...])
    table = jnp.concatenate([high, high, low, jnp.zeros_like(low)], axis=0)
    for handler in range(handlers):
        rows = slice(handler * slots, (handler + 1) * slots)
        cos_b = jnp.concatenate([cos_ref[rows, :]] * 4, axis=0)
        sin_b = jnp.concatenate([sin_ref[rows, :]] * 4, axis=0)
        for hop in range(chips):
            u_hi, u_lo = (
                half.astype(jnp.float32) for half in halves(u_ref[chip[hop] * handlers + handler])
            )
            stack = jnp.concatenate([u_hi, u_lo, u_hi, jnp.zeros_like(u_hi)], axis=0)
            cells = dot_bf16(stack.T.astype(jnp.bfloat16), table, ((1,), (0,)))
            turned = cells * cos_b - pltpu.roll(cells, LANES // 2, 1) * sin_b
            gbufs[hop][handler * LANES : (handler + 1) * LANES, :] = turned
    for out in outs:
        out[...] = jnp.zeros_like(out)
    band = band_of_lane(planes, chunk)

    def put(handler, carry):
        base = pl.multiple_of(handler * LANES, LANES)
        for slot in range(slots):
            block = handler * slots + slot
            here, after = in_window(band, info[1, block], chunk)
            first = pl.ds(info[0, block], 4)
            second = pl.ds(info[0, block] + LANES, 4)
            for hop in range(chips):
                cells = gbufs[hop][pl.ds(base + slot, 4, stride=slots), :]
                old_first = outs[hop][first, :]
                old_second = outs[hop][second, :]
                outs[hop][first, :] = old_first + jnp.where(here, cells, 0.0)
                outs[hop][second, :] = old_second + jnp.where(after, cells, 0.0)
        return carry

    lax.fori_loop(0, handlers, put, 0)


def inverse_kernel(
    info, chip, quarters, u_ref, cos_ref, sin_ref, shift_ref, s_ref, table_ref, *refs,
    planes, part, length, chunk, slots, chips
):
    far_maps = refs[: chips - 1]
    outs = refs[chips - 1 : chips + 1]
    refs = refs[chips + 1 :]
    grids, gbufs, refs = refs[:chips], refs[chips : 2 * chips], refs[2 * chips :]
    ybuf, images, maps, sems = refs
    copies = [
        pltpu.make_async_copy(far_maps[at], maps.at[at], sems.at[at]) for at in range(chips - 1)
    ]
    for copy in copies:
        copy.start()
    place_boxes(info, chip, u_ref, cos_ref, sin_ref, shift_ref, grids, gbufs, planes, chunk, slots)
    rows = length * planes
    own = length // chips
    table = []
    for half in range(2):
        bands = [
            table_ref[half, pl.ds(pl.multiple_of(ri * length + chip[0] * own, own), own), :]
            for ri in range(2)
        ]
        table.append(jnp.concatenate(bands, axis=0))
    for hop in range(chips):
        for band in range(length // chunk):
            tile = grids[hop][band * length : (band + 1) * length, :].T
            ybuf[hop, band * 64 : (band + 1) * 64, :] = tile[:64]
            ybuf[hop, rows + band * 64 : rows + (band + 1) * 64, :] = tile[64:]
        for pair in range(planes // 2):
            columns = [
                jnp.concatenate(
                    [
                        ybuf[hop, pl.ds(ri * rows + plane, length, stride=planes), :]
                        for ri in range(2)
                    ],
                    axis=0,
                )
                for plane in (2 * pair, 2 * pair + 1)
            ]
            done = dot_left(table, jnp.concatenate(columns, axis=1))
            for inner in range(2):
                for ri in range(2):
                    images[hop, ri, 2 * pair + inner] = done[
                        ri * own : (ri + 1) * own, inner * LANES : (inner + 1) * LANES
                    ]
    for copy in copies:
        copy.wait()
    table = (table_ref[2], table_ref[3])
    batch = min(planes, 256 // part)
    for at in range(2):
        local = pl.ds(pl.multiple_of(quarters[2 + at], part), part)
        whole = pl.ds(pl.multiple_of(quarters[at], part), part)
        for base in range(0, planes, batch):
            total_re, total_im = 0.0, 0.0
            for hop in range(chips):
                bands = [
                    jnp.concatenate([images[hop, ri, plane, local, :] for ri in range(2)], axis=1)
                    for plane in range(base, base + batch)
                ]
                done = dot_right(jnp.concatenate(bands, axis=0), table)
                i_re = done[:, :length].reshape(batch, part, length)
                i_im = done[:, length:].reshape(batch, part, length)
                if hop:
                    s_re = maps[hop - 1, 0, base : base + batch, local, :]
                    s_im = maps[hop - 1, 1, base : base + batch, local, :]
                else:
                    s_re = s_ref[0, base : base + batch, whole, :]
                    s_im = s_ref[1, base : base + batch, whole, :]
                total_re = total_re + (s_re * i_re + s_im * i_im)
                total_im = total_im + (s_re * i_im - s_im * i_re)
            outs[at][0, base : base + batch] = total_re
            outs[at][1, base : base + batch] = total_im


def inverse(info, chip_order, quarters, spread, phases, shift, smap, tables, far_maps, part, chunk, slots):
    _, planes, length, _ = smap.shape
    chips = len(far_maps) + 1
    handlers = info.shape[1] // slots
    rows = length * (length // chunk + 1)
    kernel = functools.partial(
        inverse_kernel, planes=planes, part=part, length=length, chunk=chunk, slots=slots,
        chips=chips,
    )
    return call(
        kernel,
        [(2, planes, part, length)] * 2,
        [(rows, LANES)] * chips
        + [(handlers * LANES, LANES)] * chips
        + [
            (chips, 2 * length * planes, length),
            (chips, 2, planes, 2 * part, length),
            (chips - 1, 2, planes, 2 * part, length),
            pltpu.SemaphoreType.DMA((chips - 1,)),
        ],
        [info, chip_order, quarters, spread, *phases, shift, smap, tables, *far_maps],
        3,
        48 * planes * length**3,
        "inverse",
        hbm=range(9, 9 + chips - 1),
    )


def sums_kernel(*refs, terms):
    term_refs = refs[:terms]
    p_ref, r_ref, normal_ref, out_ref = refs[terms:]
    shape = p_ref.shape

    def add(plane, held):
        held = list(held)
        for ri in range(2):
            normal = term_refs[0][ri, plane]
            for term in term_refs[1:]:
                normal = normal + term[ri, plane]
            normal_ref[ri, plane] = normal
            p = p_ref[ri, plane]
            r = r_ref[ri, plane]
            for at, product in enumerate((r * r, p * normal, r * normal, normal * normal)):
                held[at] = held[at] + jnp.sum(product.reshape(-1, 8, LANES), axis=0)
        return tuple(held)

    start = tuple(jnp.zeros((8, LANES), jnp.float32) for _ in range(4))
    held = lax.fori_loop(0, shape[1], add, start, unroll=4)
    lane = lax.broadcasted_iota(jnp.int32, out_ref.shape, 1)
    found = jnp.zeros(out_ref.shape, jnp.float32)
    for at in range(4):
        found = jnp.where(lane == at, jnp.sum(held[at]), found)
    out_ref[...] = found


def sums(terms, p, r, devices):
    kernel = functools.partial(sums_kernel, terms=len(terms))
    return call(kernel, [p.shape, (devices, LANES)], [], [*terms, p, r], 0, 10**7, "sums")


def finish_kernel(total_ref, x_ref, r_ref, p_ref, normal_ref, x_out, r_out, p_out):
    total = jnp.sum(total_ref[...], axis=0, keepdims=True)
    r_r, p_n, r_n, n_n = (total[:, at : at + 1] for at in range(4))
    alpha = r_r / p_n
    beta = (r_r + alpha * (alpha * n_n - 2.0 * r_n)) / r_r
    for plane in range(x_ref.shape[1]):
        for ri in range(2):
            p = p_ref[ri, plane]
            next_r = r_ref[ri, plane] - alpha * normal_ref[ri, plane]
            x_out[ri, plane] = x_ref[ri, plane] + alpha * p
            r_out[ri, plane] = next_r
            p_out[ri, plane] = next_r + beta * p


def finish(total, x, r, p, normal):
    return call(finish_kernel, [x.shape] * 3, [], [total, x, r, p, normal], 0, 10**7, "finish")


def matrices_kernel(info, tile, weights_ref, out_ref, held, *, slots):
    def one(block, carry):
        w_x = weights_ref[block, 0]
        w_y = weights_ref[block, 1]
        w_z = weights_ref[block, 2]
        twice = jnp.concatenate([w_x, w_x], axis=0)
        rolled = [twice] + [pltpu.roll(twice, 8 - d, 0) for d in range(1, 4)]
        low = lax.broadcasted_iota(jnp.int32, (8, LANES), 0) < 4
        along_x = [twice * jnp.where(low, rolled[d], rolled[d + 1]) for d in (0, 2)]
        right = []
        for f in range(4):
            for d_z in range(4):
                other = (f + d_z) % 4
                along_z = w_z[f : f + 1] * w_z[other : other + 1]
                right += [along * along_z for along in along_x]
        turned = pltpu.roll(
            jnp.concatenate([w_y, w_y], axis=0), info[1, tile[0] * slots + block] % 4, 0
        )[:4]
        left = jnp.concatenate([turned * turned[e : e + 1] for e in range(4)], axis=0)
        done = dot_right(left, halves(jnp.concatenate(right, axis=0)), ((1,), (1,)))
        for f in range(4):
            lanes = done[:, f // 2 * LANES : (f // 2 + 1) * LANES]
            if f % 2:
                lanes = pltpu.roll(lanes, LANES // 2, 1)
            held[pl.ds(f * slots + block, 16, stride=LANES), :] = lanes
        return carry

    lax.fori_loop(0, slots, one, 0, unroll=4)

    def turn(pair, carry):
        at = pl.ds(pl.multiple_of(pair * LANES, LANES), LANES)
        rows = held[at, :].T
        for group in range(16):
            four = rows[4 * group : 4 * group + 4]
            out_ref[pl.ds(pl.multiple_of(pair * LANES + 8 * group, 8), 8), :] = jnp.concatenate(
                [four, four], axis=0
            )
        return carry

    lax.fori_loop(0, 16, turn, 0, unroll=2)


def block_matrices(info, tile, weights):
    slots = weights.shape[0]
    return call(
        functools.partial(matrices_kernel, slots=slots),
        [(16 * LANES, LANES)],
        [(16 * LANES, LANES)],
        [info, tile, weights],
        2,
        10**9,
        "matrices",
    )[0]


def block_offsets(gathered, slots, ntile, capacity):
    owners = gathered[:, :slots]
    lists = gathered[:, slots:].reshape(ntile, 3, ntile, capacity)
    earlier = jnp.tril(jnp.ones((slots, slots), jnp.int32), -1)
    same = (owners[:, :, None] == owners[:, None, :]).astype(jnp.int32)
    ranks = jnp.sum(same * earlier[None], axis=2)
    wanted = owners * capacity + ranks
    lists = jnp.transpose(lists, (1, 2, 0, 3)).reshape(3, ntile, 1, ntile * capacity)
    hit = wanted[:, :, None] == jnp.arange(ntile * capacity, dtype=jnp.int32)
    found = jnp.sum(jnp.where(hit[None], lists, 0), axis=3)
    return found[0], found[1] + owners * (LANES // ntile), found[2]


def shards(image_p, image_x, image_r, sensitivity, kb_weights, block_owner, owner_list):
    ntile = lax.axis_size("tile")
    ncoil = lax.axis_size("coil")
    chips = ncoil // 2
    slots = kb_weights.shape[0]
    capacity = owner_list.shape[3]
    planes, length = image_p.shape[1], image_p.shape[3]
    part = image_p.shape[2]
    chunk = LANES // (2 * planes)
    tile = lax.axis_index("tile")
    coil = lax.axis_index("coil")
    chip, core = coil // 2, coil % 2
    smap = sensitivity[0]
    tables = fourier_tables(length)

    def from_chip(values, by):
        pairs = [
            (a * 2 + k, (a - by) % chips * 2 + k) for a in range(chips) for k in range(2)
        ]
        return lax.ppermute(values, "coil", pairs)

    def other_core(values):
        pairs = [(a * 2 + k, a * 2 + 1 - k) for a in range(chips) for k in range(2)]
        return lax.ppermute(values, "coil", pairs)

    hops = jnp.arange(chips, dtype=jnp.int32)
    chip_order = (chip + hops) % chips
    starts = jnp.concatenate(
        [(chip_order * 2 + at) * part for at in (core, 1 - core)]
        + [jnp.stack([core * part, (1 - core) * part])]
    )

    p_same = [image_p] + [from_chip(image_p, by) for by in range(1, chips)]
    p_other = [other_core(piece) for piece in p_same]
    mine = jnp.concatenate([block_owner, owner_list[:, 0].reshape(-1)])
    gathered = lax.all_to_all(
        jnp.broadcast_to(mine[None], (ntile, mine.shape[0])), "tile", 0, 0, tiled=True
    )
    near = coil_z(starts, [p_same[0], p_other[0]], [0, chips], smap, tables)
    far = coil_z(starts, p_same[1:], list(range(1, chips)), smap, tables, chips - 1)
    far_maps = [from_chip(rows, by) for by, rows in enumerate(far[chips - 1 :], 1)]
    gathered, near = lax.optimization_barrier((gathered, near))

    off_x, off_y, off_z = block_offsets(gathered, slots, ntile, capacity)
    info = jnp.stack(
        [(off_y // chunk * length + off_z).reshape(-1), (off_y % chunk).reshape(-1)]
    )
    lane = jnp.arange(LANES, dtype=jnp.int32)
    lane_ri = lane // (LANES // 2)
    lane_q = lane // planes % chunk
    lane_x = lane % planes + tile * planes
    unit = 2.0 * math.pi / length
    angle = unit * (off_x.reshape(-1, 1) * lane_x[None] % length).astype(jnp.float32)
    phases = (jnp.cos(angle), jnp.sin(angle) * jnp.where(lane_ri == 0, 1.0, -1.0)[None])
    row = jnp.arange(32, dtype=jnp.int32)[:, None]
    row_q, row_ri, row_i = row // 8, row // 4 % 2, row % 4
    angle = unit * (row_i * lane_x[None] % length).astype(jnp.float32)
    sine = jnp.where(row_ri == 0, 1.0, -1.0) * jnp.sin(angle)
    shift = jnp.where(row_ri == lane_ri[None], jnp.cos(angle), sine)
    shift = jnp.where(lane_q[None] % 4 == row_q, shift / math.sqrt(length), 0.0)
    done = [near[0], *far[: chips - 1], near[1]]
    partial = forward(
        info, starts[: 2 * chips], done, p_other[1:], smap, tables, phases, shift, chunk, slots
    )
    partial, weights = lax.optimization_barrier((partial, kb_weights))
    parts = lax.all_to_all(partial, "tile", 0, 0, tiled=True)
    done = regrid(parts, block_matrices(info, tile[None], weights), chips * ntile)
    groups = [
        [at * ntile + t for at in range(ncoil) if at % 2 == k for t in range(ntile)]
        for k in range(2)
    ]
    spread = lax.all_to_all(
        done, ("coil", "tile"), 0, 0, axis_index_groups=groups, tiled=True
    )
    quarters = jnp.stack([chip * 2 + 1 - core, chip * 2 + core, 1 - core, core]) * part
    sent, kept = inverse(
        info, chip_order, quarters, spread, phases, shift, smap, tables, far_maps, part, chunk,
        slots,
    )
    normal, found = sums([kept, other_core(sent)], image_p, image_r, ncoil * ntile)
    total = lax.all_to_all(found, ("coil", "tile"), 0, 0, tiled=True)
    return tuple(finish(total, image_x, image_r, image_p, normal))


def solution(mesh):
    return jax.shard_map(
        shards,
        mesh=mesh,
        in_specs=(
            P(None, "tile", "coil", None),
            P(None, "tile", "coil", None),
            P(None, "tile", "coil", None),
            P("coil", None, "tile", None, None),
            P("tile", None, None, None),
            P("tile"),
            P(None, "tile", None, None),
        ),
        out_specs=(
            P(None, "tile", "coil", None),
            P(None, "tile", "coil", None),
            P(None, "tile", "coil", None),
        ),
        check_vma=False,
    )
```

profile of v0, /device:TPU:0, one launch (start us, length us, event | category | flops | bytes accessed | tf_op | source)
XLA Modules:
  0.0 87.1 jit_solution(7722630474035764419)
XLA Ops:
  0.6 0.5 collective-permute-start
  1.1 2.6 %collective-permute-start.1 = (f32[2,16,32,128]{3,2,1,0:T(8,128)}, f32[2,16,32,128]{3,2,1,0:T(8,128)S(1)}, u32[]{:S(2)}, u32[]{:S(2)}) collective-permute-start(f32[2,16,32,128]{3,2,1,0:T(8,128)} %p_ref.1), channel_id=1, source_target_pairs={{0,16},{8,24},{16,0},{24,8},{1,17},{9,25},{17,1},{25,9},{2,18},{10... | collective-permute-start | bytes 1572872 | tf_op jit(solution)/shard_map/ppermute | solution.py:563
  3.7 0.8 reshape_squeeze.4
  4.5 0.7 pad_add_fusion
  5.2 0.6 broadcast_in_dim.70
  5.8 5.8 %all-to-all-start = ((s32[8,1,416]{2,1,0:T(1,128)}), s32[8,1,416]{2,1,0:T(1,128)S(1)}, u32[]{:S(2)}, u32[]{:S(2)}) async-start(s32[8,1,416]{2,1,0:T(1,128)} %broadcast_in_dim.70), calls=%async_computation | async-start | bytes 32768 | tf_op jit(solution)/shard_map/all_to_all | solution.py:579
  11.7 0.5 compare_select_fusion.9
  12.3 0.1 pad_add_fusion.3.starts
  12.4 0.1 fusion.7
  12.4 0.2 multiply_select_fusion.2.refs_8_.shift_ref
  12.6 0.1 pad_add_fusion.2.starts
  12.7 5.6 %all-to-all-done = s32[8,1,416]{2,1,0:T(1,128)S(1)} async-done(((s32[8,1,416]{2,1,0:T(1,128)}), s32[8,1,416]{2,1,0:T(1,128)S(1)}, u32[]{:S(2)}, u32[]{:S(2)}) %all-to-all-start) | async-done | bytes 13344 | tf_op jit(solution)/shard_map/all_to_all | solution.py:579
  18.3 0.0 collective-permute-done.refs_1_
  18.3 0.8 copy-done.9
  19.1 1.6 %copy-done = f32[1,2,16,128,128]{4,3,2,1,0:T(8,128)S(1)} copy-done((f32[1,2,16,128,128]{4,3,2,1,0:T(8,128)S(1)}, f32[1,2,16,128,128]{4,3,2,1,0:T(8,128)}, u32[]{:S(2)}) %copy-start) | copy-done | bytes 2097176
  20.7 1.0 %copy-done.2 = f32[2,16,32,128]{3,2,1,0:T(8,128)S(1)} copy-done((f32[2,16,32,128]{3,2,1,0:T(8,128)S(1)}, f32[2,16,32,128]{3,2,1,0:T(8,128)}, u32[]{:S(2)}) %copy-start.2) | copy-done | bytes 524312
  21.7 1.0 %copy-done.5 = bf16[4,256,256]{2,1,0:T(8,128)(2,1)S(1)} copy-done((bf16[4,256,256]{2,1,0:T(8,128)(2,1)S(1)}, bf16[4,256,256]{2,1,0:T(8,128)(2,1)}, u32[]{:S(2)}) %copy-start.5) | copy-done | bytes 524312
  22.7 1.0 %copy-done.10 = f32[2,16,32,128]{3,2,1,0:T(8,128)S(1)} copy-done((f32[2,16,32,128]{3,2,1,0:T(8,128)S(1)}, f32[2,16,32,128]{3,2,1,0:T(8,128)}, u32[]{:S(2)}) %copy-start.10) | copy-done | bytes 524312
  23.8 1.1 %coil_z.2 = (f32[2,16,32,128]{3,2,1,0:T(8,128)S(1)}, f32[2,16,32,128]{3,2,1,0:T(8,128)S(1)}) custom-call(s32[6]{0:T(128)S(1)} %pad_add_fusion.2.starts, f32[2,16,32,128]{3,2,1,0:T(8,128)S(1)} %copy-done.2, f32[2,16,32,128]{3,2,1,0:T(8,128)S(1)} %copy-done.10, f32[2,16,128,128]{3,2,1,0:T(8,128)S(1)} %bitcast.32, bf16[4,256,256]{2,1,0:T(8,128)(2,1)S(1)} %copy-done.5), custom_call_target="tpu_custom_call" | custom-call | flops 402653184 | bytes 3670040 | tf_op jit(solution)/shard_map/coil_z/pallas_call | solution.py:78
  24.9 0.0 copy-start.16
  25.0 0.8 copy-done.16
  25.7 0.8 copy-done.18
  26.5 0.1 slice.18
  26.6 0.1 reshape.212
  26.7 0.1 broadcast_in_dim.74
  26.8 0.3 select_reduce_fusion.1
  27.1 0.1 iota_compare_fusion
  27.2 0.5 select_reduce_fusion
  27.7 0.0 collective-permute-done.1.refs_0_
  27.7 0.1 collective-permute-start.2
  27.8 0.1 stack_reshape.7
  27.9 0.1 stack_reshape.6
  28.0 0.1 mul.112
  28.1 0.0 copy-start.19
  28.1 1.8 %coil_z.3 = (f32[2,16,32,128]{3,2,1,0:T(8,128)S(1)}, f32[2,16,64,128]{3,2,1,0:T(8,128)}) custom-call(s32[6]{0:T(128)S(1)} %pad_add_fusion.2.starts, f32[2,16,32,128]{3,2,1,0:T(8,128)S(1)} %collective-permute-done.1.refs_0_, f32[2,16,128,128]{3,2,1,0:T(8,128)S(1)} %bitcast.33, bf16[4,256,256]{2,1,0:T(8,128)(2,1)S(1)} %copy-done.6), custom_call_target="tpu_custom_call" | custom-call | flops 201326592 | bytes 3145752 | tf_op jit(solution)/shard_map/coil_z/pallas_call | solution.py:78
  29.9 0.5 collective-permute-start.3
  30.5 0.0 copy-start.13
  30.5 0.6 sine_multiply_fusion
  31.1 0.0 collective-permute-done.2.refs_3_
  31.1 5.2 %forward.1 = f32[8,32,128]{2,1,0:T(8,128)} custom-call(s32[2,256]{1,0:T(2,128)S(1)} %pad_add_fusion.1.info, s32[4]{0:T(128)S(1)} %pad_add_fusion.3.starts, f32[2,16,32,128]{3,2,1,0:T(8,128)S(1)} %copy-done.17, f32[2,16,32,128]{3,2,1,0:T(8,128)S(1)} %get-tuple-element.20.refs_1_, f32[2,16,32,128]{3,2,1,0:T(8,128)S(1)} %copy-done.19, ...), custom_call_target="tpu_custom_call" | custom-call | flops 1610612736 | bytes 4999184 | tf_op jit(solution)/shard_map/forward/pallas_call | solution.py:78
  36.3 0.7 copy-done.11
  37.0 3.4 %all-to-all-start.1 = ((f32[8,32,128]{2,1,0:T(8,128)}), f32[8,32,128]{2,1,0:T(8,128)S(1)}, u32[]{:S(2)}, u32[]{:S(2)}) async-start(f32[8,32,128]{2,1,0:T(8,128)} %forward.1), calls=%async_computation.1 | async-start | bytes 262144 | tf_op jit(solution)/shard_map/all_to_all | solution.py:609
  40.4 0.0 copy-start.20
  40.4 0.9 %copy-done.20 = f32[32,3,4,128]{3,2,1,0:T(4,128)S(1)} copy-done((f32[32,3,4,128]{3,2,1,0:T(4,128)S(1)}, f32[32,3,4,128]{3,2,1,0:T(4,128)}, u32[]{:S(2)}) %copy-start.20) | copy-done | bytes 196632
  41.3 4.6 %matrices.1.matrix_ref = f32[2048,128]{1,0:T(8,128)S(1)} custom-call(s32[2,256]{1,0:T(2,128)S(1)} %pad_add_fusion.1.info, s32[1]{0:T(128)} %bitcast.10.tile, f32[32,3,4,128]{3,2,1,0:T(4,128)S(1)} %copy-done.20), custom_call_target="tpu_custom_call" | custom-call | flops 1000000000 | bytes 198660 | tf_op jit(solution)/shard_map/matrices/pallas_call | solution.py:78
  45.9 2.1 %all-to-all-done.1.parts_ref = f32[8,32,128]{2,1,0:T(8,128)S(1)} async-done(((f32[8,32,128]{2,1,0:T(8,128)}), f32[8,32,128]{2,1,0:T(8,128)S(1)}, u32[]{:S(2)}, u32[]{:S(2)}) %all-to-all-start.1) | async-done | bytes 131104 | tf_op jit(solution)/shard_map/all_to_all | solution.py:609
  47.9 0.9 %regrid.1 = f32[16,32,128]{2,1,0:T(8,128)} custom-call(f32[8,32,128]{2,1,0:T(8,128)S(1)} %all-to-all-done.1.parts_ref, f32[2048,128]{1,0:T(8,128)S(1)} %matrices.1.matrix_ref), custom_call_target="tpu_custom_call" | custom-call | flops 10000000 | bytes 1000000 | tf_op jit(solution)/shard_map/regrid/pallas_call | solution.py:272
  48.8 4.9 %all-to-all-start.2 = ((f32[16,32,128]{2,1,0:T(8,128)}), f32[16,32,128]{2,1,0:T(8,128)S(1)}, u32[]{:S(2)}, u32[]{:S(2)}) async-start(f32[16,32,128]{2,1,0:T(8,128)} %regrid.1), calls=%async_computation.2 | async-start | bytes 524288 | tf_op jit(solution)/shard_map/all_to_all | solution.py:615
  53.8 0.6 and_select_fusion.9.chip
  54.3 0.6 add_multiply_fusion.quarters
  54.9 0.9 collective-permute-done.3.refs_0_
  55.8 7.9 %all-to-all-done.2.u_ref = f32[16,32,128]{2,1,0:T(8,128)S(1)} async-done(((f32[16,32,128]{2,1,0:T(8,128)}), f32[16,32,128]{2,1,0:T(8,128)S(1)}, u32[]{:S(2)}, u32[]{:S(2)}) %all-to-all-start.2) | async-done | bytes 262176 | tf_op jit(solution)/shard_map/all_to_all | solution.py:615
  63.7 1.0 %copy-done.7 = bf16[4,256,256]{2,1,0:T(8,128)(2,1)S(1)} copy-done((bf16[4,256,256]{2,1,0:T(8,128)(2,1)S(1)}, bf16[4,256,256]{2,1,0:T(8,128)(2,1)}, u32[]{:S(2)}) %copy-start.7) | copy-done | bytes 524312
  64.8 0.9 %copy-done.12 = f32[256,128]{1,0:T(8,128)S(1)} copy-done((f32[256,128]{1,0:T(8,128)S(1)}, f32[256,128]{1,0:T(8,128)}, u32[]{:S(2)}) %copy-start.12) | copy-done | bytes 131096
  65.7 0.7 copy-done.14
  66.3 0.6 copy-done.15
  67.0 0.7 copy-done.21
  67.6 6.5 %inverse.1 = (f32[2,16,32,128]{3,2,1,0:T(8,128)S(1)}, f32[2,16,32,128]{3,2,1,0:T(8,128)S(1)}) custom-call(s32[2,256]{1,0:T(2,128)S(1)} %copy-done.14, s32[2]{0:T(128)S(1)} %copy-done.21, s32[4]{0:T(128)S(1)} %copy-done.15, f32[16,32,128]{2,1,0:T(8,128)S(1)} %all-to-all-done.2.u_ref, f32[256,128]{1,0:T(8,128)S(1)} %copy-done.12, ...), custom_call_target="tpu_custom_call" | custom-call | flops 1610612736 | bytes 4212760 | tf_op jit(solution)/shard_map/inverse/pallas_call | solution.py:78
  74.2 0.0 copy-start.8
  74.2 0.1 collective-permute-start.4
  74.3 1.9 %collective-permute-done.4.refs_1_ = f32[2,16,32,128]{3,2,1,0:T(8,128)S(1)} collective-permute-done((f32[2,16,32,128]{3,2,1,0:T(8,128)S(1)}, f32[2,16,32,128]{3,2,1,0:T(8,128)S(1)}, u32[]{:S(2)}, u32[]{:S(2)}) %collective-permute-start.4) | collective-permute-done | bytes 524320 | tf_op jit(solution)/shard_map/ppermute | solution.py:567
  76.2 0.3 sums.1
  76.5 9.3 %all_to_all.30 = f32[32,1,128]{2,1,0:T(1,128)S(1)} all-to-all(f32[32,1,128]{2,1,0:T(1,128)S(1)} %bitcast.37), channel_id=1, replica_groups=mesh['coil'=4,'tile'=8] {'coil','tile'}, dimensions={0} | all-to-all | bytes 32768 | tf_op jit(solution)/shard_map/all_to_all | solution.py:624
  85.7 1.3 %finish.1 = (f32[2,16,32,128]{3,2,1,0:T(8,128)}, f32[2,16,32,128]{3,2,1,0:T(8,128)}, f32[2,16,32,128]{3,2,1,0:T(8,128)}) custom-call(f32[32,128]{1,0:T(8,128)S(1)} %bitcast.36, f32[2,16,32,128]{3,2,1,0:T(8,128)S(1)} %copy-done.8, f32[2,16,32,128]{3,2,1,0:T(8,128)S(1)} %copy-done.4, f32[2,16,32,128]{3,2,1,0:T(8,128)S(1)} %copy-done.3, ...), custom_call_target="tpu_custom_call" | custom-call | flops 10000000 | bytes 2113536 | tf_op jit(solution)/shard_map/finish/pallas_call | solution.py:78
  (41 shorter events, 0.1 us)
Async XLA Ops:
  0.6 17.6 %collective-permute-start = (f32[2,16,32,128]{3,2,1,0:T(8,128)}, f32[2,16,32,128]{3,2,1,0:T(8,128)S(1)}, u32[]{:S(2)}, u32[]{:S(2)}) collective-permute-start(f32[2,16,32,128]{3,2,1,0:T(8,128)} %p_ref.1), channel_id=1, source_target_pairs={{0,8},{8,0},{16,24},{24,16},{1,9},{9,1},{17,25},{25,17},{2,10},{10... | collective-permute-start | bytes 1572872 | tf_op jit(solution)/shard_map/ppermute | solution.py:567
  1.1 26.6 %collective-permute-start.1 = (f32[2,16,32,128]{3,2,1,0:T(8,128)}, f32[2,16,32,128]{3,2,1,0:T(8,128)S(1)}, u32[]{:S(2)}, u32[]{:S(2)}) collective-permute-start(f32[2,16,32,128]{3,2,1,0:T(8,128)} %p_ref.1), channel_id=1, source_target_pairs={{0,16},{8,24},{16,0},{24,8},{1,17},{9,25},{17,1},{25,9},{2,18},{10... | collective-permute-start | bytes 1572872 | tf_op jit(solution)/shard_map/ppermute | solution.py:563
  5.8 12.4 %all-to-all-start = ((s32[8,1,416]{2,1,0:T(1,128)}), s32[8,1,416]{2,1,0:T(1,128)S(1)}, u32[]{:S(2)}, u32[]{:S(2)}) async-start(s32[8,1,416]{2,1,0:T(1,128)} %broadcast_in_dim.70), calls=%async_computation | async-start | bytes 32768 | tf_op jit(solution)/shard_map/all_to_all | solution.py:579
  18.3 0.8 copy-start.9
  19.1 1.6 %copy-start = (f32[1,2,16,128,128]{4,3,2,1,0:T(8,128)S(1)}, f32[1,2,16,128,128]{4,3,2,1,0:T(8,128)}, u32[]{:S(2)}) copy-start(f32[1,2,16,128,128]{4,3,2,1,0:T(8,128)} %param.11) | copy-start | bytes 6291460
  20.7 1.0 %copy-start.2 = (f32[2,16,32,128]{3,2,1,0:T(8,128)S(1)}, f32[2,16,32,128]{3,2,1,0:T(8,128)}, u32[]{:S(2)}) copy-start(f32[2,16,32,128]{3,2,1,0:T(8,128)} %p_ref.1) | copy-start | bytes 1572868
  21.7 1.0 %copy-start.5 = (bf16[4,256,256]{2,1,0:T(8,128)(2,1)S(1)}, bf16[4,256,256]{2,1,0:T(8,128)(2,1)}, u32[]{:S(2)}) copy-start(bf16[4,256,256]{2,1,0:T(8,128)(2,1)} %constant.211.clone.refs_3_.refs_2_.refs_5_.table_ref) | copy-start | bytes 1572868
  22.7 1.0 %copy-start.10 = (f32[2,16,32,128]{3,2,1,0:T(8,128)S(1)}, f32[2,16,32,128]{3,2,1,0:T(8,128)}, u32[]{:S(2)}) copy-start(f32[2,16,32,128]{3,2,1,0:T(8,128)} %copy-done.9) | copy-start | bytes 1572868
  23.8 4.3 %copy-start.1 = (f32[1,2,16,128,128]{4,3,2,1,0:T(8,128)S(1)}, f32[1,2,16,128,128]{4,3,2,1,0:T(8,128)}, u32[]{:S(2)}) copy-start(f32[1,2,16,128,128]{4,3,2,1,0:T(8,128)} %param.11) | copy-start | bytes 6291460
  23.8 4.3 %copy-start.6 = (bf16[4,256,256]{2,1,0:T(8,128)(2,1)S(1)}, bf16[4,256,256]{2,1,0:T(8,128)(2,1)}, u32[]{:S(2)}) copy-start(bf16[4,256,256]{2,1,0:T(8,128)(2,1)} %constant.211.clone.refs_3_.refs_2_.refs_5_.table_ref) | copy-start | bytes 1572868
  24.9 0.8 copy-start.16
  25.7 0.8 copy-start.18
  26.5 3.9 %copy-start.22 = (f32[128]{0:T(128)S(1)}, f32[128]{0:T(128)}, u32[]{:S(2)}) copy-start(f32[128]{0:T(128)} %compare_select_fusion.9) | copy-start | bytes 1540
  27.7 3.3 %collective-permute-start.2 = (f32[2,16,32,128]{3,2,1,0:T(8,128)S(1)}, f32[2,16,32,128]{3,2,1,0:T(8,128)}, u32[]{:S(2)}, u32[]{:S(2)}) collective-permute-start(f32[2,16,32,128]{3,2,1,0:T(8,128)S(1)} %collective-permute-done.1.refs_0_), channel_id=1, source_target_pairs={{0,8},{8,0},{16,24},{24,16},{1,9},{9,1},{17,25},{25,17},{2,10},{10... | collective-permute-start | bytes 1572872 | tf_op jit(solution)/shard_map/ppermute | solution.py:567
  28.1 3.0 %copy-start.17 = (f32[2,16,32,128]{3,2,1,0:T(8,128)S(1)}, f32[2,16,32,128]{3,2,1,0:T(8,128)}, u32[]{:S(2)}) copy-start(f32[2,16,32,128]{3,2,1,0:T(8,128)} %copy-done.16) | copy-start | bytes 1572868
  28.1 3.0 %copy-start.19 = (f32[2,16,32,128]{3,2,1,0:T(8,128)S(1)}, f32[2,16,32,128]{3,2,1,0:T(8,128)}, u32[]{:S(2)}) copy-start(f32[2,16,32,128]{3,2,1,0:T(8,128)} %copy-done.18) | copy-start | bytes 1572868
  29.9 25.9 %collective-permute-start.3 = (f32[2,16,64,128]{3,2,1,0:T(8,128)}, f32[2,16,64,128]{3,2,1,0:T(8,128)}, u32[]{:S(2)}, u32[]{:S(2)}) collective-permute-start(f32[2,16,64,128]{3,2,1,0:T(8,128)} %get-tuple-element.24), channel_id=1, source_target_pairs={{0,16},{8,24},{16,0},{24,8},{1,17},{9,25},{17,1},{25,9},{2,18},{10... | collective-permute-start | bytes 3145736 | tf_op jit(solution)/shard_map/ppermute | solution.py:563
  30.5 9.9 %copy-start.13 = (s32[2,256]{1,0:T(2,128)}, s32[2,256]{1,0:T(2,128)S(1)}, u32[]{:S(2)}) copy-start(s32[2,256]{1,0:T(2,128)S(1)} %pad_add_fusion.1.info) | copy-start | bytes 6148
  36.3 0.7 copy-start.11
  37.0 11.0 %all-to-all-start.1 = ((f32[8,32,128]{2,1,0:T(8,128)}), f32[8,32,128]{2,1,0:T(8,128)S(1)}, u32[]{:S(2)}, u32[]{:S(2)}) async-start(f32[8,32,128]{2,1,0:T(8,128)} %forward.1), calls=%async_computation.1 | async-start | bytes 262144 | tf_op jit(solution)/shard_map/all_to_all | solution.py:609
  40.4 0.9 %copy-start.20 = (f32[32,3,4,128]{3,2,1,0:T(4,128)S(1)}, f32[32,3,4,128]{3,2,1,0:T(4,128)}, u32[]{:S(2)}) copy-start(f32[32,3,4,128]{3,2,1,0:T(4,128)} %weights_ref) | copy-start | bytes 589828
  48.8 14.9 %all-to-all-start.2 = ((f32[16,32,128]{2,1,0:T(8,128)}), f32[16,32,128]{2,1,0:T(8,128)S(1)}, u32[]{:S(2)}, u32[]{:S(2)}) async-start(f32[16,32,128]{2,1,0:T(8,128)} %regrid.1), calls=%async_computation.2 | async-start | bytes 524288 | tf_op jit(solution)/shard_map/all_to_all | solution.py:615
  54.9 21.2 %copy-start.3 = (f32[2,16,32,128]{3,2,1,0:T(8,128)S(1)}, f32[2,16,32,128]{3,2,1,0:T(8,128)}, u32[]{:S(2)}) copy-start(f32[2,16,32,128]{3,2,1,0:T(8,128)} %p_ref.1) | copy-start | bytes 1572868
  54.9 21.2 %copy-start.4 = (f32[2,16,32,128]{3,2,1,0:T(8,128)S(1)}, f32[2,16,32,128]{3,2,1,0:T(8,128)}, u32[]{:S(2)}) copy-start(f32[2,16,32,128]{3,2,1,0:T(8,128)} %r_ref.1) | copy-start | bytes 1572868
  63.7 1.0 %copy-start.7 = (bf16[4,256,256]{2,1,0:T(8,128)(2,1)S(1)}, bf16[4,256,256]{2,1,0:T(8,128)(2,1)}, u32[]{:S(2)}) copy-start(bf16[4,256,256]{2,1,0:T(8,128)(2,1)} %constant.211.clone.refs_3_.refs_2_.refs_5_.table_ref) | copy-start | bytes 1572868
  64.8 0.9 %copy-start.12 = (f32[256,128]{1,0:T(8,128)S(1)}, f32[256,128]{1,0:T(8,128)}, u32[]{:S(2)}) copy-start(f32[256,128]{1,0:T(8,128)} %copy-done.11) | copy-start | bytes 393220
  65.7 0.7 copy-start.14
  66.3 0.6 copy-start.15
  67.0 0.7 copy-start.21
  74.2 11.6 %copy-start.8 = (f32[2,16,32,128]{3,2,1,0:T(8,128)S(1)}, f32[2,16,32,128]{3,2,1,0:T(8,128)}, u32[]{:S(2)}) copy-start(f32[2,16,32,128]{3,2,1,0:T(8,128)} %x_ref.1) | copy-start | bytes 1572868
  74.2 2.0 %collective-permute-start.4 = (f32[2,16,32,128]{3,2,1,0:T(8,128)S(1)}, f32[2,16,32,128]{3,2,1,0:T(8,128)S(1)}, u32[]{:S(2)}, u32[]{:S(2)}) collective-permute-start(f32[2,16,32,128]{3,2,1,0:T(8,128)S(1)} %get-tuple-element.26), channel_id=1, source_target_pairs={{0,8},{8,0},{16,24},{24,16},{1,9},{9,1},{17,25},{25,17},{2,10},{10... | collective-permute-start | bytes 1572872 | tf_op jit(solution)/shard_map/ppermute | solution.py:567
where the time goes:
time: 87.9 us; the launch traced here: 87.1 us
  Pallas kernels  21.8 us (25%)
  waiting for transfers between devices  18.3 us (21%)
  starting transfers between devices  17.9 us (20%)
  local copies, waits for them, and re-layouts  14.5 us (16%)
  blocking collectives  9.28 us (11%)
  other arithmetic  4.34 us (5%)
  between operations  0.95 us (1%)
    pallas_call x7, Pallas kernels, call(): pl.pallas_call(kernel, out_shape=[jax.ShapeDtypeStruct(shape, jnp.float32...  20.9 us
    unnamed x47, local copies, waits for them, and re-layouts  12.6 us
    all_to_all x1, blocking collectives, shards(): total = lax.all_to_all(found, ('coil', 'tile'), 0, 0, tiled=True)  9.28 us
    all_to_all x1, waiting for transfers between devices, shards(): lax.all_to_all(done, ('coil', 'tile'), 0, 0, axis_index_groups=groups, ti...  7.92 us
    all_to_all x1, starting transfers between devices, shards(): lax.all_to_all(jnp.broadcast_to(mine[None], (ntile, mine.shape[0])), 'til...  5.83 us
    all_to_all x1, waiting for transfers between devices, shards(): lax.all_to_all(jnp.broadcast_to(mine[None], (ntile, mine.shape[0])), 'til...  5.58 us
    all_to_all x1, starting transfers between devices, shards(): lax.all_to_all(done, ('coil', 'tile'), 0, 0, axis_index_groups=groups, ti...  4.91 us
    all_to_all x1, starting transfers between devices, shards(): parts = lax.all_to_all(partial, 'tile', 0, 0, tiled=True)  3.37 us
  transfers between devices with their start and end apart: 8, of which 5 were waited for; matrix products, arithmetic and copies ran while one was open for 7% of the time, Pallas kernels for 16%

commit v1 on v0

--- a/solution.py
+++ b/solution.py
@@ -69,80 +69,71 @@
     return here, past < 4 - chunk
 
 
-def call(kernel, outs, scratch, operands, smem, flops, name, hbm=(), limit=VMEM):
-    specs = [pl.BlockSpec(memory_space=pltpu.SMEM)] * smem
-    specs += [pl.BlockSpec(memory_space=pltpu.VMEM)] * (len(operands) - smem)
-    for at in hbm:
-        specs[at] = pl.BlockSpec(memory_space=pltpu.HBM)
+def call(kernel, outs, scratch, operands, flops, name, hbm=(), hbm_outs=()):
+    here = pl.BlockSpec(memory_space=pltpu.VMEM)
+    there = pl.BlockSpec(memory_space=pltpu.HBM)
     moved = sum(math.prod(a.shape) * a.dtype.itemsize for a in operands)
     return pl.pallas_call(
         kernel,
         out_shape=[jax.ShapeDtypeStruct(shape, jnp.float32) for shape in outs],
-        in_specs=specs,
-        out_specs=[pl.BlockSpec(memory_space=pltpu.VMEM)] * len(outs),
+        in_specs=[there if at in hbm else here for at in range(len(operands))],
+        out_specs=[there if at in hbm_outs else here for at in range(len(outs))],
         scratch_shapes=[
             pltpu.VMEM(shape, jnp.float32) if isinstance(shape, tuple) else shape
             for shape in scratch
         ],
-        compiler_params=pltpu.CompilerParams(vmem_limit_bytes=limit),
+        compiler_params=pltpu.CompilerParams(vmem_limit_bytes=VMEM),
         cost_estimate=pl.CostEstimate(flops=flops, bytes_accessed=moved, transcendentals=0),
         name=name,
     )(*operands)
 
 
-def z_of_coil(p_ref, s_ref, out_ref, rows, table):
-    _, planes, part, length = p_ref.shape
-    batch = min(planes, 256 // part)
-    for base in range(0, planes, batch):
-        bands = []
-        for plane in range(base, base + batch):
-            s_re = s_ref[0, plane, rows, :]
-            s_im = s_ref[1, plane, rows, :]
-            p_re = p_ref[0, plane]
-            p_im = p_ref[1, plane]
-            bands.append(
-                jnp.concatenate([s_re * p_re - s_im * p_im, s_re * p_im + s_im * p_re], axis=1)
-            )
-        done = dot_right(jnp.concatenate(bands, axis=0), table)
-        for ri in range(2):
-            half = done[:, ri * length : (ri + 1) * length]
-            out_ref[ri, base : base + batch] = half.reshape(batch, part, length)
-
-
-def quarter(starts, at, part):
-    return pl.ds(pl.multiple_of(starts[at], part), part)
-
-
-def coil_z_kernel(starts, *refs, quarters, sends):
-    count = len(quarters)
-    p_refs = refs[:count]
-    s_ref, table_ref = refs[count : count + 2]
-    outs = refs[count + 2 :]
-    part = p_refs[0].shape[2]
-    table = (table_ref[0], table_ref[1])
-    for at in range(count):
-        z_of_coil(p_refs[at], s_ref, outs[at], quarter(starts, quarters[at], part), table)
-    chips = sends + 1
-    for by in range(1, chips):
-        hop = chips - by
-        for half in range(2):
-            rows = quarter(starts, half * chips + hop, part)
-            to = quarter(starts, 2 * chips + half, part)
-            for ri in range(2):
-                outs[count + by - 1][ri, :, to, :] = s_ref[ri, :, rows, :]
-
-
-def coil_z(starts, pieces, quarters, smap, tables, sends=0):
-    _, planes, part, length = pieces[0].shape
-    count = len(pieces)
+def started(pairs, sems):
+    copies = [
+        pltpu.make_async_copy(source, to, sems.at[at]) for at, (source, to) in enumerate(pairs)
+    ]
+    for copy in copies:
+        copy.start()
+    return copies
+
+
+def place_on_coil():
+    coil = lax.axis_index("coil")
+    return coil // 2, coil % 2
+
+
+def quarters_of(chips, part):
+    chip, core = place_on_coil()
+    return [
+        pl.multiple_of(((chip + hop) % chips * 2 + at) * part, part)
+        for at in (core, 1 - core)
+        for hop in range(chips)
+    ]
+
+
+def map_rows_kernel(s_ref, *refs, chips):
+    outs, sems = refs[:-1], refs[-1]
+    chip, _ = place_on_coil()
+    own = s_ref.shape[2] // chips
+    pairs = [
+        (s_ref.at[:, :, pl.ds(pl.multiple_of((chip + chips - by) % chips * own, own), own), :], out)
+        for by, out in enumerate(outs, 1)
+    ]
+    for copy in started(pairs, sems):
+        copy.wait()
+
+
+def map_rows(smap, chips):
+    _, planes, length, _ = smap.shape
     return call(
-        functools.partial(coil_z_kernel, quarters=quarters, sends=sends),
-        [pieces[0].shape] * count + [(2, planes, 2 * part, length)] * sends,
-        [],
-        [starts, *pieces, smap, tables],
-        1,
-        count * planes * part * 24 * length * length,
-        "coil_z",
+        functools.partial(map_rows_kernel, chips=chips),
+        [(2, planes, length // chips, length)] * (chips - 1),
+        [pltpu.SemaphoreType.DMA((chips - 1,))],
+        [smap],
+        0,
+        "map_rows",
+        hbm=[0],
+        hbm_outs=range(chips - 1),
     )
 
 
@@ -181,21 +172,52 @@
         out_ref[handler] = both[:32] + both[32:]
 
 
-def forward_kernel(info, starts, *refs, done, pieces, planes, part, length, chunk, slots):
-    t_refs = refs[:done]
-    p_refs = refs[done:pieces]
-    s_ref, table_ref, cos_ref, sin_ref, shift_ref = refs[pieces : pieces + 5]
-    out_ref, natural, ybuf, grid, gbuf, late = refs[pieces + 5 :]
+def forward_kernel(*refs, pieces, chunk, slots):
+    p_hbm = refs[:pieces]
+    s_hbm, table_hbm, info_hbm, cos_hbm, sin_hbm, shift_hbm, out_ref = refs[pieces : pieces + 7]
+    pbuf, sbuf, tables, info, cos_ref, sin_ref, shift_ref = refs[pieces + 7 : pieces + 14]
+    natural, ybuf, grid, gbuf, sems = refs[pieces + 14 :]
+    _, planes, part, length = p_hbm[0].shape
     rows = length * planes
-    table = (table_ref[0], table_ref[1])
-    for at in range(done, pieces):
-        z_of_coil(p_refs[at - done], s_ref, late.at[at - done], quarter(starts, at, part), table)
-    for at in range(pieces):
-        to = quarter(starts, at, part)
-        source = t_refs[at] if at < done else late.at[at - done]
-        for ri in range(2):
-            natural[ri, :, to, :] = source[ri]
-    table = (table_ref[2], table_ref[3])
+    starts = quarters_of(pieces // 2, part)
+    order = [0, pieces // 2]
+    order += [at for at in range(pieces) if at not in order]
+    first = [(table_hbm.at[0:2], tables.at[0:2])]
+    for at in order:
+        first += [(p_hbm[at], pbuf.at[at]), (s_hbm.at[:, :, pl.ds(starts[at], part), :], sbuf.at[at])]
+    last = [
+        (table_hbm.at[2:4], tables.at[2:4]),
+        (info_hbm, info),
+        (cos_hbm, cos_ref),
+        (sin_hbm, sin_ref),
+        (shift_hbm, shift_ref),
+    ]
+    copies = started(first + last, sems)
+    copies[0].wait()
+    batch = min(planes, 256 // part)
+    table = (tables[0], tables[1])
+    for turn, at in enumerate(order):
+        copies[1 + 2 * turn].wait()
+        copies[2 + 2 * turn].wait()
+        for base in range(0, planes, batch):
+            bands = []
+            for plane in range(base, base + batch):
+                s_re = sbuf[at, 0, plane]
+                s_im = sbuf[at, 1, plane]
+                p_re = pbuf[at, 0, plane]
+                p_im = pbuf[at, 1, plane]
+                bands.append(
+                    jnp.concatenate([s_re * p_re - s_im * p_im, s_re * p_im + s_im * p_re], axis=1)
+                )
+            done = dot_right(jnp.concatenate(bands, axis=0), table)
+            for ri in range(2):
+                half = done[:, ri * length : (ri + 1) * length]
+                natural[ri, base : base + batch, pl.ds(starts[at], part), :] = half.reshape(
+                    batch, part, length
+                )
+    for copy in copies[1 + 2 * pieces :]:
+        copy.wait()
+    table = (tables[2], tables[3])
     for pair in range(planes // 2):
         columns = [
             jnp.concatenate([natural[0, plane], natural[1, plane]], axis=0)
@@ -214,28 +236,32 @@
     cut_boxes(info, grid, cos_ref, sin_ref, shift_ref, out_ref, gbuf, planes, chunk, slots)
 
 
-def forward(info, starts, done, rest, smap, tables, phases, shift, chunk, slots):
-    _, planes, part, length = done[0].shape
-    pieces = len(done) + len(rest)
-    handlers = info.shape[1] // slots
-    kernel = functools.partial(
-        forward_kernel, done=len(done), pieces=pieces, planes=planes, part=part, length=length,
-        chunk=chunk, slots=slots,
-    )
+def forward(pieces, smap, tables, info, phases, shift, chunk, slots):
+    _, planes, part, length = pieces[0].shape
+    count = len(pieces)
+    blocks = info.shape[1]
+    operands = [*pieces, smap, tables, info, *phases, shift]
     return call(
-        kernel,
-        [(handlers, 32, LANES)],
+        functools.partial(forward_kernel, pieces=count, chunk=chunk, slots=slots),
+        [(blocks // slots, 32, LANES)],
         [
+            (count, 2, planes, part, length),
+            (count, 2, planes, part, length),
+            pltpu.VMEM(tables.shape, tables.dtype),
+            pltpu.SMEM(info.shape, info.dtype),
+            (blocks, LANES),
+            (blocks, LANES),
+            shift.shape,
             (2, planes, length, length),
             (2 * length * planes, length),
             (length * (length // chunk + 1), LANES),
-            (handlers * LANES, LANES),
-            (len(rest), 2, planes, part, length),
+            (blocks * 4, LANES),
+            pltpu.SemaphoreType.DMA((2 * count + 6,)),
         ],
-        [info, starts, *done, *rest, smap, tables, *phases, shift],
-        2,
+        operands,
         48 * planes * length**3,
         "forward",
+        hbm=range(len(operands)),
     )[0]
 
 
@@ -269,16 +295,15 @@
 
 def regrid(parts, matrix, copies):
     shape = (copies,) + parts.shape[1:]
-    return pl.pallas_call(
+    return call(
         regrid_kernel,
-        out_shape=jax.ShapeDtypeStruct(shape, jnp.float32),
-        in_specs=[pl.BlockSpec(memory_space=pltpu.VMEM)] * 2,
-        out_specs=pl.BlockSpec(memory_space=pltpu.HBM),
-        scratch_shapes=[pltpu.VMEM(shape, jnp.float32), pltpu.SemaphoreType.DMA],
-        compiler_params=pltpu.CompilerParams(vmem_limit_bytes=VMEM // 2),
-        cost_estimate=pl.CostEstimate(flops=10**7, bytes_accessed=10**6, transcendentals=0),
-        name="regrid",
-    )(parts, matrix)
+        [shape],
+        [shape, pltpu.SemaphoreType.DMA],
+        [parts, matrix],
+        10**7,
+        "regrid",
+        hbm_outs=[0],
+    )[0]
 
 
 def place_boxes(info, chip, u_ref, cos_ref, sin_ref, shift_ref, outs, gbufs, planes, chunk, slots):
@@ -292,14 +317,12 @@
         sin_b = jnp.concatenate([sin_ref[rows, :]] * 4, axis=0)
         for hop in range(chips):
             u_hi, u_lo = (
-                half.astype(jnp.float32) for half in halves(u_ref[chip[hop] * handlers + handler])
+                half.astype(jnp.float32) for half in halves(u_ref[(chip + hop) % chips * handlers + handler])
             )
             stack = jnp.concatenate([u_hi, u_lo, u_hi, jnp.zeros_like(u_hi)], axis=0)
             cells = dot_bf16(stack.T.astype(jnp.bfloat16), table, ((1,), (0,)))
             turned = cells * cos_b - pltpu.roll(cells, LANES // 2, 1) * sin_b
             gbufs[hop][handler * LANES : (handler + 1) * LANES, :] = turned
-    for out in outs:
-        out[...] = jnp.zeros_like(out)
     band = band_of_lane(planes, chunk)
 
     def put(handler, carry):
@@ -320,27 +343,39 @@
     lax.fori_loop(0, handlers, put, 0)
 
 
-def inverse_kernel(
-    info, chip, quarters, u_ref, cos_ref, sin_ref, shift_ref, s_ref, table_ref, *refs,
-    planes, part, length, chunk, slots, chips
-):
-    far_maps = refs[: chips - 1]
-    outs = refs[chips - 1 : chips + 1]
-    refs = refs[chips + 1 :]
+def inverse_kernel(*refs, part, length, chunk, slots, chips):
+    u_ref, info_hbm, cos_hbm, sin_hbm, shift_hbm, table_hbm, s_hbm = refs[:7]
+    far_maps = refs[7 : 6 + chips]
+    outs = refs[6 + chips : 8 + chips]
+    refs = refs[8 + chips :]
     grids, gbufs, refs = refs[:chips], refs[chips : 2 * chips], refs[2 * chips :]
-    ybuf, images, maps, sems = refs
-    copies = [
-        pltpu.make_async_copy(far_maps[at], maps.at[at], sems.at[at]) for at in range(chips - 1)
-    ]
-    for copy in copies:
-        copy.start()
-    place_boxes(info, chip, u_ref, cos_ref, sin_ref, shift_ref, grids, gbufs, planes, chunk, slots)
+    info, cos_ref, sin_ref, shift_ref, table_ref, ybuf, images, maps, sems = refs
+    planes = s_hbm.shape[1]
     rows = length * planes
     own = length // chips
+    chip, core = place_on_coil()
+    own_rows = pl.multiple_of(chip * own, own)
+    pairs = [
+        (info_hbm, info),
+        (cos_hbm, cos_ref),
+        (sin_hbm, sin_ref),
+        (shift_hbm, shift_ref),
+        (table_hbm, table_ref),
+        (s_hbm.at[:, :, pl.ds(own_rows, own), :], maps.at[0]),
+    ]
+    pairs += [(far_map, maps.at[at]) for at, far_map in enumerate(far_maps, 1)]
+    copies = started(pairs, sems)
+    for grid in grids:
+        grid[...] = jnp.zeros_like(grid)
+    for copy in copies[:4]:
+        copy.wait()
+    place_boxes(info, chip, u_ref, cos_ref, sin_ref, shift_ref, grids, gbufs, planes, chunk, slots)
+    for copy in copies[4:]:
+        copy.wait()
     table = []
     for half in range(2):
         bands = [
-            table_ref[half, pl.ds(pl.multiple_of(ri * length + chip[0] * own, own), own), :]
+            table_ref[half, pl.ds(pl.multiple_of(ri * length + own_rows, own), own), :]
             for ri in range(2)
         ]
         table.append(jnp.concatenate(bands, axis=0))
@@ -366,13 +401,10 @@
                     images[hop, ri, 2 * pair + inner] = done[
                         ri * own : (ri + 1) * own, inner * LANES : (inner + 1) * LANES
                     ]
-    for copy in copies:
-        copy.wait()
     table = (table_ref[2], table_ref[3])
     batch = min(planes, 256 // part)
-    for at in range(2):
-        local = pl.ds(pl.multiple_of(quarters[2 + at], part), part)
-        whole = pl.ds(pl.multiple_of(quarters[at], part), part)
+    for at, half in enumerate((1 - core, core)):
+        local = pl.ds(pl.multiple_of(half * part, part), part)
         for base in range(0, planes, batch):
             total_re, total_im = 0.0, 0.0
             for hop in range(chips):
@@ -383,43 +415,43 @@
                 done = dot_right(jnp.concatenate(bands, axis=0), table)
                 i_re = done[:, :length].reshape(batch, part, length)
                 i_im = done[:, length:].reshape(batch, part, length)
-                if hop:
-                    s_re = maps[hop - 1, 0, base : base + batch, local, :]
-                    s_im = maps[hop - 1, 1, base : base + batch, local, :]
-                else:
-                    s_re = s_ref[0, base : base + batch, whole, :]
-                    s_im = s_ref[1, base : base + batch, whole, :]
+                s_re = maps[hop, 0, base : base + batch, local, :]
+                s_im = maps[hop, 1, base : base + batch, local, :]
                 total_re = total_re + (s_re * i_re + s_im * i_im)
                 total_im = total_im + (s_re * i_im - s_im * i_re)
             outs[at][0, base : base + batch] = total_re
             outs[at][1, base : base + batch] = total_im
 
 
-def inverse(info, chip_order, quarters, spread, phases, shift, smap, tables, far_maps, part, chunk, slots):
+def inverse(spread, info, phases, shift, tables, smap, far_maps, part, chunk, slots):
     _, planes, length, _ = smap.shape
     chips = len(far_maps) + 1
-    handlers = info.shape[1] // slots
+    blocks = info.shape[1]
     rows = length * (length // chunk + 1)
-    kernel = functools.partial(
-        inverse_kernel, planes=planes, part=part, length=length, chunk=chunk, slots=slots,
-        chips=chips,
-    )
+    own = (chips, 2, planes, 2 * part, length)
+    operands = [spread, info, *phases, shift, tables, smap, *far_maps]
     return call(
-        kernel,
+        functools.partial(
+            inverse_kernel, part=part, length=length, chunk=chunk, slots=slots, chips=chips
+        ),
         [(2, planes, part, length)] * 2,
         [(rows, LANES)] * chips
-        + [(handlers * LANES, LANES)] * chips
+        + [(blocks * 4, LANES)] * chips
         + [
+            pltpu.SMEM(info.shape, info.dtype),
+            (blocks, LANES),
+            (blocks, LANES),
+            shift.shape,
+            pltpu.VMEM(tables.shape, tables.dtype),
             (chips, 2 * length * planes, length),
-            (chips, 2, planes, 2 * part, length),
-            (chips - 1, 2, planes, 2 * part, length),
-            pltpu.SemaphoreType.DMA((chips - 1,)),
+            own,
+            own,
+            pltpu.SemaphoreType.DMA((5 + chips,)),
         ],
-        [info, chip_order, quarters, spread, *phases, shift, smap, tables, *far_maps],
-        3,
+        operands,
         48 * planes * length**3,
         "inverse",
-        hbm=range(9, 9 + chips - 1),
+        hbm=range(1, len(operands)),
     )
 
 
@@ -452,7 +484,7 @@
 
 def sums(terms, p, r, devices):
     kernel = functools.partial(sums_kernel, terms=len(terms))
-    return call(kernel, [p.shape, (devices, LANES)], [], [*terms, p, r], 0, 10**7, "sums")
+    return call(kernel, [p.shape, (devices, LANES)], [], [*terms, p, r], 10**7, "sums")
 
 
 def finish_kernel(total_ref, x_ref, r_ref, p_ref, normal_ref, x_out, r_out, p_out):
@@ -470,10 +502,15 @@
 
 
 def finish(total, x, r, p, normal):
-    return call(finish_kernel, [x.shape] * 3, [], [total, x, r, p, normal], 0, 10**7, "finish")
-
-
-def matrices_kernel(info, tile, weights_ref, out_ref, held, *, slots):
+    return call(finish_kernel, [x.shape] * 3, [], [total, x, r, p, normal], 10**7, "finish")
+
+
+def matrices_kernel(info_hbm, weights_ref, out_ref, held, info, sem, *, slots):
+    base = lax.axis_index("tile") * slots
+    copy = pltpu.make_async_copy(info_hbm, info, sem)
+    copy.start()
+    copy.wait()
+
     def one(block, carry):
         w_x = weights_ref[block, 0]
         w_y = weights_ref[block, 1]
@@ -489,7 +526,7 @@
                 along_z = w_z[f : f + 1] * w_z[other : other + 1]
                 right += [along * along_z for along in along_x]
         turned = pltpu.roll(
-            jnp.concatenate([w_y, w_y], axis=0), info[1, tile[0] * slots + block] % 4, 0
+            jnp.concatenate([w_y, w_y], axis=0), info[1, base + block] % 4, 0
         )[:4]
         left = jnp.concatenate([turned * turned[e : e + 1] for e in range(4)], axis=0)
         done = dot_right(left, halves(jnp.concatenate(right, axis=0)), ((1,), (1,)))
@@ -515,16 +552,15 @@
     lax.fori_loop(0, 16, turn, 0, unroll=2)
 
 
-def block_matrices(info, tile, weights):
-    slots = weights.shape[0]
+def block_matrices(info, weights):
     return call(
-        functools.partial(matrices_kernel, slots=slots),
+        functools.partial(matrices_kernel, slots=weights.shape[0]),
         [(16 * LANES, LANES)],
-        [(16 * LANES, LANES)],
-        [info, tile, weights],
-        2,
+        [(16 * LANES, LANES), pltpu.SMEM(info.shape, info.dtype), pltpu.SemaphoreType.DMA],
+        [info, weights],
         10**9,
         "matrices",
+        hbm=[0],
     )[0]
 
 
@@ -551,8 +587,6 @@
     part = image_p.shape[2]
     chunk = LANES // (2 * planes)
     tile = lax.axis_index("tile")
-    coil = lax.axis_index("coil")
-    chip, core = coil // 2, coil % 2
     smap = sensitivity[0]
     tables = fourier_tables(length)
 
@@ -566,23 +600,15 @@
         pairs = [(a * 2 + k, a * 2 + 1 - k) for a in range(chips) for k in range(2)]
         return lax.ppermute(values, "coil", pairs)
 
-    hops = jnp.arange(chips, dtype=jnp.int32)
-    chip_order = (chip + hops) % chips
-    starts = jnp.concatenate(
-        [(chip_order * 2 + at) * part for at in (core, 1 - core)]
-        + [jnp.stack([core * part, (1 - core) * part])]
-    )
-
     p_same = [image_p] + [from_chip(image_p, by) for by in range(1, chips)]
     p_other = [other_core(piece) for piece in p_same]
     mine = jnp.concatenate([block_owner, owner_list[:, 0].reshape(-1)])
     gathered = lax.all_to_all(
         jnp.broadcast_to(mine[None], (ntile, mine.shape[0])), "tile", 0, 0, tiled=True
     )
-    near = coil_z(starts, [p_same[0], p_other[0]], [0, chips], smap, tables)
-    far = coil_z(starts, p_same[1:], list(range(1, chips)), smap, tables, chips - 1)
-    far_maps = [from_chip(rows, by) for by, rows in enumerate(far[chips - 1 :], 1)]
-    gathered, near = lax.optimization_barrier((gathered, near))
+    far_rows = map_rows(smap, chips)
+    far_rows, p_same[1:] = lax.optimization_barrier((far_rows, p_same[1:]))
+    far_maps = [from_chip(rows, by) for by, rows in enumerate(far_rows, 1)]
 
     off_x, off_y, off_z = block_offsets(gathered, slots, ntile, capacity)
     info = jnp.stack(
@@ -601,13 +627,10 @@
     sine = jnp.where(row_ri == 0, 1.0, -1.0) * jnp.sin(angle)
     shift = jnp.where(row_ri == lane_ri[None], jnp.cos(angle), sine)
     shift = jnp.where(lane_q[None] % 4 == row_q, shift / math.sqrt(length), 0.0)
-    done = [near[0], *far[: chips - 1], near[1]]
-    partial = forward(
-        info, starts[: 2 * chips], done, p_other[1:], smap, tables, phases, shift, chunk, slots
-    )
+    partial = forward(p_same + p_other, smap, tables, info, phases, shift, chunk, slots)
     partial, weights = lax.optimization_barrier((partial, kb_weights))
     parts = lax.all_to_all(partial, "tile", 0, 0, tiled=True)
-    done = regrid(parts, block_matrices(info, tile[None], weights), chips * ntile)
+    done = regrid(parts, block_matrices(info, weights), chips * ntile)
     groups = [
         [at * ntile + t for at in range(ncoil) if at % 2 == k for t in range(ntile)]
         for k in range(2)
@@ -615,10 +638,8 @@
     spread = lax.all_to_all(
         done, ("coil", "tile"), 0, 0, axis_index_groups=groups, tiled=True
     )
-    quarters = jnp.stack([chip * 2 + 1 - core, chip * 2 + core, 1 - core, core]) * part
     sent, kept = inverse(
-        info, chip_order, quarters, spread, phases, shift, smap, tables, far_maps, part, chunk,
-        slots,
+        spread, info, phases, shift, tables, smap, far_maps, part, chunk, slots
     )
     normal, found = sums([kept, other_core(sent)], image_p, image_r, ncoil * ntile)
     total = lax.all_to_all(found, ("coil", "tile"), 0, 0, tiled=True)

time: 87.9 us -> 80.7 us (0.918)
  local copies, waits for them, and re-layouts: 14.5 us -> 12 us
  Pallas kernels: 21.8 us -> 19.9 us
  other arithmetic: 4.34 us -> 2.48 us
  waiting for transfers between devices: 18.3 us -> 16.9 us
    unnamed x47 -> x31, local copies, waits for them, and re-layouts: 12.6 us -> 10.1 us
    all_to_all x1, waiting for transfers between devices: 5.58 us -> 3.52 us  [shards(): lax.all_to_all(jnp.broadcast_to(mine[None], (ntile, mine.shape[0])), 'til...]
    all_to_all x1, waiting for transfers between devices: 7.92 us -> 9.59 us  [shards(): lax.all_to_all(done, ('coil', 'tile'), 0, 0, axis_index_groups=groups, ti...]
    all_to_all x1, waiting for transfers between devices: 2.07 us -> 1 us  [shards(): parts = lax.all_to_all(partial, 'tile', 0, 0, tiled=True)]
    pallas_call x7, Pallas kernels: 20.9 us -> 19.9 us  [call(): pl.pallas_call(kernel, out_shape=[jax.ShapeDtypeStruct(shape, jnp.float32...]
  transfers between devices with their start and end apart: 8 -> 8, of which waited for: 5 -> 5; matrix products, arithmetic and copies ran while one was open for 7% -> 5% of each run, Pallas kernels for 16% -> 15%
where the time goes in v1:
time: 80.7 us; the launch traced here: 80.1 us
  Pallas kernels  19.9 us (25%)
  starting transfers between devices  18.7 us (23%)
  waiting for transfers between devices  16.9 us (21%)
  local copies, waits for them, and re-layouts  12 us (15%)
  blocking collectives  9.27 us (11%)
  other arithmetic  2.48 us (3%)
  between operations  0.93 us (1%)
    pallas_call x7, Pallas kernels, call(): pl.pallas_call(kernel, out_shape=[jax.ShapeDtypeStruct(shape, jnp.float32...  19.9 us
    unnamed x31, local copies, waits for them, and re-layouts  10.1 us
    all_to_all x1, waiting for transfers between devices, shards(): lax.all_to_all(done, ('coil', 'tile'), 0, 0, axis_index_groups=groups, ti...  9.59 us
    all_to_all x1, blocking collectives, shards(): total = lax.all_to_all(found, ('coil', 'tile'), 0, 0, tiled=True)  9.27 us
    all_to_all x1, starting transfers between devices, shards(): lax.all_to_all(jnp.broadcast_to(mine[None], (ntile, mine.shape[0])), 'til...  5.83 us
    all_to_all x1, starting transfers between devices, shards(): lax.all_to_all(done, ('coil', 'tile'), 0, 0, axis_index_groups=groups, ti...  5.73 us
    all_to_all x1, waiting for transfers between devices, shards(): lax.all_to_all(jnp.broadcast_to(mine[None], (ntile, mine.shape[0])), 'til...  3.52 us
    all_to_all x1, starting transfers between devices, shards(): parts = lax.all_to_all(partial, 'tile', 0, 0, tiled=True)  3.37 us
  transfers between devices with their start and end apart: 8, of which 5 were waited for; matrix products, arithmetic and copies ran while one was open for 5% of the time, Pallas kernels for 15%

profile of v1, /device:TPU:0, one launch (start us, length us, event | category | flops | bytes accessed | tf_op | source)
XLA Modules:
  0.0 80.1 jit_solution(523972716877161743)
XLA Ops:
  0.6 0.5 collective-permute-start.1
  1.1 2.6 %collective-permute-start = (f32[2,16,32,128]{3,2,1,0:T(8,128)}, f32[2,16,32,128]{3,2,1,0:T(8,128)}, u32[]{:S(2)}, u32[]{:S(2)}) collective-permute-start(f32[2,16,32,128]{3,2,1,0:T(8,128)} %p_ref.1), channel_id=1, source_target_pairs={{0,16},{8,24},{16,0},{24,8},{1,17},{9,25},{17,1},{25,9},{2,18},{10... | collective-permute-start | bytes 1572872 | tf_op jit(solution)/shard_map/ppermute | solution.py:597
  3.7 0.8 reshape_squeeze.4
  4.5 0.7 pad_add_fusion
  5.2 0.6 broadcast_in_dim.67
  5.8 5.8 %all-to-all-start = ((s32[8,1,416]{2,1,0:T(1,128)}), s32[8,1,416]{2,1,0:T(1,128)S(1)}, u32[]{:S(2)}, u32[]{:S(2)}) async-start(s32[8,1,416]{2,1,0:T(1,128)} %broadcast_in_dim.67), calls=%async_computation | async-start | bytes 32768 | tf_op jit(solution)/shard_map/all_to_all | solution.py:606
  11.7 0.1 fusion.7
  11.8 0.2 multiply_select_fusion.2.refs_9_.refs_4_
  12.0 0.0 copy-start
  12.0 1.6 %copy-done = f32[1,2,16,128,128]{4,3,2,1,0:T(8,128)S(1)} copy-done((f32[1,2,16,128,128]{4,3,2,1,0:T(8,128)S(1)}, f32[1,2,16,128,128]{4,3,2,1,0:T(8,128)}, u32[]{:S(2)}) %copy-start) | copy-done | bytes 2097176
  13.6 0.0 copy-start.1
  13.6 0.0 copy-start.2
  13.6 0.1 map_rows.1
  13.7 0.0 copy-start.4
  13.7 1.0 %copy-done.4 = f32[2,16,64,128]{3,2,1,0:T(8,128)} copy-done((f32[2,16,64,128]{3,2,1,0:T(8,128)}, f32[2,16,64,128]{3,2,1,0:T(8,128)S(1)}, u32[]{:S(2)}) %copy-start.4) | copy-done | bytes 1048600
  14.7 3.5 %all-to-all-done = s32[8,1,416]{2,1,0:T(1,128)S(1)} async-done(((s32[8,1,416]{2,1,0:T(1,128)}), s32[8,1,416]{2,1,0:T(1,128)S(1)}, u32[]{:S(2)}, u32[]{:S(2)}) %all-to-all-start) | async-done | bytes 13344 | tf_op jit(solution)/shard_map/all_to_all | solution.py:606
  18.3 0.1 slice.21
  18.3 0.1 reshape.212
  18.5 0.1 broadcast_in_dim.71
  18.6 0.3 select_reduce_fusion.1
  18.9 0.1 iota_compare_fusion
  19.0 0.5 select_reduce_fusion
  19.5 0.1 mul.82
  19.6 0.0 collective-permute-done.refs_1_
  19.6 0.0 collective-permute-start.2
  19.6 0.1 stack_reshape.6
  19.7 0.1 stack_reshape.7
  19.8 0.0 copy-start.10
  19.8 0.6 collective-permute-start.3
  20.4 0.6 sine_multiply_fusion
  21.0 0.0 collective-permute-done.1.refs_2_
  21.0 0.8 %collective-permute-done.2.refs_3_ = f32[2,16,32,128]{3,2,1,0:T(8,128)} collective-permute-done((f32[2,16,32,128]{3,2,1,0:T(8,128)}, f32[2,16,32,128]{3,2,1,0:T(8,128)}, u32[]{:S(2)}, u32[]{:S(2)}) %collective-permute-start.2) | collective-permute-done | bytes 524320 | tf_op jit(solution)/shard_map/ppermute | solution.py:601
  21.8 0.0 copy-done.1
  21.8 0.0 copy-done.2
  21.8 1.0 %copy-done.13 = bf16[4,256,256]{2,1,0:T(8,128)(2,1)S(1)} copy-done((bf16[4,256,256]{2,1,0:T(8,128)(2,1)S(1)}, bf16[4,256,256]{2,1,0:T(8,128)(2,1)}, u32[]{:S(2)}) %copy-start.13) | copy-done | bytes 524312
  22.9 6.1 %forward.1 = f32[8,32,128]{2,1,0:T(8,128)} custom-call(f32[2,16,32,128]{3,2,1,0:T(8,128)S(1)} %copy-done.2, f32[2,16,32,128]{3,2,1,0:T(8,128)} %collective-permute-done.refs_1_, f32[2,16,32,128]{3,2,1,0:T(8,128)S(1)} %collective-permute-done.1.refs_2_, f32[2,16,32,128]{3,2,1,0:T(8,128)} %collective-permute-done.2.refs_3_, f32[2,16,128,128]{3,2,1,0:T(8,128)S(1)} %bitcast.26, ...), custom_call_target="tpu_custom_call" | custom-call | flops 1610612736 | bytes 4999168 | tf_op jit(solution)/shard_map/forward/pallas_call | solution.py:76
  29.0 0.0 copy-start.8
  29.0 0.6 copy-done.8
  29.7 3.4 %all-to-all-start.1 = ((f32[8,32,128]{2,1,0:T(8,128)}), f32[8,32,128]{2,1,0:T(8,128)S(1)}, u32[]{:S(2)}, u32[]{:S(2)}) async-start(f32[8,32,128]{2,1,0:T(8,128)} %forward.1), calls=%async_computation.1 | async-start | bytes 262144 | tf_op jit(solution)/shard_map/all_to_all | solution.py:632
  33.0 0.0 copy-done.10
  33.0 0.0 copy-start.12
  33.1 0.9 %copy-done.12 = f32[32,3,4,128]{3,2,1,0:T(4,128)S(1)} copy-done((f32[32,3,4,128]{3,2,1,0:T(4,128)S(1)}, f32[32,3,4,128]{3,2,1,0:T(4,128)}, u32[]{:S(2)}) %copy-start.12) | copy-done | bytes 196632
  34.0 4.6 %matrices.1.matrix_ref = f32[2048,128]{1,0:T(8,128)S(1)} custom-call(s32[2,256]{1,0:T(2,128)S(1)} %pad_add_fusion.1.refs_6_.info_hbm.refs_1_, f32[32,3,4,128]{3,2,1,0:T(4,128)S(1)} %copy-done.12), custom_call_target="tpu_custom_call" | custom-call | flops 1000000000 | bytes 198656 | tf_op jit(solution)/shard_map/matrices/pallas_call | solution.py:76
  38.6 0.0 copy-start.5
  38.6 1.0 %copy-done.5 = f32[2048,128]{1,0:T(8,128)} copy-done((f32[2048,128]{1,0:T(8,128)}, f32[2048,128]{1,0:T(8,128)S(1)}, u32[]{:S(2)}) %copy-start.5) | copy-done | bytes 1048600
  39.5 1.0 %all-to-all-done.1.parts_ref = f32[8,32,128]{2,1,0:T(8,128)S(1)} async-done(((f32[8,32,128]{2,1,0:T(8,128)}), f32[8,32,128]{2,1,0:T(8,128)S(1)}, u32[]{:S(2)}, u32[]{:S(2)}) %all-to-all-start.1) | async-done | bytes 131104 | tf_op jit(solution)/shard_map/all_to_all | solution.py:632
  40.5 1.2 %copy-done.6 = f32[2048,128]{1,0:T(8,128)S(1)} copy-done((f32[2048,128]{1,0:T(8,128)S(1)}, f32[2048,128]{1,0:T(8,128)}, u32[]{:S(2)}) %copy-start.6) | copy-done | bytes 1048600
  41.8 0.9 %regrid.1 = f32[16,32,128]{2,1,0:T(8,128)} custom-call(f32[8,32,128]{2,1,0:T(8,128)S(1)} %all-to-all-done.1.parts_ref, f32[2048,128]{1,0:T(8,128)S(1)} %copy-done.6), custom_call_target="tpu_custom_call" | custom-call | flops 10000000 | bytes 1179648 | tf_op jit(solution)/shard_map/regrid/pallas_call | solution.py:76
  42.7 5.7 %all-to-all-start.2 = ((f32[16,32,128]{2,1,0:T(8,128)}), f32[16,32,128]{2,1,0:T(8,128)S(1)}, u32[]{:S(2)}, u32[]{:S(2)}) async-start(f32[16,32,128]{2,1,0:T(8,128)} %regrid.1), calls=%async_computation.2 | async-start | bytes 524288 | tf_op jit(solution)/shard_map/all_to_all | solution.py:638
  48.4 0.0 copy-start.3
  48.4 0.0 collective-permute-done.3.refs_7_
  48.4 9.6 %all-to-all-done.2.refs_0_ = f32[16,32,128]{2,1,0:T(8,128)S(1)} async-done(((f32[16,32,128]{2,1,0:T(8,128)}), f32[16,32,128]{2,1,0:T(8,128)S(1)}, u32[]{:S(2)}, u32[]{:S(2)}) %all-to-all-start.2) | async-done | bytes 262176 | tf_op jit(solution)/shard_map/all_to_all | solution.py:638
  58.0 0.9 %copy-done.9 = f32[256,128]{1,0:T(8,128)S(1)} copy-done((f32[256,128]{1,0:T(8,128)S(1)}, f32[256,128]{1,0:T(8,128)}, u32[]{:S(2)}) %copy-start.9) | copy-done | bytes 131096
  58.9 0.7 copy-done.11
  59.6 1.0 %copy-done.14 = bf16[4,256,256]{2,1,0:T(8,128)(2,1)S(1)} copy-done((bf16[4,256,256]{2,1,0:T(8,128)(2,1)S(1)}, bf16[4,256,256]{2,1,0:T(8,128)(2,1)}, u32[]{:S(2)}) %copy-start.14) | copy-done | bytes 524312
  60.6 6.5 %inverse.1 = (f32[2,16,32,128]{3,2,1,0:T(8,128)S(1)}, f32[2,16,32,128]{3,2,1,0:T(8,128)S(1)}) custom-call(f32[16,32,128]{2,1,0:T(8,128)S(1)} %all-to-all-done.2.refs_0_, s32[2,256]{1,0:T(2,128)S(1)} %copy-done.11, f32[256,128]{1,0:T(8,128)S(1)} %copy-done.9, f32[256,128]{1,0:T(8,128)S(1)} %get-tuple-element.21.refs_8_.refs_3_, ...), custom_call_target="tpu_custom_call" | custom-call | flops 1610612736 | bytes 4212736 | tf_op jit(solution)/shard_map/inverse/pallas_call | solution.py:76
  67.2 0.0 copy-start.7
  67.2 0.1 collective-permute-start.4
  67.3 1.9 %collective-permute-done.4.refs_1_ = f32[2,16,32,128]{3,2,1,0:T(8,128)S(1)} collective-permute-done((f32[2,16,32,128]{3,2,1,0:T(8,128)S(1)}, f32[2,16,32,128]{3,2,1,0:T(8,128)S(1)}, u32[]{:S(2)}, u32[]{:S(2)}) %collective-permute-start.4) | collective-permute-done | bytes 524320 | tf_op jit(solution)/shard_map/ppermute | solution.py:601
  69.2 0.0 copy-done.3
  69.2 0.3 sums.1
  69.5 9.3 %all_to_all.30 = f32[32,1,128]{2,1,0:T(1,128)S(1)} all-to-all(f32[32,1,128]{2,1,0:T(1,128)S(1)} %bitcast.29), channel_id=1, replica_groups=mesh['coil'=4,'tile'=8] {'coil','tile'}, dimensions={0} | all-to-all | bytes 32768 | tf_op jit(solution)/shard_map/all_to_all | solution.py:645
  78.8 0.0 copy-done.7
  78.8 1.3 %finish.1 = (f32[2,16,32,128]{3,2,1,0:T(8,128)}, f32[2,16,32,128]{3,2,1,0:T(8,128)}, f32[2,16,32,128]{3,2,1,0:T(8,128)}) custom-call(f32[32,128]{1,0:T(8,128)S(1)} %bitcast.28, f32[2,16,32,128]{3,2,1,0:T(8,128)S(1)} %copy-done.7, f32[2,16,32,128]{3,2,1,0:T(8,128)S(1)} %copy-done.3, f32[2,16,32,128]{3,2,1,0:T(8,128)S(1)} %copy-done.2, ...), custom_call_target="tpu_custom_call" | custom-call | flops 10000000 | bytes 2113536 | tf_op jit(solution)/shard_map/finish/pallas_call | solution.py:76
  (19 shorter events, 0.1 us)
Async XLA Ops:
  0.6 20.3 %collective-permute-start.1 = (f32[2,16,32,128]{3,2,1,0:T(8,128)}, f32[2,16,32,128]{3,2,1,0:T(8,128)S(1)}, u32[]{:S(2)}, u32[]{:S(2)}) collective-permute-start(f32[2,16,32,128]{3,2,1,0:T(8,128)} %p_ref.1), channel_id=1, source_target_pairs={{0,8},{8,0},{16,24},{24,16},{1,9},{9,1},{17,25},{25,17},{2,10},{10... | collective-permute-start | bytes 1572872 | tf_op jit(solution)/shard_map/ppermute | solution.py:601
  1.1 18.4 %collective-permute-start = (f32[2,16,32,128]{3,2,1,0:T(8,128)}, f32[2,16,32,128]{3,2,1,0:T(8,128)}, u32[]{:S(2)}, u32[]{:S(2)}) collective-permute-start(f32[2,16,32,128]{3,2,1,0:T(8,128)} %p_ref.1), channel_id=1, source_target_pairs={{0,16},{8,24},{16,0},{24,8},{1,17},{9,25},{17,1},{25,9},{2,18},{10... | collective-permute-start | bytes 1572872 | tf_op jit(solution)/shard_map/ppermute | solution.py:597
  5.8 12.4 %all-to-all-start = ((s32[8,1,416]{2,1,0:T(1,128)}), s32[8,1,416]{2,1,0:T(1,128)S(1)}, u32[]{:S(2)}, u32[]{:S(2)}) async-start(s32[8,1,416]{2,1,0:T(1,128)} %broadcast_in_dim.67), calls=%async_computation | async-start | bytes 32768 | tf_op jit(solution)/shard_map/all_to_all | solution.py:606
  12.0 1.6 %copy-start = (f32[1,2,16,128,128]{4,3,2,1,0:T(8,128)S(1)}, f32[1,2,16,128,128]{4,3,2,1,0:T(8,128)}, u32[]{:S(2)}) copy-start(f32[1,2,16,128,128]{4,3,2,1,0:T(8,128)} %param.11) | copy-start | bytes 6291460
  13.6 8.2 %copy-start.1 = (f32[1,2,16,128,128]{4,3,2,1,0:T(8,128)S(1)}, f32[1,2,16,128,128]{4,3,2,1,0:T(8,128)}, u32[]{:S(2)}) copy-start(f32[1,2,16,128,128]{4,3,2,1,0:T(8,128)} %param.11) | copy-start | bytes 6291460
  13.6 8.2 %copy-start.2 = (f32[2,16,32,128]{3,2,1,0:T(8,128)S(1)}, f32[2,16,32,128]{3,2,1,0:T(8,128)}, u32[]{:S(2)}) copy-start(f32[2,16,32,128]{3,2,1,0:T(8,128)} %p_ref.1) | copy-start | bytes 1572868
  13.7 1.0 %copy-start.4 = (f32[2,16,64,128]{3,2,1,0:T(8,128)}, f32[2,16,64,128]{3,2,1,0:T(8,128)S(1)}, u32[]{:S(2)}) copy-start(f32[2,16,64,128]{3,2,1,0:T(8,128)S(1)} %map_rows.1) | copy-start | bytes 3145732
  19.6 2.3 %collective-permute-start.2 = (f32[2,16,32,128]{3,2,1,0:T(8,128)}, f32[2,16,32,128]{3,2,1,0:T(8,128)}, u32[]{:S(2)}, u32[]{:S(2)}) collective-permute-start(f32[2,16,32,128]{3,2,1,0:T(8,128)} %collective-permute-done.refs_1_), channel_id=1, source_target_pairs={{0,8},{8,0},{16,24},{24,16},{1,9},{9,1},{17,25},{25,17},{2,10},{10... | collective-permute-start | bytes 1572872 | tf_op jit(solution)/shard_map/ppermute | solution.py:601
  19.8 13.3 %copy-start.10 = (s32[2,256]{1,0:T(2,128)}, s32[2,256]{1,0:T(2,128)S(1)}, u32[]{:S(2)}) copy-start(s32[2,256]{1,0:T(2,128)S(1)} %pad_add_fusion.1.refs_6_.info_hbm.refs_1_) | copy-start | bytes 6148
  19.8 28.6 %collective-permute-start.3 = (f32[2,16,64,128]{3,2,1,0:T(8,128)}, f32[2,16,64,128]{3,2,1,0:T(8,128)}, u32[]{:S(2)}, u32[]{:S(2)}) collective-permute-start(f32[2,16,64,128]{3,2,1,0:T(8,128)} %copy-done.4), channel_id=1, source_target_pairs={{0,16},{8,24},{16,0},{24,8},{1,17},{9,25},{17,1},{25,9},{2,18},{10... | collective-permute-start | bytes 3145736 | tf_op jit(solution)/shard_map/ppermute | solution.py:597
  21.8 1.0 %copy-start.13 = (bf16[4,256,256]{2,1,0:T(8,128)(2,1)S(1)}, bf16[4,256,256]{2,1,0:T(8,128)(2,1)}, u32[]{:S(2)}) copy-start(bf16[4,256,256]{2,1,0:T(8,128)(2,1)} %constant.177.clone.refs_5_) | copy-start | bytes 1572868
  29.0 0.7 copy-start.8
  29.7 10.9 %all-to-all-start.1 = ((f32[8,32,128]{2,1,0:T(8,128)}), f32[8,32,128]{2,1,0:T(8,128)S(1)}, u32[]{:S(2)}, u32[]{:S(2)}) async-start(f32[8,32,128]{2,1,0:T(8,128)} %forward.1), calls=%async_computation.1 | async-start | bytes 262144 | tf_op jit(solution)/shard_map/all_to_all | solution.py:632
  33.0 0.9 %copy-start.12 = (f32[32,3,4,128]{3,2,1,0:T(4,128)S(1)}, f32[32,3,4,128]{3,2,1,0:T(4,128)}, u32[]{:S(2)}) copy-start(f32[32,3,4,128]{3,2,1,0:T(4,128)} %weights_ref) | copy-start | bytes 589828
  38.6 1.0 %copy-start.5 = (f32[2048,128]{1,0:T(8,128)}, f32[2048,128]{1,0:T(8,128)S(1)}, u32[]{:S(2)}) copy-start(f32[2048,128]{1,0:T(8,128)S(1)} %matrices.1.matrix_ref) | copy-start | bytes 3145732
  40.5 1.2 %copy-start.6 = (f32[2048,128]{1,0:T(8,128)S(1)}, f32[2048,128]{1,0:T(8,128)}, u32[]{:S(2)}) copy-start(f32[2048,128]{1,0:T(8,128)} %copy-done.5) | copy-start | bytes 3145732
  42.7 15.4 %all-to-all-start.2 = ((f32[16,32,128]{2,1,0:T(8,128)}), f32[16,32,128]{2,1,0:T(8,128)S(1)}, u32[]{:S(2)}, u32[]{:S(2)}) async-start(f32[16,32,128]{2,1,0:T(8,128)} %regrid.1), calls=%async_computation.2 | async-start | bytes 524288 | tf_op jit(solution)/shard_map/all_to_all | solution.py:638
  48.4 20.8 %copy-start.3 = (f32[2,16,32,128]{3,2,1,0:T(8,128)S(1)}, f32[2,16,32,128]{3,2,1,0:T(8,128)}, u32[]{:S(2)}) copy-start(f32[2,16,32,128]{3,2,1,0:T(8,128)} %r_ref.1) | copy-start | bytes 1572868
  58.0 0.9 %copy-start.9 = (f32[256,128]{1,0:T(8,128)S(1)}, f32[256,128]{1,0:T(8,128)}, u32[]{:S(2)}) copy-start(f32[256,128]{1,0:T(8,128)} %copy-done.8) | copy-start | bytes 393220
  58.9 0.7 copy-start.11
  59.6 1.0 %copy-start.14 = (bf16[4,256,256]{2,1,0:T(8,128)(2,1)S(1)}, bf16[4,256,256]{2,1,0:T(8,128)(2,1)}, u32[]{:S(2)}) copy-start(bf16[4,256,256]{2,1,0:T(8,128)(2,1)} %constant.177.clone.refs_5_) | copy-start | bytes 1572868
  67.2 11.6 %copy-start.7 = (f32[2,16,32,128]{3,2,1,0:T(8,128)S(1)}, f32[2,16,32,128]{3,2,1,0:T(8,128)}, u32[]{:S(2)}) copy-start(f32[2,16,32,128]{3,2,1,0:T(8,128)} %x_ref.1) | copy-start | bytes 1572868
  67.2 2.0 %collective-permute-start.4 = (f32[2,16,32,128]{3,2,1,0:T(8,128)S(1)}, f32[2,16,32,128]{3,2,1,0:T(8,128)S(1)}, u32[]{:S(2)}, u32[]{:S(2)}) collective-permute-start(f32[2,16,32,128]{3,2,1,0:T(8,128)S(1)} %get-tuple-element.16), channel_id=1, source_target_pairs={{0,8},{8,0},{16,24},{24,16},{1,9},{9,1},{17,25},{25,17},{2,10},{10... | collective-permute-start | bytes 1572872 | tf_op jit(solution)/shard_map/ppermute | solution.py:601

commit v2 on v1

--- a/solution.py
+++ b/solution.py
@@ -69,7 +69,11 @@
     return here, past < 4 - chunk
 
 
-def call(kernel, outs, scratch, operands, flops, name, hbm=(), hbm_outs=()):
+def call(kernel, outs, scratch, operands, flops, name, hbm=(), hbm_outs=(), vmem=(), fixed=()):
+    operands = list(operands)
+    for listed, space in ((fixed, pltpu.HBM), (vmem, pltpu.VMEM)):
+        for at in listed:
+            operands[at] = pltpu.with_memory_space_constraint(operands[at], space)
     here = pl.BlockSpec(memory_space=pltpu.VMEM)
     there = pl.BlockSpec(memory_space=pltpu.HBM)
     moved = sum(math.prod(a.shape) * a.dtype.itemsize for a in operands)
@@ -112,29 +116,52 @@
 
 
 def map_rows_kernel(s_ref, *refs, chips):
-    outs, sems = refs[:-1], refs[-1]
+    outs, (held, sems) = refs[:-2], refs[-2:]
     chip, _ = place_on_coil()
     own = s_ref.shape[2] // chips
-    pairs = [
-        (s_ref.at[:, :, pl.ds(pl.multiple_of((chip + chips - by) % chips * own, own), own), :], out)
-        for by, out in enumerate(outs, 1)
-    ]
-    for copy in started(pairs, sems):
-        copy.wait()
+    for by in range(1, chips):
+        rows = pl.ds(pl.multiple_of((chip + chips - by) % chips * own, own), own)
+        for copy in started([(s_ref.at[:, :, rows, :], held)], sems):
+            copy.wait()
+        for copy in started([(held, outs[by - 1])], sems):
+            copy.wait()
 
 
 def map_rows(smap, chips):
     _, planes, length, _ = smap.shape
+    shape = (2, planes, length // chips, length)
     return call(
         functools.partial(map_rows_kernel, chips=chips),
-        [(2, planes, length // chips, length)] * (chips - 1),
-        [pltpu.SemaphoreType.DMA((chips - 1,))],
+        [shape] * (chips - 1),
+        [shape, pltpu.SemaphoreType.DMA((1,))],
         [smap],
         0,
         "map_rows",
         hbm=[0],
+        fixed=[0],
         hbm_outs=range(chips - 1),
     )
+
+
+def message_kernel(owner_ref, list_ref, out_ref):
+    _, _, ntile, capacity = list_ref.shape
+    out_ref[...] = jnp.zeros_like(out_ref)
+    slots = owner_ref.shape[1]
+    for to in range(ntile):
+        for axis in range(3):
+            out_ref[to, :, axis * capacity : (axis + 1) * capacity] = list_ref[axis, 0]
+        out_ref[to, 0:1, 3 * capacity : 3 * capacity + slots] = owner_ref[...]
+
+
+def message(block_owner, owner_list):
+    ntile = owner_list.shape[2]
+    return pl.pallas_call(
+        message_kernel,
+        out_shape=jax.ShapeDtypeStruct((ntile, ntile, LANES), jnp.int32),
+        in_specs=[pl.BlockSpec(memory_space=pltpu.VMEM)] * 2,
+        out_specs=pl.BlockSpec(memory_space=pltpu.VMEM),
+        name="message",
+    )(block_owner[None], owner_list)
 
 
 def cut_boxes(info, grid, cos_ref, sin_ref, shift_ref, out_ref, gbuf, planes, chunk, slots):
@@ -262,6 +289,7 @@
         48 * planes * length**3,
         "forward",
         hbm=range(len(operands)),
+        fixed=range(count, len(operands)),
     )[0]
 
 
@@ -303,6 +331,7 @@
         10**7,
         "regrid",
         hbm_outs=[0],
+        vmem=[1],
     )[0]
 
 
@@ -452,6 +481,7 @@
         48 * planes * length**3,
         "inverse",
         hbm=range(1, len(operands)),
+        fixed=range(1, 7),
     )
 
 
@@ -565,13 +595,13 @@
 
 
 def block_offsets(gathered, slots, ntile, capacity):
-    owners = gathered[:, :slots]
-    lists = gathered[:, slots:].reshape(ntile, 3, ntile, capacity)
+    owners = gathered[:, 0, 3 * capacity : 3 * capacity + slots]
+    lists = gathered[:, :, : 3 * capacity].reshape(ntile, ntile, 3, capacity)
     earlier = jnp.tril(jnp.ones((slots, slots), jnp.int32), -1)
     same = (owners[:, :, None] == owners[:, None, :]).astype(jnp.int32)
     ranks = jnp.sum(same * earlier[None], axis=2)
     wanted = owners * capacity + ranks
-    lists = jnp.transpose(lists, (1, 2, 0, 3)).reshape(3, ntile, 1, ntile * capacity)
+    lists = jnp.transpose(lists, (2, 1, 0, 3)).reshape(3, ntile, 1, ntile * capacity)
     hit = wanted[:, :, None] == jnp.arange(ntile * capacity, dtype=jnp.int32)
     found = jnp.sum(jnp.where(hit[None], lists, 0), axis=3)
     return found[0], found[1] + owners * (LANES // ntile), found[2]
@@ -602,12 +632,10 @@
 
     p_same = [image_p] + [from_chip(image_p, by) for by in range(1, chips)]
     p_other = [other_core(piece) for piece in p_same]
-    mine = jnp.concatenate([block_owner, owner_list[:, 0].reshape(-1)])
-    gathered = lax.all_to_all(
-        jnp.broadcast_to(mine[None], (ntile, mine.shape[0])), "tile", 0, 0, tiled=True
-    )
+    gathered = lax.all_to_all(message(block_owner, owner_list), "tile", 0, 0, tiled=True)
+    gathered, _ = lax.optimization_barrier((gathered, p_same[1:]))
     far_rows = map_rows(smap, chips)
-    far_rows, p_same[1:] = lax.optimization_barrier((far_rows, p_same[1:]))
+    far_rows, _ = lax.optimization_barrier((far_rows, p_same[1:]))
     far_maps = [from_chip(rows, by) for by, rows in enumerate(far_rows, 1)]
 
     off_x, off_y, off_z = block_offsets(gathered, slots, ntile, capacity)

time: 80.7 us -> 76.1 us (0.943)
  local copies, waits for them, and re-layouts: 12 us -> 0.6 us
  Pallas kernels: 19.9 us -> 23.2 us
  waiting for transfers between devices: 16.9 us -> 18.8 us
  other arithmetic: 2.48 us -> 3.73 us
    unnamed x31 -> x10, local copies, waits for them, and re-layouts: 10.1 us -> 0.03 us
    all_to_all x1, starting transfers between devices: 3.37 us -> 5.85 us  [shards(): parts = lax.all_to_all(partial, 'tile', 0, 0, tiled=True)]
    all_to_all x1, starting transfers between devices: 5.73 us -> 3.55 us  [shards(): lax.all_to_all(done, ('coil', 'tile'), 0, 0, axis_index_groups=groups, ti...]
    all_to_all x1, waiting for transfers between devices: 1 us -> 3.04 us  [shards(): parts = lax.all_to_all(partial, 'tile', 0, 0, tiled=True)]
    pallas_call x7, Pallas kernels: 19.9 us -> 21.8 us  [call(): pl.pallas_call(kernel, out_shape=[jax.ShapeDtypeStruct(shape, jnp.float32...]
    pallas_call x0 -> x1, Pallas kernels: none -> 1.43 us  [message(): pl.pallas_call(message_kernel, out_shape=jax.ShapeDtypeStruct((ntile, nti...]
    another operation x3 -> x0, local copies, waits for them, and re-layouts: 0.94 us -> none  [the longest x1 0.79 us: shards(): mine = jnp.concatenate([block_owner, owner_list[:, 0].reshape(-1)])]
    all_to_all x1, waiting for transfers between devices: 3.52 us -> 4.39 us  [shards(): lax.all_to_all(message(block_owner, owner_list), 'tile', 0, 0, tiled=True)]
  transfers between devices with their start and end apart: 8 -> 8, of which waited for: 5 -> 4; matrix products, arithmetic and copies ran while one was open for 5% -> 6% of each run, Pallas kernels for 15% -> 20%
where the time goes in v2:
time: 76.1 us; the launch traced here: 75.5 us
  Pallas kernels  23.2 us (30%)
  starting transfers between devices  19 us (25%)
  waiting for transfers between devices  18.8 us (25%)
  blocking collectives  9.28 us (12%)
  other arithmetic  3.73 us (5%)
  between operations  0.88 us (1%)
    pallas_call x7, Pallas kernels, call(): pl.pallas_call(kernel, out_shape=[jax.ShapeDtypeStruct(shape, jnp.float32...  21.8 us
    all_to_all x1, waiting for transfers between devices, shards(): lax.all_to_all(done, ('coil', 'tile'), 0, 0, axis_index_groups=groups, ti...  9.47 us
    all_to_all x1, blocking collectives, shards(): total = lax.all_to_all(found, ('coil', 'tile'), 0, 0, tiled=True)  9.28 us
    all_to_all x1, starting transfers between devices, shards(): parts = lax.all_to_all(partial, 'tile', 0, 0, tiled=True)  5.85 us
    all_to_all x1, starting transfers between devices, shards(): lax.all_to_all(message(block_owner, owner_list), 'tile', 0, 0, tiled=True)  5.83 us
    all_to_all x1, waiting for transfers between devices, shards(): lax.all_to_all(message(block_owner, owner_list), 'tile', 0, 0, tiled=True)  4.39 us
    all_to_all x1, starting transfers between devices, shards(): lax.all_to_all(done, ('coil', 'tile'), 0, 0, axis_index_groups=groups, ti...  3.55 us
    ppermute x2, starting transfers between devices, from_chip(): return lax.ppermute(values, 'coil', pairs)  3.11 us
  transfers between devices with their start and end apart: 8, of which 4 were waited for; matrix products, arithmetic and copies ran while one was open for 6% of the time, Pallas kernels for 20%

profile of v2, /device:TPU:0, one launch (start us, length us, event | category | flops | bytes accessed | tf_op | source)
XLA Modules:
  0.0 75.5 jit_solution(6116190162227934887)
XLA Ops:
  0.6 0.5 collective-permute-start.1
  1.1 2.6 %collective-permute-start = (f32[2,16,32,128]{3,2,1,0:T(8,128)}, f32[2,16,32,128]{3,2,1,0:T(8,128)S(1)}, u32[]{:S(2)}, u32[]{:S(2)}) collective-permute-start(f32[2,16,32,128]{3,2,1,0:T(8,128)} %p_ref.1), channel_id=1, source_target_pairs={{0,16},{8,24},{16,0},{24,8},{1,17},{9,25},{17,1},{25,9},{2,18},{10... | collective-permute-start | bytes 1572872 | tf_op jit(solution)/shard_map/ppermute | solution.py:627
  3.7 1.4 %message.1 = s32[8,8,128]{2,1,0:T(8,128)} custom-call(s32[1,32]{1,0:T(1,128)} %bitcast.20, s32[3,1,8,16]{3,2,1,0:T(8,128)} %list_ref.1), custom_call_target="tpu_custom_call" | custom-call | tf_op jit(solution)/shard_map/message/pallas_call | solution.py:158
  5.1 5.8 %all-to-all-start = ((s32[8,8,128]{2,1,0:T(8,128)}), s32[8,8,128]{2,1,0:T(8,128)S(1)}, u32[]{:S(2)}, u32[]{:S(2)}) async-start(s32[8,8,128]{2,1,0:T(8,128)} %message.1), calls=%async_computation | async-start | bytes 65536 | tf_op jit(solution)/shard_map/all_to_all | solution.py:635
  11.0 0.0 copy-start
  11.1 1.4 %map_rows.1 = f32[2,16,64,128]{3,2,1,0:T(8,128)S(1)} custom-call(f32[2,16,128,128]{3,2,1,0:T(8,128)} %bitcast.13), custom_call_target="tpu_custom_call" | custom-call | bytes 2097152 | tf_op jit(solution)/shard_map/map_rows/pallas_call | solution.py:80
  12.4 0.1 fusion.7
  12.5 0.8 %multiply_select_fusion.2.refs_9_.refs_4_ = f32[32,128]{1,0:T(8,128)} fusion(f32[32]{0:T(128)S(1)} %compare_select_fusion.9, s32[128]{0:T(128)S(1)} %fusion.8, s32[32]{0:T(128)S(1)} %get-tuple-element.28, s32[128]{0:T(128)S(1)} %get-tuple-element.31, s32[128]{0:T(128)S(1)} %get-tuple-element.30, s32[32]{0:T(128)S(1)} %get-tuple-element.29, ...), kind=kLoop, calls=%fused_computation.21 | loop fusion | flops 81920 | bytes 18432 | tf_op jit(solution)/shard_map/jit(_where)/select_n | solution.py:657
  13.3 4.4 %all-to-all-done = s32[8,8,128]{2,1,0:T(8,128)S(1)} async-done(((s32[8,8,128]{2,1,0:T(8,128)}), s32[8,8,128]{2,1,0:T(8,128)S(1)}, u32[]{:S(2)}, u32[]{:S(2)}) %all-to-all-start) | async-done | bytes 32800 | tf_op jit(solution)/shard_map/all_to_all | solution.py:635
  17.7 0.0 collective-permute-done.refs_1_
  17.7 0.1 multiply_reduce_fusion
  17.8 0.1 mul.108
  17.8 0.3 select_reduce_fusion.1
  18.1 0.1 iota_compare_fusion
  18.3 0.1 reshape.319
  18.4 0.1 copy.14
  18.4 0.1 broadcast_in_dim.66
  18.5 0.5 select_reduce_fusion
  19.0 0.1 mul.111
  19.1 0.1 squeeze.15
  19.2 0.1 squeeze.14
  19.3 0.5 collective-permute-start.3
  19.8 0.1 collective-permute-start.2
  19.9 0.6 pad_add_fusion.refs_6_.info_hbm.refs_1_
  20.5 1.3 %sine_multiply_fusion = (f32[256,128]{1,0:T(8,128)}, f32[256,128]{1,0:T(8,128)}) fusion(f32[128]{0:T(128)S(1)} %compare_select_fusion.10, s32[128]{0:T(128)S(1)} %fusion.8, s32[256]{0:T(256)S(1)} %mul.111), kind=kLoop, calls=%fused_computation.9 | loop fusion | flops 491520 | bytes 264192 | tf_op jit(solution)/shard_map/mul | solution.py:651
  21.8 0.0 collective-permute-done.1.refs_2_
  21.8 0.0 collective-permute-done.2.refs_3_
  21.8 0.0 copy-done
  21.8 0.0 copy-start.3
  21.8 0.0 copy-start.4
  21.8 6.6 %forward.1 = f32[8,32,128]{2,1,0:T(8,128)} custom-call(f32[2,16,32,128]{3,2,1,0:T(8,128)S(1)} %copy-done, f32[2,16,32,128]{3,2,1,0:T(8,128)S(1)} %collective-permute-done.refs_1_, f32[2,16,32,128]{3,2,1,0:T(8,128)S(1)} %collective-permute-done.1.refs_2_, f32[2,16,32,128]{3,2,1,0:T(8,128)S(1)} %collective-permute-done.2.refs_3_, ...), custom_call_target="tpu_custom_call" | custom-call | flops 1610612736 | bytes 4999168 | tf_op jit(solution)/shard_map/forward/pallas_call | solution.py:80
  28.5 5.8 %all-to-all-start.1 = ((f32[8,32,128]{2,1,0:T(8,128)}), f32[8,32,128]{2,1,0:T(8,128)S(1)}, u32[]{:S(2)}, u32[]{:S(2)}) async-start(f32[8,32,128]{2,1,0:T(8,128)} %forward.1), calls=%async_computation.1 | async-start | bytes 262144 | tf_op jit(solution)/shard_map/all_to_all | solution.py:660
  34.3 0.0 copy-done.3
  34.3 0.0 copy-done.4
  34.3 4.6 %matrices.1.matrix_ref = f32[2048,128]{1,0:T(8,128)S(1)} custom-call(s32[2,256]{1,0:T(2,128)S(1)} %copy-done.3, f32[32,3,4,128]{3,2,1,0:T(4,128)S(1)} %copy-done.4), custom_call_target="tpu_custom_call" | custom-call | flops 1000000000 | bytes 198656 | tf_op jit(solution)/shard_map/matrices/pallas_call | solution.py:80
  38.9 3.0 %all-to-all-done.1.parts_ref = f32[8,32,128]{2,1,0:T(8,128)S(1)} async-done(((f32[8,32,128]{2,1,0:T(8,128)}), f32[8,32,128]{2,1,0:T(8,128)S(1)}, u32[]{:S(2)}, u32[]{:S(2)}) %all-to-all-start.1) | async-done | bytes 131104 | tf_op jit(solution)/shard_map/all_to_all | solution.py:660
  41.9 0.9 %regrid.1 = f32[16,32,128]{2,1,0:T(8,128)} custom-call(f32[8,32,128]{2,1,0:T(8,128)S(1)} %all-to-all-done.1.parts_ref, f32[2048,128]{1,0:T(8,128)S(1)} %matrices.1.matrix_ref), custom_call_target="tpu_custom_call" | custom-call | flops 10000000 | bytes 1179648 | tf_op jit(solution)/shard_map/regrid/pallas_call | solution.py:80
  42.8 3.5 %all-to-all-start.2 = ((f32[16,32,128]{2,1,0:T(8,128)}), f32[16,32,128]{2,1,0:T(8,128)S(1)}, u32[]{:S(2)}, u32[]{:S(2)}) async-start(f32[16,32,128]{2,1,0:T(8,128)} %regrid.1), calls=%async_computation.2 | async-start | bytes 524288 | tf_op jit(solution)/shard_map/all_to_all | solution.py:666
  46.4 0.0 copy-start.1
  46.4 0.0 collective-permute-done.3.refs_7_
  46.4 9.5 %all-to-all-done.2.refs_0_ = f32[16,32,128]{2,1,0:T(8,128)S(1)} async-done(((f32[16,32,128]{2,1,0:T(8,128)}), f32[16,32,128]{2,1,0:T(8,128)S(1)}, u32[]{:S(2)}, u32[]{:S(2)}) %all-to-all-start.2) | async-done | bytes 262176 | tf_op jit(solution)/shard_map/all_to_all | solution.py:666
  55.9 6.7 %inverse.1 = (f32[2,16,32,128]{3,2,1,0:T(8,128)S(1)}, f32[2,16,32,128]{3,2,1,0:T(8,128)S(1)}) custom-call(f32[16,32,128]{2,1,0:T(8,128)S(1)} %all-to-all-done.2.refs_0_, s32[2,256]{1,0:T(2,128)} %pad_add_fusion.refs_6_.info_hbm.refs_1_, f32[256,128]{1,0:T(8,128)} %get-tuple-element.27.refs_7_.refs_2_, f32[256,128]{1,0:T(8,128)} %get-tuple-element.26.refs_8_.refs_3_, ...), custom_call_target="tpu_custom_call" | custom-call | flops 1610612736 | bytes 4212736 | tf_op jit(solution)/shard_map/inverse/pallas_call | solution.py:80
  62.6 0.0 copy-start.2
  62.6 0.1 collective-permute-start.4
  62.7 1.9 %collective-permute-done.4.refs_1_ = f32[2,16,32,128]{3,2,1,0:T(8,128)S(1)} collective-permute-done((f32[2,16,32,128]{3,2,1,0:T(8,128)S(1)}, f32[2,16,32,128]{3,2,1,0:T(8,128)S(1)}, u32[]{:S(2)}, u32[]{:S(2)}) %collective-permute-start.4) | collective-permute-done | bytes 524320 | tf_op jit(solution)/shard_map/ppermute | solution.py:631
  64.6 0.0 copy-done.1
  64.6 0.3 sums.1
  64.9 9.3 %all_to_all.26 = f32[32,1,128]{2,1,0:T(1,128)S(1)} all-to-all(f32[32,1,128]{2,1,0:T(1,128)S(1)} %bitcast.12), channel_id=1, replica_groups=mesh['coil'=4,'tile'=8] {'coil','tile'}, dimensions={0} | all-to-all | bytes 32768 | tf_op jit(solution)/shard_map/all_to_all | solution.py:673
  74.2 0.0 copy-done.2
  74.2 1.3 %finish.1 = (f32[2,16,32,128]{3,2,1,0:T(8,128)}, f32[2,16,32,128]{3,2,1,0:T(8,128)}, f32[2,16,32,128]{3,2,1,0:T(8,128)}) custom-call(f32[32,128]{1,0:T(8,128)S(1)} %bitcast.11, f32[2,16,32,128]{3,2,1,0:T(8,128)S(1)} %copy-done.2, f32[2,16,32,128]{3,2,1,0:T(8,128)S(1)} %copy-done.1, f32[2,16,32,128]{3,2,1,0:T(8,128)S(1)} %copy-done, ...), custom_call_target="tpu_custom_call" | custom-call | flops 10000000 | bytes 2113536 | tf_op jit(solution)/shard_map/finish/pallas_call | solution.py:80
  (11 shorter events, 0.1 us)
Async XLA Ops:
  0.6 21.2 %collective-permute-start.1 = (f32[2,16,32,128]{3,2,1,0:T(8,128)}, f32[2,16,32,128]{3,2,1,0:T(8,128)S(1)}, u32[]{:S(2)}, u32[]{:S(2)}) collective-permute-start(f32[2,16,32,128]{3,2,1,0:T(8,128)} %p_ref.1), channel_id=1, source_target_pairs={{0,8},{8,0},{16,24},{24,16},{1,9},{9,1},{17,25},{25,17},{2,10},{10... | collective-permute-start | bytes 1572872 | tf_op jit(solution)/shard_map/ppermute | solution.py:631
  1.1 16.5 %collective-permute-start = (f32[2,16,32,128]{3,2,1,0:T(8,128)}, f32[2,16,32,128]{3,2,1,0:T(8,128)S(1)}, u32[]{:S(2)}, u32[]{:S(2)}) collective-permute-start(f32[2,16,32,128]{3,2,1,0:T(8,128)} %p_ref.1), channel_id=1, source_target_pairs={{0,16},{8,24},{16,0},{24,8},{1,17},{9,25},{17,1},{25,9},{2,18},{10... | collective-permute-start | bytes 1572872 | tf_op jit(solution)/shard_map/ppermute | solution.py:627
  5.1 12.5 %all-to-all-start = ((s32[8,8,128]{2,1,0:T(8,128)}), s32[8,8,128]{2,1,0:T(8,128)S(1)}, u32[]{:S(2)}, u32[]{:S(2)}) async-start(s32[8,8,128]{2,1,0:T(8,128)} %message.1), calls=%async_computation | async-start | bytes 65536 | tf_op jit(solution)/shard_map/all_to_all | solution.py:635
  11.0 10.8 %copy-start = (f32[2,16,32,128]{3,2,1,0:T(8,128)S(1)}, f32[2,16,32,128]{3,2,1,0:T(8,128)}, u32[]{:S(2)}) copy-start(f32[2,16,32,128]{3,2,1,0:T(8,128)} %p_ref.1) | copy-start | bytes 1572868
  19.3 27.1 %collective-permute-start.3 = (f32[2,16,64,128]{3,2,1,0:T(8,128)S(1)}, f32[2,16,64,128]{3,2,1,0:T(8,128)}, u32[]{:S(2)}, u32[]{:S(2)}) collective-permute-start(f32[2,16,64,128]{3,2,1,0:T(8,128)S(1)} %map_rows.1), channel_id=1, source_target_pairs={{0,16},{8,24},{16,0},{24,8},{1,17},{9,25},{17,1},{25,9},{2,18},{10... | collective-permute-start | bytes 3145736 | tf_op jit(solution)/shard_map/ppermute | solution.py:627
  19.8 2.0 %collective-permute-start.2 = (f32[2,16,32,128]{3,2,1,0:T(8,128)S(1)}, f32[2,16,32,128]{3,2,1,0:T(8,128)S(1)}, u32[]{:S(2)}, u32[]{:S(2)}) collective-permute-start(f32[2,16,32,128]{3,2,1,0:T(8,128)S(1)} %collective-permute-done.refs_1_), channel_id=1, source_target_pairs={{0,8},{8,0},{16,24},{24,16},{1,9},{9,1},{17,25},{25,17},{2,10},{10... | collective-permute-start | bytes 1572872 | tf_op jit(solution)/shard_map/ppermute | solution.py:631
  21.8 12.5 %copy-start.3 = (s32[2,256]{1,0:T(2,128)S(1)}, s32[2,256]{1,0:T(2,128)}, u32[]{:S(2)}) copy-start(s32[2,256]{1,0:T(2,128)} %pad_add_fusion.refs_6_.info_hbm.refs_1_) | copy-start | bytes 6148
  21.8 12.5 %copy-start.4 = (f32[32,3,4,128]{3,2,1,0:T(4,128)S(1)}, f32[32,3,4,128]{3,2,1,0:T(4,128)}, u32[]{:S(2)}) copy-start(f32[32,3,4,128]{3,2,1,0:T(4,128)} %weights_ref) | copy-start | bytes 589828
  28.5 13.5 %all-to-all-start.1 = ((f32[8,32,128]{2,1,0:T(8,128)}), f32[8,32,128]{2,1,0:T(8,128)S(1)}, u32[]{:S(2)}, u32[]{:S(2)}) async-start(f32[8,32,128]{2,1,0:T(8,128)} %forward.1), calls=%async_computation.1 | async-start | bytes 262144 | tf_op jit(solution)/shard_map/all_to_all | solution.py:660
  42.8 13.0 %all-to-all-start.2 = ((f32[16,32,128]{2,1,0:T(8,128)}), f32[16,32,128]{2,1,0:T(8,128)S(1)}, u32[]{:S(2)}, u32[]{:S(2)}) async-start(f32[16,32,128]{2,1,0:T(8,128)} %regrid.1), calls=%async_computation.2 | async-start | bytes 524288 | tf_op jit(solution)/shard_map/all_to_all | solution.py:666
  46.4 18.2 %copy-start.1 = (f32[2,16,32,128]{3,2,1,0:T(8,128)S(1)}, f32[2,16,32,128]{3,2,1,0:T(8,128)}, u32[]{:S(2)}) copy-start(f32[2,16,32,128]{3,2,1,0:T(8,128)} %r_ref.1) | copy-start | bytes 1572868
  62.6 11.6 %copy-start.2 = (f32[2,16,32,128]{3,2,1,0:T(8,128)S(1)}, f32[2,16,32,128]{3,2,1,0:T(8,128)}, u32[]{:S(2)}) copy-start(f32[2,16,32,128]{3,2,1,0:T(8,128)} %x_ref.1) | copy-start | bytes 1572868
  62.6 2.0 %collective-permute-start.4 = (f32[2,16,32,128]{3,2,1,0:T(8,128)S(1)}, f32[2,16,32,128]{3,2,1,0:T(8,128)S(1)}, u32[]{:S(2)}, u32[]{:S(2)}) collective-permute-start(f32[2,16,32,128]{3,2,1,0:T(8,128)S(1)} %get-tuple-element.16), channel_id=1, source_target_pairs={{0,8},{8,0},{16,24},{24,16},{1,9},{9,1},{17,25},{25,17},{2,10},{10... | collective-permute-start | bytes 1572872 | tf_op jit(solution)/shard_map/ppermute | solution.py:631

commit v3 on v2

--- a/solution.py
+++ b/solution.py
@@ -79,7 +79,12 @@
     moved = sum(math.prod(a.shape) * a.dtype.itemsize for a in operands)
     return pl.pallas_call(
         kernel,
-        out_shape=[jax.ShapeDtypeStruct(shape, jnp.float32) for shape in outs],
+        out_shape=[
+            pltpu.HBM(shape, jnp.float32)
+            if at in hbm_outs
+            else jax.ShapeDtypeStruct(shape, jnp.float32)
+            for at, shape in enumerate(outs)
+        ],
         in_specs=[there if at in hbm else here for at in range(len(operands))],
         out_specs=[there if at in hbm_outs else here for at in range(len(outs))],
         scratch_shapes=[
@@ -558,8 +563,10 @@
         turned = pltpu.roll(
             jnp.concatenate([w_y, w_y], axis=0), info[1, base + block] % 4, 0
         )[:4]
-        left = jnp.concatenate([turned * turned[e : e + 1] for e in range(4)], axis=0)
-        done = dot_right(left, halves(jnp.concatenate(right, axis=0)), ((1,), (1,)))
+        left = halves(jnp.concatenate([turned * turned[e : e + 1] for e in range(4)], axis=0))
+        high, low = halves(jnp.concatenate(right, axis=0))
+        both = dot_bf16(jnp.concatenate(left, axis=0), high, ((1,), (1,)))
+        done = both[:16] + both[16:] + dot_bf16(left[0], low, ((1,), (1,)))
         for f in range(4):
             lanes = done[:, f // 2 * LANES : (f // 2 + 1) * LANES]
             if f % 2:
@@ -631,13 +638,9 @@
         return lax.ppermute(values, "coil", pairs)
 
     p_same = [image_p] + [from_chip(image_p, by) for by in range(1, chips)]
-    p_other = [other_core(piece) for piece in p_same]
+    p_other = [other_core(image_p)]
     gathered = lax.all_to_all(message(block_owner, owner_list), "tile", 0, 0, tiled=True)
-    gathered, _ = lax.optimization_barrier((gathered, p_same[1:]))
     far_rows = map_rows(smap, chips)
-    far_rows, _ = lax.optimization_barrier((far_rows, p_same[1:]))
-    far_maps = [from_chip(rows, by) for by, rows in enumerate(far_rows, 1)]
-
     off_x, off_y, off_z = block_offsets(gathered, slots, ntile, capacity)
     info = jnp.stack(
         [(off_y // chunk * length + off_z).reshape(-1), (off_y % chunk).reshape(-1)]
@@ -655,7 +658,12 @@
     sine = jnp.where(row_ri == 0, 1.0, -1.0) * jnp.sin(angle)
     shift = jnp.where(row_ri == lane_ri[None], jnp.cos(angle), sine)
     shift = jnp.where(lane_q[None] % 4 == row_q, shift / math.sqrt(length), 0.0)
-    partial = forward(p_same + p_other, smap, tables, info, phases, shift, chunk, slots)
+    p_far, far_rows, info, phases, shift = lax.optimization_barrier(
+        (p_same[1:], far_rows, info, phases, shift)
+    )
+    p_other += [other_core(piece) for piece in p_far]
+    far_maps = [from_chip(rows, by) for by, rows in enumerate(far_rows, 1)]
+    partial = forward([image_p, *p_far, *p_other], smap, tables, info, phases, shift, chunk, slots)
     partial, weights = lax.optimization_barrier((partial, kb_weights))
     parts = lax.all_to_all(partial, "tile", 0, 0, tiled=True)
     done = regrid(parts, block_matrices(info, weights), chips * ntile)

time: 76.1 us -> 74.5 us (0.979)
  starting transfers between devices: 19 us -> 16.6 us
    all_to_all x1, waiting for transfers between devices: 9.47 us -> 6.85 us  [shards(): lax.all_to_all(done, ('coil', 'tile'), 0, 0, axis_index_groups=groups, ti...]
    all_to_all x1, starting transfers between devices: 5.85 us -> 3.38 us  [shards(): parts = lax.all_to_all(partial, 'tile', 0, 0, tiled=True)]
    ppermute x2, waiting for transfers between devices: 0.01 us -> 2.3 us  [from_chip(): return lax.ppermute(values, 'coil', pairs)]
    ppermute x3, waiting for transfers between devices: 1.9 us -> 3.19 us  [other_core(): return lax.ppermute(values, 'coil', pairs)]
    all_to_all x1, waiting for transfers between devices: 4.39 us -> 3.51 us  [shards(): lax.all_to_all(message(block_owner, owner_list), 'tile', 0, 0, tiled=True)]
  transfers between devices with their start and end apart: 8 -> 8, of which waited for: 4 -> 6; matrix products, arithmetic and copies ran while one was open for 6% -> 6% of each run, Pallas kernels for 20% -> 21%
where the time goes in v3:
time: 74.5 us; the launch traced here: 73.9 us
  Pallas kernels  23.7 us (32%)
  waiting for transfers between devices  19.1 us (26%)
  starting transfers between devices  16.6 us (22%)
  blocking collectives  9.28 us (12%)
  other arithmetic  3.73 us (5%)
  between operations  0.87 us (1%)
    pallas_call x7, Pallas kernels, call(): pl.pallas_call(kernel, out_shape=[pltpu.HBM(shape, jnp.float32) if at in...  22.3 us
    all_to_all x1, blocking collectives, shards(): total = lax.all_to_all(found, ('coil', 'tile'), 0, 0, tiled=True)  9.28 us
    all_to_all x1, waiting for transfers between devices, shards(): lax.all_to_all(done, ('coil', 'tile'), 0, 0, axis_index_groups=groups, ti...  6.85 us
    all_to_all x1, starting transfers between devices, shards(): lax.all_to_all(message(block_owner, owner_list), 'tile', 0, 0, tiled=True)  5.83 us
    all_to_all x1, starting transfers between devices, shards(): lax.all_to_all(done, ('coil', 'tile'), 0, 0, axis_index_groups=groups, ti...  3.55 us
    all_to_all x1, waiting for transfers between devices, shards(): lax.all_to_all(message(block_owner, owner_list), 'tile', 0, 0, tiled=True)  3.51 us
    all_to_all x1, starting transfers between devices, shards(): parts = lax.all_to_all(partial, 'tile', 0, 0, tiled=True)  3.38 us
    all_to_all x1, waiting for transfers between devices, shards(): parts = lax.all_to_all(partial, 'tile', 0, 0, tiled=True)  3.23 us
  transfers between devices with their start and end apart: 8, of which 6 were waited for; matrix products, arithmetic and copies ran while one was open for 6% of the time, Pallas kernels for 21%

profile of v3, /device:TPU:0, one launch (start us, length us, event | category | flops | bytes accessed | tf_op | source)
XLA Modules:
  0.0 73.9 jit_solution(3829692904147796447)
XLA Ops:
  0.6 0.5 collective-permute-start.1
  1.1 2.6 %collective-permute-start = (f32[2,16,32,128]{3,2,1,0:T(8,128)}, f32[2,16,32,128]{3,2,1,0:T(8,128)S(1)}, u32[]{:S(2)}, u32[]{:S(2)}) collective-permute-start(f32[2,16,32,128]{3,2,1,0:T(8,128)} %p_ref.1), channel_id=1, source_target_pairs={{0,16},{8,24},{16,0},{24,8},{1,17},{9,25},{17,1},{25,9},{2,18},{10... | collective-permute-start | bytes 1572872 | tf_op jit(solution)/shard_map/ppermute | solution.py:634
  3.7 1.4 %message.1 = s32[8,8,128]{2,1,0:T(8,128)} custom-call(s32[1,32]{1,0:T(1,128)} %bitcast.20, s32[3,1,8,16]{3,2,1,0:T(8,128)} %list_ref.1), custom_call_target="tpu_custom_call" | custom-call | tf_op jit(solution)/shard_map/message/pallas_call | solution.py:163
  5.1 5.8 %all-to-all-start = ((s32[8,8,128]{2,1,0:T(8,128)}), s32[8,8,128]{2,1,0:T(8,128)S(1)}, u32[]{:S(2)}, u32[]{:S(2)}) async-start(s32[8,8,128]{2,1,0:T(8,128)} %message.1), calls=%async_computation | async-start | bytes 65536 | tf_op jit(solution)/shard_map/all_to_all | solution.py:642
  11.0 0.0 copy-start
  11.1 0.1 fusion.7
  11.1 2.3 %map_rows.1 = f32[2,16,64,128]{3,2,1,0:T(8,128)} custom-call(f32[2,16,128,128]{3,2,1,0:T(8,128)} %bitcast.13), custom_call_target="tpu_custom_call" | custom-call | bytes 2097152 | tf_op jit(solution)/shard_map/map_rows/pallas_call | solution.py:80
  13.4 0.8 %multiply_select_fusion.2.refs_9_.refs_4_ = f32[32,128]{1,0:T(8,128)} fusion(f32[32]{0:T(128)S(1)} %compare_select_fusion.9, s32[128]{0:T(128)S(1)} %fusion.8, s32[32]{0:T(128)S(1)} %get-tuple-element.36, s32[128]{0:T(128)S(1)} %get-tuple-element.39, s32[128]{0:T(128)S(1)} %get-tuple-element.38, s32[32]{0:T(128)S(1)} %get-tuple-element.37, ...), kind=kLoop, calls=%fused_computation.21 | loop fusion | flops 81920 | bytes 18432 | tf_op jit(solution)/shard_map/jit(_where)/select_n | solution.py:660
  14.2 3.5 %all-to-all-done = s32[8,8,128]{2,1,0:T(8,128)S(1)} async-done(((s32[8,8,128]{2,1,0:T(8,128)}), s32[8,8,128]{2,1,0:T(8,128)S(1)}, u32[]{:S(2)}, u32[]{:S(2)}) %all-to-all-start) | async-done | bytes 32800 | tf_op jit(solution)/shard_map/all_to_all | solution.py:642
  17.7 0.1 multiply_reduce_fusion
  17.8 0.1 mul.108
  17.8 0.3 select_reduce_fusion.1
  18.1 0.1 iota_compare_fusion
  18.3 0.1 reshape.319
  18.4 0.1 copy.14
  18.4 0.1 broadcast_in_dim.66
  18.5 0.5 select_reduce_fusion
  19.0 0.1 mul.111
  19.1 0.1 squeeze.15
  19.2 0.1 squeeze.14
  19.3 0.6 pad_add_fusion.refs_6_.info_hbm.refs_1_
  19.9 1.3 %sine_multiply_fusion = (f32[256,128]{1,0:T(8,128)}, f32[256,128]{1,0:T(8,128)}) fusion(f32[128]{0:T(128)S(1)} %compare_select_fusion.10, s32[128]{0:T(128)S(1)} %fusion.8, s32[256]{0:T(256)S(1)} %mul.111), kind=kLoop, calls=%fused_computation.9 | loop fusion | flops 491520 | bytes 264192 | tf_op jit(solution)/shard_map/mul | solution.py:654
  21.2 0.0 collective-permute-done.refs_1_
  21.2 0.0 copy-start.3
  21.2 0.0 copy-start.4
  21.2 0.1 collective-permute-start.2
  21.3 0.6 collective-permute-start.3
  21.9 0.0 collective-permute-done.1.refs_2_
  21.9 1.3 %collective-permute-done.2.refs_3_ = f32[2,16,32,128]{3,2,1,0:T(8,128)S(1)} collective-permute-done((f32[2,16,32,128]{3,2,1,0:T(8,128)S(1)}, f32[2,16,32,128]{3,2,1,0:T(8,128)S(1)}, u32[]{:S(2)}, u32[]{:S(2)}) %collective-permute-start.2) | collective-permute-done | bytes 524320 | tf_op jit(solution)/shard_map/ppermute | solution.py:638
  23.2 0.0 copy-done
  23.2 6.6 %forward.1 = f32[8,32,128]{2,1,0:T(8,128)} custom-call(f32[2,16,32,128]{3,2,1,0:T(8,128)S(1)} %copy-done, f32[2,16,32,128]{3,2,1,0:T(8,128)S(1)} %collective-permute-done.refs_1_, f32[2,16,32,128]{3,2,1,0:T(8,128)S(1)} %collective-permute-done.1.refs_2_, f32[2,16,32,128]{3,2,1,0:T(8,128)S(1)} %collective-permute-done.2.refs_3_, ...), custom_call_target="tpu_custom_call" | custom-call | flops 1610612736 | bytes 4999168 | tf_op jit(solution)/shard_map/forward/pallas_call | solution.py:80
  29.8 3.4 %all-to-all-start.1 = ((f32[8,32,128]{2,1,0:T(8,128)}), f32[8,32,128]{2,1,0:T(8,128)S(1)}, u32[]{:S(2)}, u32[]{:S(2)}) async-start(f32[8,32,128]{2,1,0:T(8,128)} %forward.1), calls=%async_computation.1 | async-start | bytes 262144 | tf_op jit(solution)/shard_map/all_to_all | solution.py:668
  33.2 0.0 copy-done.3
  33.2 0.0 copy-done.4
  33.2 4.2 %matrices.1.matrix_ref = f32[2048,128]{1,0:T(8,128)S(1)} custom-call(s32[2,256]{1,0:T(2,128)S(1)} %copy-done.3, f32[32,3,4,128]{3,2,1,0:T(4,128)S(1)} %copy-done.4), custom_call_target="tpu_custom_call" | custom-call | flops 1000000000 | bytes 198656 | tf_op jit(solution)/shard_map/matrices/pallas_call | solution.py:80
  37.4 3.2 %all-to-all-done.1.parts_ref = f32[8,32,128]{2,1,0:T(8,128)S(1)} async-done(((f32[8,32,128]{2,1,0:T(8,128)}), f32[8,32,128]{2,1,0:T(8,128)S(1)}, u32[]{:S(2)}, u32[]{:S(2)}) %all-to-all-start.1) | async-done | bytes 131104 | tf_op jit(solution)/shard_map/all_to_all | solution.py:668
  40.7 0.9 %regrid.1 = f32[16,32,128]{2,1,0:T(8,128)} custom-call(f32[8,32,128]{2,1,0:T(8,128)S(1)} %all-to-all-done.1.parts_ref, f32[2048,128]{1,0:T(8,128)S(1)} %matrices.1.matrix_ref), custom_call_target="tpu_custom_call" | custom-call | flops 10000000 | bytes 1179648 | tf_op jit(solution)/shard_map/regrid/pallas_call | solution.py:80
  41.5 3.5 %all-to-all-start.2 = ((f32[16,32,128]{2,1,0:T(8,128)}), f32[16,32,128]{2,1,0:T(8,128)S(1)}, u32[]{:S(2)}, u32[]{:S(2)}) async-start(f32[16,32,128]{2,1,0:T(8,128)} %regrid.1), calls=%async_computation.2 | async-start | bytes 524288 | tf_op jit(solution)/shard_map/all_to_all | solution.py:674
  45.1 0.0 copy-start.1
  45.1 2.3 %collective-permute-done.3.refs_7_ = f32[2,16,64,128]{3,2,1,0:T(8,128)S(1)} collective-permute-done((f32[2,16,64,128]{3,2,1,0:T(8,128)}, f32[2,16,64,128]{3,2,1,0:T(8,128)S(1)}, u32[]{:S(2)}, u32[]{:S(2)}) %collective-permute-start.3) | collective-permute-done | bytes 1048608 | tf_op jit(solution)/shard_map/ppermute | solution.py:634
  47.4 6.9 %all-to-all-done.2.refs_0_ = f32[16,32,128]{2,1,0:T(8,128)S(1)} async-done(((f32[16,32,128]{2,1,0:T(8,128)}), f32[16,32,128]{2,1,0:T(8,128)S(1)}, u32[]{:S(2)}, u32[]{:S(2)}) %all-to-all-start.2) | async-done | bytes 262176 | tf_op jit(solution)/shard_map/all_to_all | solution.py:674
  54.3 6.7 %inverse.1 = (f32[2,16,32,128]{3,2,1,0:T(8,128)S(1)}, f32[2,16,32,128]{3,2,1,0:T(8,128)S(1)}) custom-call(f32[16,32,128]{2,1,0:T(8,128)S(1)} %all-to-all-done.2.refs_0_, s32[2,256]{1,0:T(2,128)} %pad_add_fusion.refs_6_.info_hbm.refs_1_, f32[256,128]{1,0:T(8,128)} %get-tuple-element.17.refs_7_.refs_2_, f32[256,128]{1,0:T(8,128)} %get-tuple-element.18.refs_8_.refs_3_, ...), custom_call_target="tpu_custom_call" | custom-call | flops 1610612736 | bytes 4212736 | tf_op jit(solution)/shard_map/inverse/pallas_call | solution.py:80
  61.0 0.0 copy-start.2
  61.0 0.1 collective-permute-start.4
  61.1 1.9 %collective-permute-done.4.refs_1_ = f32[2,16,32,128]{3,2,1,0:T(8,128)S(1)} collective-permute-done((f32[2,16,32,128]{3,2,1,0:T(8,128)S(1)}, f32[2,16,32,128]{3,2,1,0:T(8,128)S(1)}, u32[]{:S(2)}, u32[]{:S(2)}) %collective-permute-start.4) | collective-permute-done | bytes 524320 | tf_op jit(solution)/shard_map/ppermute | solution.py:638
  63.0 0.0 copy-done.1
  63.0 0.3 sums.1
  63.3 9.3 %all_to_all.26 = f32[32,1,128]{2,1,0:T(1,128)S(1)} all-to-all(f32[32,1,128]{2,1,0:T(1,128)S(1)} %bitcast.12), channel_id=1, replica_groups=mesh['coil'=4,'tile'=8] {'coil','tile'}, dimensions={0} | all-to-all | bytes 32768 | tf_op jit(solution)/shard_map/all_to_all | solution.py:681
  72.6 0.0 copy-done.2
  72.6 1.3 %finish.1 = (f32[2,16,32,128]{3,2,1,0:T(8,128)}, f32[2,16,32,128]{3,2,1,0:T(8,128)}, f32[2,16,32,128]{3,2,1,0:T(8,128)}) custom-call(f32[32,128]{1,0:T(8,128)S(1)} %bitcast.11, f32[2,16,32,128]{3,2,1,0:T(8,128)S(1)} %copy-done.2, f32[2,16,32,128]{3,2,1,0:T(8,128)S(1)} %copy-done.1, f32[2,16,32,128]{3,2,1,0:T(8,128)S(1)} %copy-done, ...), custom_call_target="tpu_custom_call" | custom-call | flops 10000000 | bytes 2113536 | tf_op jit(solution)/shard_map/finish/pallas_call | solution.py:80
  (11 shorter events, 0.1 us)
Async XLA Ops:
  0.6 21.2 %collective-permute-start.1 = (f32[2,16,32,128]{3,2,1,0:T(8,128)}, f32[2,16,32,128]{3,2,1,0:T(8,128)S(1)}, u32[]{:S(2)}, u32[]{:S(2)}) collective-permute-start(f32[2,16,32,128]{3,2,1,0:T(8,128)} %p_ref.1), channel_id=1, source_target_pairs={{0,8},{8,0},{16,24},{24,16},{1,9},{9,1},{17,25},{25,17},{2,10},{10... | collective-permute-start | bytes 1572872 | tf_op jit(solution)/shard_map/ppermute | solution.py:638
  1.1 20.0 %collective-permute-start = (f32[2,16,32,128]{3,2,1,0:T(8,128)}, f32[2,16,32,128]{3,2,1,0:T(8,128)S(1)}, u32[]{:S(2)}, u32[]{:S(2)}) collective-permute-start(f32[2,16,32,128]{3,2,1,0:T(8,128)} %p_ref.1), channel_id=1, source_target_pairs={{0,16},{8,24},{16,0},{24,8},{1,17},{9,25},{17,1},{25,9},{2,18},{10... | collective-permute-start | bytes 1572872 | tf_op jit(solution)/shard_map/ppermute | solution.py:634
  5.1 12.5 %all-to-all-start = ((s32[8,8,128]{2,1,0:T(8,128)}), s32[8,8,128]{2,1,0:T(8,128)S(1)}, u32[]{:S(2)}, u32[]{:S(2)}) async-start(s32[8,8,128]{2,1,0:T(8,128)} %message.1), calls=%async_computation | async-start | bytes 65536 | tf_op jit(solution)/shard_map/all_to_all | solution.py:642
  11.0 12.1 %copy-start = (f32[2,16,32,128]{3,2,1,0:T(8,128)S(1)}, f32[2,16,32,128]{3,2,1,0:T(8,128)}, u32[]{:S(2)}) copy-start(f32[2,16,32,128]{3,2,1,0:T(8,128)} %p_ref.1) | copy-start | bytes 1572868
  21.2 12.0 %copy-start.3 = (s32[2,256]{1,0:T(2,128)S(1)}, s32[2,256]{1,0:T(2,128)}, u32[]{:S(2)}) copy-start(s32[2,256]{1,0:T(2,128)} %pad_add_fusion.refs_6_.info_hbm.refs_1_) | copy-start | bytes 6148
  21.2 12.0 %copy-start.4 = (f32[32,3,4,128]{3,2,1,0:T(4,128)S(1)}, f32[32,3,4,128]{3,2,1,0:T(4,128)}, u32[]{:S(2)}) copy-start(f32[32,3,4,128]{3,2,1,0:T(4,128)} %weights_ref) | copy-start | bytes 589828
  21.2 2.0 %collective-permute-start.2 = (f32[2,16,32,128]{3,2,1,0:T(8,128)S(1)}, f32[2,16,32,128]{3,2,1,0:T(8,128)S(1)}, u32[]{:S(2)}, u32[]{:S(2)}) collective-permute-start(f32[2,16,32,128]{3,2,1,0:T(8,128)S(1)} %collective-permute-done.refs_1_), channel_id=1, source_target_pairs={{0,8},{8,0},{16,24},{24,16},{1,9},{9,1},{17,25},{25,17},{2,10},{10... | collective-permute-start | bytes 1572872 | tf_op jit(solution)/shard_map/ppermute | solution.py:638
  21.3 26.1 %collective-permute-start.3 = (f32[2,16,64,128]{3,2,1,0:T(8,128)}, f32[2,16,64,128]{3,2,1,0:T(8,128)S(1)}, u32[]{:S(2)}, u32[]{:S(2)}) collective-permute-start(f32[2,16,64,128]{3,2,1,0:T(8,128)} %map_rows.1), channel_id=1, source_target_pairs={{0,16},{8,24},{16,0},{24,8},{1,17},{9,25},{17,1},{25,9},{2,18},{10... | collective-permute-start | bytes 3145736 | tf_op jit(solution)/shard_map/ppermute | solution.py:634
  29.8 10.9 %all-to-all-start.1 = ((f32[8,32,128]{2,1,0:T(8,128)}), f32[8,32,128]{2,1,0:T(8,128)S(1)}, u32[]{:S(2)}, u32[]{:S(2)}) async-start(f32[8,32,128]{2,1,0:T(8,128)} %forward.1), calls=%async_computation.1 | async-start | bytes 262144 | tf_op jit(solution)/shard_map/all_to_all | solution.py:668
  41.5 12.7 %all-to-all-start.2 = ((f32[16,32,128]{2,1,0:T(8,128)}), f32[16,32,128]{2,1,0:T(8,128)S(1)}, u32[]{:S(2)}, u32[]{:S(2)}) async-start(f32[16,32,128]{2,1,0:T(8,128)} %regrid.1), calls=%async_computation.2 | async-start | bytes 524288 | tf_op jit(solution)/shard_map/all_to_all | solution.py:674
  45.1 17.9 %copy-start.1 = (f32[2,16,32,128]{3,2,1,0:T(8,128)S(1)}, f32[2,16,32,128]{3,2,1,0:T(8,128)}, u32[]{:S(2)}) copy-start(f32[2,16,32,128]{3,2,1,0:T(8,128)} %r_ref.1) | copy-start | bytes 1572868
  61.0 11.6 %copy-start.2 = (f32[2,16,32,128]{3,2,1,0:T(8,128)S(1)}, f32[2,16,32,128]{3,2,1,0:T(8,128)}, u32[]{:S(2)}) copy-start(f32[2,16,32,128]{3,2,1,0:T(8,128)} %x_ref.1) | copy-start | bytes 1572868
  61.0 2.0 %collective-permute-start.4 = (f32[2,16,32,128]{3,2,1,0:T(8,128)S(1)}, f32[2,16,32,128]{3,2,1,0:T(8,128)S(1)}, u32[]{:S(2)}, u32[]{:S(2)}) collective-permute-start(f32[2,16,32,128]{3,2,1,0:T(8,128)S(1)} %get-tuple-element.24), channel_id=1, source_target_pairs={{0,8},{8,0},{16,24},{24,16},{1,9},{9,1},{17,25},{25,17},{2,10},{10... | collective-permute-start | bytes 1572872 | tf_op jit(solution)/shard_map/ppermute | solution.py:638

commit v4 on v3

--- a/solution.py
+++ b/solution.py
@@ -69,7 +69,7 @@
     return here, past < 4 - chunk
 
 
-def call(kernel, outs, scratch, operands, flops, name, hbm=(), hbm_outs=(), vmem=(), fixed=()):
+def call(kernel, outs, scratch, operands, flops, name, hbm=(), hbm_outs=(), vmem=(), fixed=(), free=(), limit=VMEM):
     operands = list(operands)
     for listed, space in ((fixed, pltpu.HBM), (vmem, pltpu.VMEM)):
         for at in listed:
@@ -81,7 +81,7 @@
         kernel,
         out_shape=[
             pltpu.HBM(shape, jnp.float32)
-            if at in hbm_outs
+            if at in hbm_outs and at not in free
             else jax.ShapeDtypeStruct(shape, jnp.float32)
             for at, shape in enumerate(outs)
         ],
@@ -91,7 +91,7 @@
             pltpu.VMEM(shape, jnp.float32) if isinstance(shape, tuple) else shape
             for shape in scratch
         ],
-        compiler_params=pltpu.CompilerParams(vmem_limit_bytes=VMEM),
+        compiler_params=pltpu.CompilerParams(vmem_limit_bytes=limit),
         cost_estimate=pl.CostEstimate(flops=flops, bytes_accessed=moved, transcendentals=0),
         name=name,
     )(*operands)
@@ -336,12 +336,13 @@
         10**7,
         "regrid",
         hbm_outs=[0],
+        free=[0],
         vmem=[1],
     )[0]
 
 
 def place_boxes(info, chip, u_ref, cos_ref, sin_ref, shift_ref, outs, gbufs, planes, chunk, slots):
-    chips = len(outs)
+    chips = len(gbufs)
     handlers = u_ref.shape[0] // chips
     high, low = halves(shift_ref[...])
     table = jnp.concatenate([high, high, low, jnp.zeros_like(low)], axis=0)
@@ -367,11 +368,12 @@
             first = pl.ds(info[0, block], 4)
             second = pl.ds(info[0, block] + LANES, 4)
             for hop in range(chips):
+                out = outs[hop + slot % 2 * chips]
                 cells = gbufs[hop][pl.ds(base + slot, 4, stride=slots), :]
-                old_first = outs[hop][first, :]
-                old_second = outs[hop][second, :]
-                outs[hop][first, :] = old_first + jnp.where(here, cells, 0.0)
-                outs[hop][second, :] = old_second + jnp.where(after, cells, 0.0)
+                old_first = out[first, :]
+                old_second = out[second, :]
+                out[first, :] = old_first + jnp.where(here, cells, 0.0)
+                out[second, :] = old_second + jnp.where(after, cells, 0.0)
         return carry
 
     lax.fori_loop(0, handlers, put, 0)
@@ -382,7 +384,7 @@
     far_maps = refs[7 : 6 + chips]
     outs = refs[6 + chips : 8 + chips]
     refs = refs[8 + chips :]
-    grids, gbufs, refs = refs[:chips], refs[chips : 2 * chips], refs[2 * chips :]
+    grids, gbufs, refs = refs[: 2 * chips], refs[2 * chips : 3 * chips], refs[3 * chips :]
     info, cos_ref, sin_ref, shift_ref, table_ref, ybuf, images, maps, sems = refs
     planes = s_hbm.shape[1]
     rows = length * planes
@@ -415,7 +417,8 @@
         table.append(jnp.concatenate(bands, axis=0))
     for hop in range(chips):
         for band in range(length // chunk):
-            tile = grids[hop][band * length : (band + 1) * length, :].T
+            at = slice(band * length, (band + 1) * length)
+            tile = (grids[hop][at, :] + grids[hop + chips][at, :]).T
             ybuf[hop, band * 64 : (band + 1) * 64, :] = tile[:64]
             ybuf[hop, rows + band * 64 : rows + (band + 1) * 64, :] = tile[64:]
         for pair in range(planes // 2):
@@ -469,7 +472,7 @@
             inverse_kernel, part=part, length=length, chunk=chunk, slots=slots, chips=chips
         ),
         [(2, planes, part, length)] * 2,
-        [(rows, LANES)] * chips
+        [(rows, LANES)] * (2 * chips)
         + [(blocks * 4, LANES)] * chips
         + [
             pltpu.SMEM(info.shape, info.dtype),
@@ -487,6 +490,7 @@
         "inverse",
         hbm=range(1, len(operands)),
         fixed=range(1, 7),
+        limit=VMEM * max(1, chips // 2),
     )
 
 
@@ -578,7 +582,7 @@
 
     def turn(pair, carry):
         at = pl.ds(pl.multiple_of(pair * LANES, LANES), LANES)
-        rows = held[at, :].T
+        rows = held[at, :64].T
         for group in range(16):
             four = rows[4 * group : 4 * group + 4]
             out_ref[pl.ds(pl.multiple_of(pair * LANES + 8 * group, 8), 8), :] = jnp.concatenate(

time: 74.5 us -> 74.3 us (level)
  no operation moved by 1% of the time
where the time goes in v4:
time: 74.3 us; the launch traced here: 73.7 us
  Pallas kernels  23.6 us (32%)
  waiting for transfers between devices  19.1 us (26%)
  starting transfers between devices  16.6 us (22%)
  blocking collectives  9.28 us (12%)
  other arithmetic  3.73 us (5%)
  between operations  0.87 us (1%)
    pallas_call x7, Pallas kernels, call(): pl.pallas_call(kernel, out_shape=[pltpu.HBM(shape, jnp.float32) if at in...  22.1 us
    all_to_all x1, blocking collectives, shards(): total = lax.all_to_all(found, ('coil', 'tile'), 0, 0, tiled=True)  9.28 us
    all_to_all x1, waiting for transfers between devices, shards(): lax.all_to_all(done, ('coil', 'tile'), 0, 0, axis_index_groups=groups, ti...  6.85 us
    all_to_all x1, starting transfers between devices, shards(): lax.all_to_all(message(block_owner, owner_list), 'tile', 0, 0, tiled=True)  5.83 us
    all_to_all x1, starting transfers between devices, shards(): lax.all_to_all(done, ('coil', 'tile'), 0, 0, axis_index_groups=groups, ti...  3.55 us
    all_to_all x1, waiting for transfers between devices, shards(): lax.all_to_all(message(block_owner, owner_list), 'tile', 0, 0, tiled=True)  3.51 us
    all_to_all x1, starting transfers between devices, shards(): parts = lax.all_to_all(partial, 'tile', 0, 0, tiled=True)  3.38 us
    all_to_all x1, waiting for transfers between devices, shards(): parts = lax.all_to_all(partial, 'tile', 0, 0, tiled=True)  3.23 us
  transfers between devices with their start and end apart: 8, of which 6 were waited for; matrix products, arithmetic and copies ran while one was open for 6% of the time, Pallas kernels for 21%

profile of v4, /device:TPU:0, one launch (start us, length us, event | category | flops | bytes accessed | tf_op | source)
XLA Modules:
  0.0 73.7 jit_solution(8515006752001797834)
XLA Ops:
  0.6 0.5 collective-permute-start.1
  1.1 2.6 %collective-permute-start = (f32[2,16,32,128]{3,2,1,0:T(8,128)}, f32[2,16,32,128]{3,2,1,0:T(8,128)S(1)}, u32[]{:S(2)}, u32[]{:S(2)}) collective-permute-start(f32[2,16,32,128]{3,2,1,0:T(8,128)} %p_ref.1), channel_id=1, source_target_pairs={{0,16},{8,24},{16,0},{24,8},{1,17},{9,25},{17,1},{25,9},{2,18},{10... | collective-permute-start | bytes 1572872 | tf_op jit(solution)/shard_map/ppermute | solution.py:638
  3.7 1.4 %message.1 = s32[8,8,128]{2,1,0:T(8,128)} custom-call(s32[1,32]{1,0:T(1,128)} %bitcast.20, s32[3,1,8,16]{3,2,1,0:T(8,128)} %list_ref.1), custom_call_target="tpu_custom_call" | custom-call | tf_op jit(solution)/shard_map/message/pallas_call | solution.py:163
  5.1 5.8 %all-to-all-start = ((s32[8,8,128]{2,1,0:T(8,128)}), s32[8,8,128]{2,1,0:T(8,128)S(1)}, u32[]{:S(2)}, u32[]{:S(2)}) async-start(s32[8,8,128]{2,1,0:T(8,128)} %message.1), calls=%async_computation | async-start | bytes 65536 | tf_op jit(solution)/shard_map/all_to_all | solution.py:646
  11.0 0.0 copy-start
  11.1 0.1 fusion.7
  11.1 2.3 %map_rows.1 = f32[2,16,64,128]{3,2,1,0:T(8,128)} custom-call(f32[2,16,128,128]{3,2,1,0:T(8,128)} %bitcast.13), custom_call_target="tpu_custom_call" | custom-call | bytes 2097152 | tf_op jit(solution)/shard_map/map_rows/pallas_call | solution.py:80
  13.4 0.8 %multiply_select_fusion.2.refs_9_.refs_4_ = f32[32,128]{1,0:T(8,128)} fusion(f32[32]{0:T(128)S(1)} %compare_select_fusion.9, s32[128]{0:T(128)S(1)} %fusion.8, s32[32]{0:T(128)S(1)} %get-tuple-element.36, s32[128]{0:T(128)S(1)} %get-tuple-element.39, s32[128]{0:T(128)S(1)} %get-tuple-element.38, s32[32]{0:T(128)S(1)} %get-tuple-element.37, ...), kind=kLoop, calls=%fused_computation.21 | loop fusion | flops 81920 | bytes 18432 | tf_op jit(solution)/shard_map/jit(_where)/select_n | solution.py:664
  14.2 3.5 %all-to-all-done = s32[8,8,128]{2,1,0:T(8,128)S(1)} async-done(((s32[8,8,128]{2,1,0:T(8,128)}), s32[8,8,128]{2,1,0:T(8,128)S(1)}, u32[]{:S(2)}, u32[]{:S(2)}) %all-to-all-start) | async-done | bytes 32800 | tf_op jit(solution)/shard_map/all_to_all | solution.py:646
  17.7 0.1 multiply_reduce_fusion
  17.8 0.1 mul.108
  17.8 0.3 select_reduce_fusion.1
  18.1 0.1 iota_compare_fusion
  18.3 0.1 reshape.319
  18.4 0.1 copy.14
  18.4 0.1 broadcast_in_dim.66
  18.5 0.5 select_reduce_fusion
  19.0 0.1 mul.111
  19.1 0.1 squeeze.15
  19.2 0.1 squeeze.14
  19.3 0.6 pad_add_fusion.refs_6_.info_hbm.refs_1_
  19.9 1.3 %sine_multiply_fusion = (f32[256,128]{1,0:T(8,128)}, f32[256,128]{1,0:T(8,128)}) fusion(f32[128]{0:T(128)S(1)} %compare_select_fusion.10, s32[128]{0:T(128)S(1)} %fusion.8, s32[256]{0:T(256)S(1)} %mul.111), kind=kLoop, calls=%fused_computation.9 | loop fusion | flops 491520 | bytes 264192 | tf_op jit(solution)/shard_map/mul | solution.py:658
  21.2 0.0 collective-permute-done.refs_1_
  21.2 0.0 copy-start.3
  21.2 0.0 copy-start.4
  21.2 0.1 collective-permute-start.2
  21.3 0.6 collective-permute-start.3
  21.9 0.0 collective-permute-done.1.refs_2_
  21.9 1.3 %collective-permute-done.2.refs_3_ = f32[2,16,32,128]{3,2,1,0:T(8,128)S(1)} collective-permute-done((f32[2,16,32,128]{3,2,1,0:T(8,128)S(1)}, f32[2,16,32,128]{3,2,1,0:T(8,128)S(1)}, u32[]{:S(2)}, u32[]{:S(2)}) %collective-permute-start.2) | collective-permute-done | bytes 524320 | tf_op jit(solution)/shard_map/ppermute | solution.py:642
  23.2 0.0 copy-done
  23.2 6.6 %forward.1 = f32[8,32,128]{2,1,0:T(8,128)} custom-call(f32[2,16,32,128]{3,2,1,0:T(8,128)S(1)} %copy-done, f32[2,16,32,128]{3,2,1,0:T(8,128)S(1)} %collective-permute-done.refs_1_, f32[2,16,32,128]{3,2,1,0:T(8,128)S(1)} %collective-permute-done.1.refs_2_, f32[2,16,32,128]{3,2,1,0:T(8,128)S(1)} %collective-permute-done.2.refs_3_, ...), custom_call_target="tpu_custom_call" | custom-call | flops 1610612736 | bytes 4999168 | tf_op jit(solution)/shard_map/forward/pallas_call | solution.py:80
  29.8 3.4 %all-to-all-start.1 = ((f32[8,32,128]{2,1,0:T(8,128)}), f32[8,32,128]{2,1,0:T(8,128)S(1)}, u32[]{:S(2)}, u32[]{:S(2)}) async-start(f32[8,32,128]{2,1,0:T(8,128)} %forward.1), calls=%async_computation.1 | async-start | bytes 262144 | tf_op jit(solution)/shard_map/all_to_all | solution.py:672
  33.2 0.0 copy-done.3
  33.2 0.0 copy-done.4
  33.2 4.2 %matrices.1.matrix_ref = f32[2048,128]{1,0:T(8,128)S(1)} custom-call(s32[2,256]{1,0:T(2,128)S(1)} %copy-done.3, f32[32,3,4,128]{3,2,1,0:T(4,128)S(1)} %copy-done.4), custom_call_target="tpu_custom_call" | custom-call | flops 1000000000 | bytes 198656 | tf_op jit(solution)/shard_map/matrices/pallas_call | solution.py:80
  37.4 3.2 %all-to-all-done.1.parts_ref = f32[8,32,128]{2,1,0:T(8,128)S(1)} async-done(((f32[8,32,128]{2,1,0:T(8,128)}), f32[8,32,128]{2,1,0:T(8,128)S(1)}, u32[]{:S(2)}, u32[]{:S(2)}) %all-to-all-start.1) | async-done | bytes 131104 | tf_op jit(solution)/shard_map/all_to_all | solution.py:672
  40.7 0.9 %regrid.1 = f32[16,32,128]{2,1,0:T(8,128)} custom-call(f32[8,32,128]{2,1,0:T(8,128)S(1)} %all-to-all-done.1.parts_ref, f32[2048,128]{1,0:T(8,128)S(1)} %matrices.1.matrix_ref), custom_call_target="tpu_custom_call" | custom-call | flops 10000000 | bytes 1179648 | tf_op jit(solution)/shard_map/regrid/pallas_call | solution.py:80
  41.5 3.5 %all-to-all-start.2 = ((f32[16,32,128]{2,1,0:T(8,128)}), f32[16,32,128]{2,1,0:T(8,128)S(1)}, u32[]{:S(2)}, u32[]{:S(2)}) async-start(f32[16,32,128]{2,1,0:T(8,128)} %regrid.1), calls=%async_computation.2 | async-start | bytes 524288 | tf_op jit(solution)/shard_map/all_to_all | solution.py:678
  45.1 0.0 copy-start.1
  45.1 2.3 %collective-permute-done.3.refs_7_ = f32[2,16,64,128]{3,2,1,0:T(8,128)S(1)} collective-permute-done((f32[2,16,64,128]{3,2,1,0:T(8,128)}, f32[2,16,64,128]{3,2,1,0:T(8,128)S(1)}, u32[]{:S(2)}, u32[]{:S(2)}) %collective-permute-start.3) | collective-permute-done | bytes 1048608 | tf_op jit(solution)/shard_map/ppermute | solution.py:638
  47.4 6.9 %all-to-all-done.2.refs_0_ = f32[16,32,128]{2,1,0:T(8,128)S(1)} async-done(((f32[16,32,128]{2,1,0:T(8,128)}), f32[16,32,128]{2,1,0:T(8,128)S(1)}, u32[]{:S(2)}, u32[]{:S(2)}) %all-to-all-start.2) | async-done | bytes 262176 | tf_op jit(solution)/shard_map/all_to_all | solution.py:678
  54.3 6.6 %inverse.1 = (f32[2,16,32,128]{3,2,1,0:T(8,128)S(1)}, f32[2,16,32,128]{3,2,1,0:T(8,128)S(1)}) custom-call(f32[16,32,128]{2,1,0:T(8,128)S(1)} %all-to-all-done.2.refs_0_, s32[2,256]{1,0:T(2,128)} %pad_add_fusion.refs_6_.info_hbm.refs_1_, f32[256,128]{1,0:T(8,128)} %get-tuple-element.17.refs_7_.refs_2_, f32[256,128]{1,0:T(8,128)} %get-tuple-element.18.refs_8_.refs_3_, ...), custom_call_target="tpu_custom_call" | custom-call | flops 1610612736 | bytes 4212736 | tf_op jit(solution)/shard_map/inverse/pallas_call | solution.py:80
  60.8 0.0 copy-start.2
  60.8 0.1 collective-permute-start.4
  60.9 1.9 %collective-permute-done.4.refs_1_ = f32[2,16,32,128]{3,2,1,0:T(8,128)S(1)} collective-permute-done((f32[2,16,32,128]{3,2,1,0:T(8,128)S(1)}, f32[2,16,32,128]{3,2,1,0:T(8,128)S(1)}, u32[]{:S(2)}, u32[]{:S(2)}) %collective-permute-start.4) | collective-permute-done | bytes 524320 | tf_op jit(solution)/shard_map/ppermute | solution.py:642
  62.8 0.0 copy-done.1
  62.8 0.3 sums.1
  63.1 9.3 %all_to_all.26 = f32[32,1,128]{2,1,0:T(1,128)S(1)} all-to-all(f32[32,1,128]{2,1,0:T(1,128)S(1)} %bitcast.12), channel_id=1, replica_groups=mesh['coil'=4,'tile'=8] {'coil','tile'}, dimensions={0} | all-to-all | bytes 32768 | tf_op jit(solution)/shard_map/all_to_all | solution.py:685
  72.4 0.0 copy-done.2
  72.4 1.3 %finish.1 = (f32[2,16,32,128]{3,2,1,0:T(8,128)}, f32[2,16,32,128]{3,2,1,0:T(8,128)}, f32[2,16,32,128]{3,2,1,0:T(8,128)}) custom-call(f32[32,128]{1,0:T(8,128)S(1)} %bitcast.11, f32[2,16,32,128]{3,2,1,0:T(8,128)S(1)} %copy-done.2, f32[2,16,32,128]{3,2,1,0:T(8,128)S(1)} %copy-done.1, f32[2,16,32,128]{3,2,1,0:T(8,128)S(1)} %copy-done, ...), custom_call_target="tpu_custom_call" | custom-call | flops 10000000 | bytes 2113536 | tf_op jit(solution)/shard_map/finish/pallas_call | solution.py:80
  (11 shorter events, 0.1 us)
Async XLA Ops:
  0.6 21.2 %collective-permute-start.1 = (f32[2,16,32,128]{3,2,1,0:T(8,128)}, f32[2,16,32,128]{3,2,1,0:T(8,128)S(1)}, u32[]{:S(2)}, u32[]{:S(2)}) collective-permute-start(f32[2,16,32,128]{3,2,1,0:T(8,128)} %p_ref.1), channel_id=1, source_target_pairs={{0,8},{8,0},{16,24},{24,16},{1,9},{9,1},{17,25},{25,17},{2,10},{10... | collective-permute-start | bytes 1572872 | tf_op jit(solution)/shard_map/ppermute | solution.py:642
  1.1 20.0 %collective-permute-start = (f32[2,16,32,128]{3,2,1,0:T(8,128)}, f32[2,16,32,128]{3,2,1,0:T(8,128)S(1)}, u32[]{:S(2)}, u32[]{:S(2)}) collective-permute-start(f32[2,16,32,128]{3,2,1,0:T(8,128)} %p_ref.1), channel_id=1, source_target_pairs={{0,16},{8,24},{16,0},{24,8},{1,17},{9,25},{17,1},{25,9},{2,18},{10... | collective-permute-start | bytes 1572872 | tf_op jit(solution)/shard_map/ppermute | solution.py:638
  5.1 12.5 %all-to-all-start = ((s32[8,8,128]{2,1,0:T(8,128)}), s32[8,8,128]{2,1,0:T(8,128)S(1)}, u32[]{:S(2)}, u32[]{:S(2)}) async-start(s32[8,8,128]{2,1,0:T(8,128)} %message.1), calls=%async_computation | async-start | bytes 65536 | tf_op jit(solution)/shard_map/all_to_all | solution.py:646
  11.0 12.1 %copy-start = (f32[2,16,32,128]{3,2,1,0:T(8,128)S(1)}, f32[2,16,32,128]{3,2,1,0:T(8,128)}, u32[]{:S(2)}) copy-start(f32[2,16,32,128]{3,2,1,0:T(8,128)} %p_ref.1) | copy-start | bytes 1572868
  21.2 12.0 %copy-start.3 = (s32[2,256]{1,0:T(2,128)S(1)}, s32[2,256]{1,0:T(2,128)}, u32[]{:S(2)}) copy-start(s32[2,256]{1,0:T(2,128)} %pad_add_fusion.refs_6_.info_hbm.refs_1_) | copy-start | bytes 6148
  21.2 12.0 %copy-start.4 = (f32[32,3,4,128]{3,2,1,0:T(4,128)S(1)}, f32[32,3,4,128]{3,2,1,0:T(4,128)}, u32[]{:S(2)}) copy-start(f32[32,3,4,128]{3,2,1,0:T(4,128)} %weights_ref) | copy-start | bytes 589828
  21.2 2.0 %collective-permute-start.2 = (f32[2,16,32,128]{3,2,1,0:T(8,128)S(1)}, f32[2,16,32,128]{3,2,1,0:T(8,128)S(1)}, u32[]{:S(2)}, u32[]{:S(2)}) collective-permute-start(f32[2,16,32,128]{3,2,1,0:T(8,128)S(1)} %collective-permute-done.refs_1_), channel_id=1, source_target_pairs={{0,8},{8,0},{16,24},{24,16},{1,9},{9,1},{17,25},{25,17},{2,10},{10... | collective-permute-start | bytes 1572872 | tf_op jit(solution)/shard_map/ppermute | solution.py:642
  21.3 26.1 %collective-permute-start.3 = (f32[2,16,64,128]{3,2,1,0:T(8,128)}, f32[2,16,64,128]{3,2,1,0:T(8,128)S(1)}, u32[]{:S(2)}, u32[]{:S(2)}) collective-permute-start(f32[2,16,64,128]{3,2,1,0:T(8,128)} %map_rows.1), channel_id=1, source_target_pairs={{0,16},{8,24},{16,0},{24,8},{1,17},{9,25},{17,1},{25,9},{2,18},{10... | collective-permute-start | bytes 3145736 | tf_op jit(solution)/shard_map/ppermute | solution.py:638
  29.8 10.9 %all-to-all-start.1 = ((f32[8,32,128]{2,1,0:T(8,128)}), f32[8,32,128]{2,1,0:T(8,128)S(1)}, u32[]{:S(2)}, u32[]{:S(2)}) async-start(f32[8,32,128]{2,1,0:T(8,128)} %forward.1), calls=%async_computation.1 | async-start | bytes 262144 | tf_op jit(solution)/shard_map/all_to_all | solution.py:672
  41.5 12.7 %all-to-all-start.2 = ((f32[16,32,128]{2,1,0:T(8,128)}), f32[16,32,128]{2,1,0:T(8,128)S(1)}, u32[]{:S(2)}, u32[]{:S(2)}) async-start(f32[16,32,128]{2,1,0:T(8,128)} %regrid.1), calls=%async_computation.2 | async-start | bytes 524288 | tf_op jit(solution)/shard_map/all_to_all | solution.py:678
  45.1 17.7 %copy-start.1 = (f32[2,16,32,128]{3,2,1,0:T(8,128)S(1)}, f32[2,16,32,128]{3,2,1,0:T(8,128)}, u32[]{:S(2)}) copy-start(f32[2,16,32,128]{3,2,1,0:T(8,128)} %r_ref.1) | copy-start | bytes 1572868
  60.8 11.6 %copy-start.2 = (f32[2,16,32,128]{3,2,1,0:T(8,128)S(1)}, f32[2,16,32,128]{3,2,1,0:T(8,128)}, u32[]{:S(2)}) copy-start(f32[2,16,32,128]{3,2,1,0:T(8,128)} %x_ref.1) | copy-start | bytes 1572868
  60.8 2.0 %collective-permute-start.4 = (f32[2,16,32,128]{3,2,1,0:T(8,128)S(1)}, f32[2,16,32,128]{3,2,1,0:T(8,128)S(1)}, u32[]{:S(2)}, u32[]{:S(2)}) collective-permute-start(f32[2,16,32,128]{3,2,1,0:T(8,128)S(1)} %get-tuple-element.24), channel_id=1, source_target_pairs={{0,8},{8,0},{16,24},{24,16},{1,9},{9,1},{17,25},{25,17},{2,10},{10... | collective-permute-start | bytes 1572872 | tf_op jit(solution)/shard_map/ppermute | solution.py:642

commit v5 on v3

--- a/solution.py
+++ b/solution.py
@@ -26,20 +26,16 @@
 
 def dot_left(table, values, dims=((1,), (0,))):
     high, low = halves(values)
-    return (
-        dot_bf16(table[0], high, dims)
-        + dot_bf16(table[0], low, dims)
-        + dot_bf16(table[1], high, dims)
-    )
+    rows = table.shape[0] // 2
+    both = dot_bf16(table, high, dims)
+    return both[:rows] + both[rows:] + dot_bf16(table[:rows], low, dims)
 
 
 def dot_right(values, table, dims=((1,), (0,))):
     high, low = halves(values)
-    return (
-        dot_bf16(high, table[0], dims)
-        + dot_bf16(low, table[0], dims)
-        + dot_bf16(high, table[1], dims)
-    )
+    rows = values.shape[0]
+    both = dot_bf16(jnp.concatenate([high, low], axis=0), table[0], dims)
+    return both[:rows] + both[rows:] + dot_bf16(high, table[1], dims)
 
 
 def fourier_tables(length):
@@ -205,51 +201,45 @@
 
 
 def forward_kernel(*refs, pieces, chunk, slots):
-    p_hbm = refs[:pieces]
+    p_refs = refs[:pieces]
     s_hbm, table_hbm, info_hbm, cos_hbm, sin_hbm, shift_hbm, out_ref = refs[pieces : pieces + 7]
-    pbuf, sbuf, tables, info, cos_ref, sin_ref, shift_ref = refs[pieces + 7 : pieces + 14]
-    natural, ybuf, grid, gbuf, sems = refs[pieces + 14 :]
-    _, planes, part, length = p_hbm[0].shape
+    sbuf, tables, info, cos_ref, sin_ref, shift_ref = refs[pieces + 7 : pieces + 13]
+    natural, ybuf, grid, gbuf, sems = refs[pieces + 13 :]
+    _, planes, part, length = p_refs[0].shape
     rows = length * planes
     starts = quarters_of(pieces // 2, part)
     order = [0, pieces // 2]
     order += [at for at in range(pieces) if at not in order]
-    first = [(table_hbm.at[0:2], tables.at[0:2])]
-    for at in order:
-        first += [(p_hbm[at], pbuf.at[at]), (s_hbm.at[:, :, pl.ds(starts[at], part), :], sbuf.at[at])]
-    last = [
+    pairs = [(table_hbm.at[0:2], tables.at[0:2])]
+    pairs += [(s_hbm.at[:, :, pl.ds(starts[at], part), :], sbuf.at[at]) for at in order]
+    pairs += [
         (table_hbm.at[2:4], tables.at[2:4]),
         (info_hbm, info),
         (cos_hbm, cos_ref),
         (sin_hbm, sin_ref),
         (shift_hbm, shift_ref),
     ]
-    copies = started(first + last, sems)
+    copies = started(pairs, sems)
     copies[0].wait()
-    batch = min(planes, 256 // part)
     table = (tables[0], tables[1])
     for turn, at in enumerate(order):
-        copies[1 + 2 * turn].wait()
-        copies[2 + 2 * turn].wait()
-        for base in range(0, planes, batch):
-            bands = []
-            for plane in range(base, base + batch):
-                s_re = sbuf[at, 0, plane]
-                s_im = sbuf[at, 1, plane]
-                p_re = pbuf[at, 0, plane]
-                p_im = pbuf[at, 1, plane]
-                bands.append(
-                    jnp.concatenate([s_re * p_re - s_im * p_im, s_re * p_im + s_im * p_re], axis=1)
-                )
-            done = dot_right(jnp.concatenate(bands, axis=0), table)
-            for ri in range(2):
-                half = done[:, ri * length : (ri + 1) * length]
-                natural[ri, base : base + batch, pl.ds(starts[at], part), :] = half.reshape(
-                    batch, part, length
-                )
-    for copy in copies[1 + 2 * pieces :]:
+        copies[1 + turn].wait()
+        bands = []
+        for plane in range(planes):
+            s_re = sbuf[at, 0, plane]
+            s_im = sbuf[at, 1, plane]
+            p_re = p_refs[at][0, plane]
+            p_im = p_refs[at][1, plane]
+            bands.append(
+                jnp.concatenate([s_re * p_re - s_im * p_im, s_re * p_im + s_im * p_re], axis=1)
+            )
+        done = dot_right(jnp.concatenate(bands, axis=0), table)
+        for ri in range(2):
+            half = done[:, ri * length : (ri + 1) * length]
+            natural[ri, :, pl.ds(starts[at], part), :] = half.reshape(planes, part, length)
+    for copy in copies[1 + pieces :]:
         copy.wait()
-    table = (tables[2], tables[3])
+    table = jnp.concatenate([tables[2], tables[3]], axis=0)
     for pair in range(planes // 2):
         columns = [
             jnp.concatenate([natural[0, plane], natural[1, plane]], axis=0)
@@ -278,7 +268,6 @@
         [(blocks // slots, 32, LANES)],
         [
             (count, 2, planes, part, length),
-            (count, 2, planes, part, length),
             pltpu.VMEM(tables.shape, tables.dtype),
             pltpu.SMEM(info.shape, info.dtype),
             (blocks, LANES),
@@ -288,12 +277,12 @@
             (2 * length * planes, length),
             (length * (length // chunk + 1), LANES),
             (blocks * 4, LANES),
-            pltpu.SemaphoreType.DMA((2 * count + 6,)),
+            pltpu.SemaphoreType.DMA((count + 6,)),
         ],
         operands,
         48 * planes * length**3,
         "forward",
-        hbm=range(len(operands)),
+        hbm=range(count, len(operands)),
         fixed=range(count, len(operands)),
     )[0]
 
@@ -345,18 +334,24 @@
     handlers = u_ref.shape[0] // chips
     high, low = halves(shift_ref[...])
     table = jnp.concatenate([high, high, low, jnp.zeros_like(low)], axis=0)
-    for handler in range(handlers):
-        rows = slice(handler * slots, (handler + 1) * slots)
-        cos_b = jnp.concatenate([cos_ref[rows, :]] * 4, axis=0)
-        sin_b = jnp.concatenate([sin_ref[rows, :]] * 4, axis=0)
-        for hop in range(chips):
+    for hop in range(chips):
+        stacks = []
+        for handler in range(handlers):
             u_hi, u_lo = (
-                half.astype(jnp.float32) for half in halves(u_ref[(chip + hop) % chips * handlers + handler])
+                half.astype(jnp.float32)
+                for half in halves(u_ref[(chip + hop) % chips * handlers + handler])
             )
             stack = jnp.concatenate([u_hi, u_lo, u_hi, jnp.zeros_like(u_hi)], axis=0)
-            cells = dot_bf16(stack.T.astype(jnp.bfloat16), table, ((1,), (0,)))
-            turned = cells * cos_b - pltpu.roll(cells, LANES // 2, 1) * sin_b
-            gbufs[hop][handler * LANES : (handler + 1) * LANES, :] = turned
+            stacks.append(stack.T.astype(jnp.bfloat16))
+        cells = dot_bf16(jnp.concatenate(stacks, axis=0), table, ((1,), (0,)))
+        for handler in range(handlers):
+            rows = slice(handler * slots, (handler + 1) * slots)
+            cos_b = jnp.concatenate([cos_ref[rows, :]] * 4, axis=0)
+            sin_b = jnp.concatenate([sin_ref[rows, :]] * 4, axis=0)
+            own = cells[handler * LANES : (handler + 1) * LANES]
+            gbufs[hop][handler * LANES : (handler + 1) * LANES, :] = (
+                own * cos_b - pltpu.roll(own, LANES // 2, 1) * sin_b
+            )
     band = band_of_lane(planes, chunk)
 
     def put(handler, carry):
@@ -406,13 +401,14 @@
     place_boxes(info, chip, u_ref, cos_ref, sin_ref, shift_ref, grids, gbufs, planes, chunk, slots)
     for copy in copies[4:]:
         copy.wait()
-    table = []
-    for half in range(2):
-        bands = [
+    table = jnp.concatenate(
+        [
             table_ref[half, pl.ds(pl.multiple_of(ri * length + own_rows, own), own), :]
+            for half in range(2)
             for ri in range(2)
-        ]
-        table.append(jnp.concatenate(bands, axis=0))
+        ],
+        axis=0,
+    )
     for hop in range(chips):
         for band in range(length // chunk):
             tile = grids[hop][band * length : (band + 1) * length, :].T
@@ -436,25 +432,23 @@
                         ri * own : (ri + 1) * own, inner * LANES : (inner + 1) * LANES
                     ]
     table = (table_ref[2], table_ref[3])
-    batch = min(planes, 256 // part)
     for at, half in enumerate((1 - core, core)):
         local = pl.ds(pl.multiple_of(half * part, part), part)
-        for base in range(0, planes, batch):
-            total_re, total_im = 0.0, 0.0
-            for hop in range(chips):
-                bands = [
-                    jnp.concatenate([images[hop, ri, plane, local, :] for ri in range(2)], axis=1)
-                    for plane in range(base, base + batch)
-                ]
-                done = dot_right(jnp.concatenate(bands, axis=0), table)
-                i_re = done[:, :length].reshape(batch, part, length)
-                i_im = done[:, length:].reshape(batch, part, length)
-                s_re = maps[hop, 0, base : base + batch, local, :]
-                s_im = maps[hop, 1, base : base + batch, local, :]
-                total_re = total_re + (s_re * i_re + s_im * i_im)
-                total_im = total_im + (s_re * i_im - s_im * i_re)
-            outs[at][0, base : base + batch] = total_re
-            outs[at][1, base : base + batch] = total_im
+        total_re, total_im = 0.0, 0.0
+        for hop in range(chips):
+            bands = [
+                jnp.concatenate([images[hop, ri, plane, local, :] for ri in range(2)], axis=1)
+                for plane in range(planes)
+            ]
+            done = dot_right(jnp.concatenate(bands, axis=0), table)
+            i_re = done[:, :length].reshape(planes, part, length)
+            i_im = done[:, length:].reshape(planes, part, length)
+            s_re = maps[hop, 0, :, local, :]
+            s_im = maps[hop, 1, :, local, :]
+            total_re = total_re + (s_re * i_re + s_im * i_im)
+            total_im = total_im + (s_re * i_im - s_im * i_re)
+        outs[at][0] = total_re
+        outs[at][1] = total_im
 
 
 def inverse(spread, info, phases, shift, tables, smap, far_maps, part, chunk, slots):
@@ -578,7 +572,7 @@
 
     def turn(pair, carry):
         at = pl.ds(pl.multiple_of(pair * LANES, LANES), LANES)
-        rows = held[at, :].T
+        rows = held[at, :64].T
         for group in range(16):
             four = rows[4 * group : 4 * group + 4]
             out_ref[pl.ds(pl.multiple_of(pair * LANES + 8 * group, 8), 8), :] = jnp.concatenate(

time: 74.5 us -> 75 us (level)
    ppermute x2, waiting for transfers between devices: 2.3 us -> 1.42 us  [from_chip(): return lax.ppermute(values, 'coil', pairs)]
    all_to_all x1, waiting for transfers between devices: 6.85 us -> 7.73 us  [shards(): lax.all_to_all(done, ('coil', 'tile'), 0, 0, axis_index_groups=groups, ti...]
where the time goes in v5:
time: 75 us; the launch traced here: 74.4 us
  Pallas kernels  24.3 us (32%)
  waiting for transfers between devices  19.1 us (25%)
  starting transfers between devices  16.6 us (22%)
  blocking collectives  9.28 us (12%)
  other arithmetic  3.73 us (5%)
  between operations  0.87 us (1%)
    pallas_call x7, Pallas kernels, call(): pl.pallas_call(kernel, out_shape=[pltpu.HBM(shape, jnp.float32) if at in...  22.8 us
    all_to_all x1, blocking collectives, shards(): total = lax.all_to_all(found, ('coil', 'tile'), 0, 0, tiled=True)  9.28 us
    all_to_all x1, waiting for transfers between devices, shards(): lax.all_to_all(done, ('coil', 'tile'), 0, 0, axis_index_groups=groups, ti...  7.73 us
    all_to_all x1, starting transfers between devices, shards(): lax.all_to_all(message(block_owner, owner_list), 'tile', 0, 0, tiled=True)  5.83 us
    all_to_all x1, starting transfers between devices, shards(): lax.all_to_all(done, ('coil', 'tile'), 0, 0, axis_index_groups=groups, ti...  3.55 us
    all_to_all x1, waiting for transfers between devices, shards(): lax.all_to_all(message(block_owner, owner_list), 'tile', 0, 0, tiled=True)  3.51 us
    all_to_all x1, starting transfers between devices, shards(): parts = lax.all_to_all(partial, 'tile', 0, 0, tiled=True)  3.38 us
    all_to_all x1, waiting for transfers between devices, shards(): parts = lax.all_to_all(partial, 'tile', 0, 0, tiled=True)  3.24 us
  transfers between devices with their start and end apart: 8, of which 6 were waited for; matrix products, arithmetic and copies ran while one was open for 6% of the time, Pallas kernels for 21%

profile of v5, /device:TPU:0, one launch (start us, length us, event | category | flops | bytes accessed | tf_op | source)
XLA Modules:
  0.0 74.4 jit_solution(8894585731877877049)
XLA Ops:
  0.6 0.5 collective-permute-start.1
  1.1 2.6 %collective-permute-start = (f32[2,16,32,128]{3,2,1,0:T(8,128)}, f32[2,16,32,128]{3,2,1,0:T(8,128)S(1)}, u32[]{:S(2)}, u32[]{:S(2)}) collective-permute-start(f32[2,16,32,128]{3,2,1,0:T(8,128)} %p_ref.1), channel_id=1, source_target_pairs={{0,16},{8,24},{16,0},{24,8},{1,17},{9,25},{17,1},{25,9},{2,18},{10... | collective-permute-start | bytes 1572872 | tf_op jit(solution)/shard_map/ppermute | solution.py:628
  3.7 1.4 %message.1 = s32[8,8,128]{2,1,0:T(8,128)} custom-call(s32[1,32]{1,0:T(1,128)} %bitcast.20, s32[3,1,8,16]{3,2,1,0:T(8,128)} %list_ref.1), custom_call_target="tpu_custom_call" | custom-call | tf_op jit(solution)/shard_map/message/pallas_call | solution.py:159
  5.1 5.8 %all-to-all-start = ((s32[8,8,128]{2,1,0:T(8,128)}), s32[8,8,128]{2,1,0:T(8,128)S(1)}, u32[]{:S(2)}, u32[]{:S(2)}) async-start(s32[8,8,128]{2,1,0:T(8,128)} %message.1), calls=%async_computation | async-start | bytes 65536 | tf_op jit(solution)/shard_map/all_to_all | solution.py:636
  11.0 0.0 copy-start
  11.1 0.1 fusion.7
  11.1 2.3 %map_rows.1 = f32[2,16,64,128]{3,2,1,0:T(8,128)} custom-call(f32[2,16,128,128]{3,2,1,0:T(8,128)} %bitcast.13), custom_call_target="tpu_custom_call" | custom-call | bytes 2097152 | tf_op jit(solution)/shard_map/map_rows/pallas_call | solution.py:76
  13.4 0.8 %multiply_select_fusion.2.refs_9_.refs_4_ = f32[32,128]{1,0:T(8,128)} fusion(f32[32]{0:T(128)S(1)} %compare_select_fusion.9, s32[128]{0:T(128)S(1)} %fusion.8, s32[32]{0:T(128)S(1)} %get-tuple-element.36, s32[128]{0:T(128)S(1)} %get-tuple-element.39, s32[128]{0:T(128)S(1)} %get-tuple-element.38, s32[32]{0:T(128)S(1)} %get-tuple-element.37, ...), kind=kLoop, calls=%fused_computation.21 | loop fusion | flops 81920 | bytes 18432 | tf_op jit(solution)/shard_map/jit(_where)/select_n | solution.py:654
  14.2 3.5 %all-to-all-done = s32[8,8,128]{2,1,0:T(8,128)S(1)} async-done(((s32[8,8,128]{2,1,0:T(8,128)}), s32[8,8,128]{2,1,0:T(8,128)S(1)}, u32[]{:S(2)}, u32[]{:S(2)}) %all-to-all-start) | async-done | bytes 32800 | tf_op jit(solution)/shard_map/all_to_all | solution.py:636
  17.7 0.1 multiply_reduce_fusion
  17.8 0.1 mul.108
  17.8 0.3 select_reduce_fusion.1
  18.1 0.1 iota_compare_fusion
  18.3 0.1 reshape.319
  18.4 0.1 copy.14
  18.4 0.1 broadcast_in_dim.66
  18.5 0.5 select_reduce_fusion
  19.0 0.1 mul.111
  19.1 0.1 squeeze.15
  19.2 0.1 squeeze.14
  19.3 0.6 pad_add_fusion.refs_6_.info_hbm.refs_1_
  19.9 1.3 %sine_multiply_fusion = (f32[256,128]{1,0:T(8,128)}, f32[256,128]{1,0:T(8,128)}) fusion(f32[128]{0:T(128)S(1)} %compare_select_fusion.10, s32[128]{0:T(128)S(1)} %fusion.8, s32[256]{0:T(256)S(1)} %mul.111), kind=kLoop, calls=%fused_computation.9 | loop fusion | flops 491520 | bytes 264192 | tf_op jit(solution)/shard_map/mul | solution.py:648
  21.2 0.0 collective-permute-done.refs_1_
  21.2 0.0 copy-start.3
  21.2 0.0 copy-start.4
  21.2 0.1 collective-permute-start.2
  21.3 0.6 collective-permute-start.3
  21.9 0.0 collective-permute-done.1.refs_2_
  21.9 1.3 %collective-permute-done.2.refs_3_ = f32[2,16,32,128]{3,2,1,0:T(8,128)S(1)} collective-permute-done((f32[2,16,32,128]{3,2,1,0:T(8,128)S(1)}, f32[2,16,32,128]{3,2,1,0:T(8,128)S(1)}, u32[]{:S(2)}, u32[]{:S(2)}) %collective-permute-start.2) | collective-permute-done | bytes 524320 | tf_op jit(solution)/shard_map/ppermute | solution.py:632
  23.2 0.0 copy-done
  23.2 7.1 %forward.1 = f32[8,32,128]{2,1,0:T(8,128)} custom-call(f32[2,16,32,128]{3,2,1,0:T(8,128)S(1)} %copy-done, f32[2,16,32,128]{3,2,1,0:T(8,128)S(1)} %collective-permute-done.refs_1_, f32[2,16,32,128]{3,2,1,0:T(8,128)S(1)} %collective-permute-done.1.refs_2_, f32[2,16,32,128]{3,2,1,0:T(8,128)S(1)} %collective-permute-done.2.refs_3_, ...), custom_call_target="tpu_custom_call" | custom-call | flops 1610612736 | bytes 4999168 | tf_op jit(solution)/shard_map/forward/pallas_call | solution.py:76
  30.3 3.4 %all-to-all-start.1 = ((f32[8,32,128]{2,1,0:T(8,128)}), f32[8,32,128]{2,1,0:T(8,128)S(1)}, u32[]{:S(2)}, u32[]{:S(2)}) async-start(f32[8,32,128]{2,1,0:T(8,128)} %forward.1), calls=%async_computation.1 | async-start | bytes 262144 | tf_op jit(solution)/shard_map/all_to_all | solution.py:662
  33.7 0.0 copy-done.3
  33.7 0.0 copy-done.4
  33.7 4.2 %matrices.1.matrix_ref = f32[2048,128]{1,0:T(8,128)S(1)} custom-call(s32[2,256]{1,0:T(2,128)S(1)} %copy-done.3, f32[32,3,4,128]{3,2,1,0:T(4,128)S(1)} %copy-done.4), custom_call_target="tpu_custom_call" | custom-call | flops 1000000000 | bytes 198656 | tf_op jit(solution)/shard_map/matrices/pallas_call | solution.py:76
  37.9 3.2 %all-to-all-done.1.parts_ref = f32[8,32,128]{2,1,0:T(8,128)S(1)} async-done(((f32[8,32,128]{2,1,0:T(8,128)}), f32[8,32,128]{2,1,0:T(8,128)S(1)}, u32[]{:S(2)}, u32[]{:S(2)}) %all-to-all-start.1) | async-done | bytes 131104 | tf_op jit(solution)/shard_map/all_to_all | solution.py:662
  41.2 0.9 %regrid.1 = f32[16,32,128]{2,1,0:T(8,128)} custom-call(f32[8,32,128]{2,1,0:T(8,128)S(1)} %all-to-all-done.1.parts_ref, f32[2048,128]{1,0:T(8,128)S(1)} %matrices.1.matrix_ref), custom_call_target="tpu_custom_call" | custom-call | flops 10000000 | bytes 1179648 | tf_op jit(solution)/shard_map/regrid/pallas_call | solution.py:76
  42.1 3.5 %all-to-all-start.2 = ((f32[16,32,128]{2,1,0:T(8,128)}), f32[16,32,128]{2,1,0:T(8,128)S(1)}, u32[]{:S(2)}, u32[]{:S(2)}) async-start(f32[16,32,128]{2,1,0:T(8,128)} %regrid.1), calls=%async_computation.2 | async-start | bytes 524288 | tf_op jit(solution)/shard_map/all_to_all | solution.py:668
  45.6 0.0 copy-start.1
  45.6 1.4 %collective-permute-done.3.refs_7_ = f32[2,16,64,128]{3,2,1,0:T(8,128)S(1)} collective-permute-done((f32[2,16,64,128]{3,2,1,0:T(8,128)}, f32[2,16,64,128]{3,2,1,0:T(8,128)S(1)}, u32[]{:S(2)}, u32[]{:S(2)}) %collective-permute-start.3) | collective-permute-done | bytes 1048608 | tf_op jit(solution)/shard_map/ppermute | solution.py:628
  47.1 7.7 %all-to-all-done.2.refs_0_ = f32[16,32,128]{2,1,0:T(8,128)S(1)} async-done(((f32[16,32,128]{2,1,0:T(8,128)}), f32[16,32,128]{2,1,0:T(8,128)S(1)}, u32[]{:S(2)}, u32[]{:S(2)}) %all-to-all-start.2) | async-done | bytes 262176 | tf_op jit(solution)/shard_map/all_to_all | solution.py:668
  54.8 6.7 %inverse.1 = (f32[2,16,32,128]{3,2,1,0:T(8,128)S(1)}, f32[2,16,32,128]{3,2,1,0:T(8,128)S(1)}) custom-call(f32[16,32,128]{2,1,0:T(8,128)S(1)} %all-to-all-done.2.refs_0_, s32[2,256]{1,0:T(2,128)} %pad_add_fusion.refs_6_.info_hbm.refs_1_, f32[256,128]{1,0:T(8,128)} %get-tuple-element.17.refs_7_.refs_2_, f32[256,128]{1,0:T(8,128)} %get-tuple-element.18.refs_8_.refs_3_, ...), custom_call_target="tpu_custom_call" | custom-call | flops 1610612736 | bytes 4212736 | tf_op jit(solution)/shard_map/inverse/pallas_call | solution.py:76
  61.5 0.0 copy-start.2
  61.5 0.1 collective-permute-start.4
  61.6 1.9 %collective-permute-done.4.refs_1_ = f32[2,16,32,128]{3,2,1,0:T(8,128)S(1)} collective-permute-done((f32[2,16,32,128]{3,2,1,0:T(8,128)S(1)}, f32[2,16,32,128]{3,2,1,0:T(8,128)S(1)}, u32[]{:S(2)}, u32[]{:S(2)}) %collective-permute-start.4) | collective-permute-done | bytes 524320 | tf_op jit(solution)/shard_map/ppermute | solution.py:632
  63.5 0.0 copy-done.1
  63.5 0.3 sums.1
  63.8 9.3 %all_to_all.26 = f32[32,1,128]{2,1,0:T(1,128)S(1)} all-to-all(f32[32,1,128]{2,1,0:T(1,128)S(1)} %bitcast.12), channel_id=1, replica_groups=mesh['coil'=4,'tile'=8] {'coil','tile'}, dimensions={0} | all-to-all | bytes 32768 | tf_op jit(solution)/shard_map/all_to_all | solution.py:675
  73.1 0.0 copy-done.2
  73.1 1.3 %finish.1 = (f32[2,16,32,128]{3,2,1,0:T(8,128)}, f32[2,16,32,128]{3,2,1,0:T(8,128)}, f32[2,16,32,128]{3,2,1,0:T(8,128)}) custom-call(f32[32,128]{1,0:T(8,128)S(1)} %bitcast.11, f32[2,16,32,128]{3,2,1,0:T(8,128)S(1)} %copy-done.2, f32[2,16,32,128]{3,2,1,0:T(8,128)S(1)} %copy-done.1, f32[2,16,32,128]{3,2,1,0:T(8,128)S(1)} %copy-done, ...), custom_call_target="tpu_custom_call" | custom-call | flops 10000000 | bytes 2113536 | tf_op jit(solution)/shard_map/finish/pallas_call | solution.py:76
  (11 shorter events, 0.1 us)
Async XLA Ops:
  0.6 21.2 %collective-permute-start.1 = (f32[2,16,32,128]{3,2,1,0:T(8,128)}, f32[2,16,32,128]{3,2,1,0:T(8,128)S(1)}, u32[]{:S(2)}, u32[]{:S(2)}) collective-permute-start(f32[2,16,32,128]{3,2,1,0:T(8,128)} %p_ref.1), channel_id=1, source_target_pairs={{0,8},{8,0},{16,24},{24,16},{1,9},{9,1},{17,25},{25,17},{2,10},{10... | collective-permute-start | bytes 1572872 | tf_op jit(solution)/shard_map/ppermute | solution.py:632
  1.1 20.0 %collective-permute-start = (f32[2,16,32,128]{3,2,1,0:T(8,128)}, f32[2,16,32,128]{3,2,1,0:T(8,128)S(1)}, u32[]{:S(2)}, u32[]{:S(2)}) collective-permute-start(f32[2,16,32,128]{3,2,1,0:T(8,128)} %p_ref.1), channel_id=1, source_target_pairs={{0,16},{8,24},{16,0},{24,8},{1,17},{9,25},{17,1},{25,9},{2,18},{10... | collective-permute-start | bytes 1572872 | tf_op jit(solution)/shard_map/ppermute | solution.py:628
  5.1 12.5 %all-to-all-start = ((s32[8,8,128]{2,1,0:T(8,128)}), s32[8,8,128]{2,1,0:T(8,128)S(1)}, u32[]{:S(2)}, u32[]{:S(2)}) async-start(s32[8,8,128]{2,1,0:T(8,128)} %message.1), calls=%async_computation | async-start | bytes 65536 | tf_op jit(solution)/shard_map/all_to_all | solution.py:636
  11.0 12.1 %copy-start = (f32[2,16,32,128]{3,2,1,0:T(8,128)S(1)}, f32[2,16,32,128]{3,2,1,0:T(8,128)}, u32[]{:S(2)}) copy-start(f32[2,16,32,128]{3,2,1,0:T(8,128)} %p_ref.1) | copy-start | bytes 1572868
  21.2 12.5 %copy-start.3 = (s32[2,256]{1,0:T(2,128)S(1)}, s32[2,256]{1,0:T(2,128)}, u32[]{:S(2)}) copy-start(s32[2,256]{1,0:T(2,128)} %pad_add_fusion.refs_6_.info_hbm.refs_1_) | copy-start | bytes 6148
  21.2 12.5 %copy-start.4 = (f32[32,3,4,128]{3,2,1,0:T(4,128)S(1)}, f32[32,3,4,128]{3,2,1,0:T(4,128)}, u32[]{:S(2)}) copy-start(f32[32,3,4,128]{3,2,1,0:T(4,128)} %weights_ref) | copy-start | bytes 589828
  21.2 2.0 %collective-permute-start.2 = (f32[2,16,32,128]{3,2,1,0:T(8,128)S(1)}, f32[2,16,32,128]{3,2,1,0:T(8,128)S(1)}, u32[]{:S(2)}, u32[]{:S(2)}) collective-permute-start(f32[2,16,32,128]{3,2,1,0:T(8,128)S(1)} %collective-permute-done.refs_1_), channel_id=1, source_target_pairs={{0,8},{8,0},{16,24},{24,16},{1,9},{9,1},{17,25},{25,17},{2,10},{10... | collective-permute-start | bytes 1572872 | tf_op jit(solution)/shard_map/ppermute | solution.py:632
  21.3 25.8 %collective-permute-start.3 = (f32[2,16,64,128]{3,2,1,0:T(8,128)}, f32[2,16,64,128]{3,2,1,0:T(8,128)S(1)}, u32[]{:S(2)}, u32[]{:S(2)}) collective-permute-start(f32[2,16,64,128]{3,2,1,0:T(8,128)} %map_rows.1), channel_id=1, source_target_pairs={{0,16},{8,24},{16,0},{24,8},{1,17},{9,25},{17,1},{25,9},{2,18},{10... | collective-permute-start | bytes 3145736 | tf_op jit(solution)/shard_map/ppermute | solution.py:628
  30.3 10.9 %all-to-all-start.1 = ((f32[8,32,128]{2,1,0:T(8,128)}), f32[8,32,128]{2,1,0:T(8,128)S(1)}, u32[]{:S(2)}, u32[]{:S(2)}) async-start(f32[8,32,128]{2,1,0:T(8,128)} %forward.1), calls=%async_computation.1 | async-start | bytes 262144 | tf_op jit(solution)/shard_map/all_to_all | solution.py:662
  42.1 12.7 %all-to-all-start.2 = ((f32[16,32,128]{2,1,0:T(8,128)}), f32[16,32,128]{2,1,0:T(8,128)S(1)}, u32[]{:S(2)}, u32[]{:S(2)}) async-start(f32[16,32,128]{2,1,0:T(8,128)} %regrid.1), calls=%async_computation.2 | async-start | bytes 524288 | tf_op jit(solution)/shard_map/all_to_all | solution.py:668
  45.6 17.9 %copy-start.1 = (f32[2,16,32,128]{3,2,1,0:T(8,128)S(1)}, f32[2,16,32,128]{3,2,1,0:T(8,128)}, u32[]{:S(2)}) copy-start(f32[2,16,32,128]{3,2,1,0:T(8,128)} %r_ref.1) | copy-start | bytes 1572868
  61.5 11.6 %copy-start.2 = (f32[2,16,32,128]{3,2,1,0:T(8,128)S(1)}, f32[2,16,32,128]{3,2,1,0:T(8,128)}, u32[]{:S(2)}) copy-start(f32[2,16,32,128]{3,2,1,0:T(8,128)} %x_ref.1) | copy-start | bytes 1572868
  61.5 2.0 %collective-permute-start.4 = (f32[2,16,32,128]{3,2,1,0:T(8,128)S(1)}, f32[2,16,32,128]{3,2,1,0:T(8,128)S(1)}, u32[]{:S(2)}, u32[]{:S(2)}) collective-permute-start(f32[2,16,32,128]{3,2,1,0:T(8,128)S(1)} %get-tuple-element.24), channel_id=1, source_target_pairs={{0,8},{8,0},{16,24},{24,16},{1,9},{9,1},{17,25},{25,17},{2,10},{10... | collective-permute-start | bytes 1572872 | tf_op jit(solution)/shard_map/ppermute | solution.py:632

commit v6 on v3

--- a/solution.py
+++ b/solution.py
@@ -56,6 +56,20 @@
     return jnp.asarray(np.stack(found))
 
 
+def shift_tables(length, planes, chunk):
+    row = np.arange(32)[:, None]
+    lane = np.arange(LANES)[None, :]
+    row_q, row_ri, row_i = row // 8, row // 4 % 2, row % 4
+    lane_ri, lane_q, lane_x = lane // (LANES // 2), lane // planes % chunk, lane % planes
+    found = []
+    for tile in range(length // planes):
+        angle = 2.0 * math.pi / length * (row_i * (lane_x + tile * planes) % length)
+        sine = np.where(row_ri == 0, 1.0, -1.0) * np.sin(angle)
+        table = np.where(row_ri == lane_ri, np.cos(angle), sine) / math.sqrt(length)
+        found.append(np.where(lane_q % 4 == row_q, table, 0.0))
+    return jnp.asarray(np.stack(found), jnp.float32)
+
+
 def band_of_lane(planes, chunk):
     return lax.broadcasted_iota(jnp.int32, (4, LANES), 1) // planes % chunk
 
@@ -69,7 +83,8 @@
     return here, past < 4 - chunk
 
 
-def call(kernel, outs, scratch, operands, flops, name, hbm=(), hbm_outs=(), vmem=(), fixed=()):
+def call(kernel, outs, scratch, operands, flops, name, hbm=(), hbm_outs=(), vmem=(), fixed=(), spaces=()):
+    spaces = dict(spaces)
     operands = list(operands)
     for listed, space in ((fixed, pltpu.HBM), (vmem, pltpu.VMEM)):
         for at in listed:
@@ -80,8 +95,8 @@
     return pl.pallas_call(
         kernel,
         out_shape=[
-            pltpu.HBM(shape, jnp.float32)
-            if at in hbm_outs
+            spaces[at](shape, jnp.float32)
+            if at in spaces
             else jax.ShapeDtypeStruct(shape, jnp.float32)
             for at, shape in enumerate(outs)
         ],
@@ -222,7 +237,7 @@
         (info_hbm, info),
         (cos_hbm, cos_ref),
         (sin_hbm, sin_ref),
-        (shift_hbm, shift_ref),
+        (shift_hbm.at[lax.axis_index("tile")], shift_ref),
     ]
     copies = started(first + last, sems)
     copies[0].wait()
@@ -283,7 +298,7 @@
             pltpu.SMEM(info.shape, info.dtype),
             (blocks, LANES),
             (blocks, LANES),
-            shift.shape,
+            shift.shape[1:],
             (2, planes, length, length),
             (2 * length * planes, length),
             (length * (length // chunk + 1), LANES),
@@ -298,7 +313,7 @@
     )[0]
 
 
-def regrid_kernel(parts_ref, matrix_ref, out_ref, held, done_sem):
+def regrid_kernel(parts_ref, matrix_ref, out_ref):
     total = parts_ref[0]
     for at in range(1, parts_ref.shape[0]):
         total = total + parts_ref[at]
@@ -319,24 +334,20 @@
                     at = 8 * (((e * 4 + source) * 4 + d_z) * 4 + d_x)
                     sums[e] = sums[e] + matrix_ref[at : at + 8] * moved
     done = jnp.concatenate(sums, axis=0)
-    for at in range(held.shape[0]):
-        held[at] = done
-    copy = pltpu.make_async_copy(held, out_ref, done_sem)
-    copy.start()
-    copy.wait()
+    for at in range(out_ref.shape[0]):
+        out_ref[at] = done
 
 
 def regrid(parts, matrix, copies):
-    shape = (copies,) + parts.shape[1:]
     return call(
         regrid_kernel,
-        [shape],
-        [shape, pltpu.SemaphoreType.DMA],
+        [(copies,) + parts.shape[1:]],
+        [],
         [parts, matrix],
         10**7,
         "regrid",
-        hbm_outs=[0],
         vmem=[1],
+        spaces={0: pltpu.VMEM},
     )[0]
 
 
@@ -393,7 +404,7 @@
         (info_hbm, info),
         (cos_hbm, cos_ref),
         (sin_hbm, sin_ref),
-        (shift_hbm, shift_ref),
+        (shift_hbm.at[lax.axis_index("tile")], shift_ref),
         (table_hbm, table_ref),
         (s_hbm.at[:, :, pl.ds(own_rows, own), :], maps.at[0]),
     ]
@@ -475,7 +486,7 @@
             pltpu.SMEM(info.shape, info.dtype),
             (blocks, LANES),
             (blocks, LANES),
-            shift.shape,
+            shift.shape[1:],
             pltpu.VMEM(tables.shape, tables.dtype),
             (chips, 2 * length * planes, length),
             own,
@@ -578,7 +589,7 @@
 
     def turn(pair, carry):
         at = pl.ds(pl.multiple_of(pair * LANES, LANES), LANES)
-        rows = held[at, :].T
+        rows = held[at, :64].T
         for group in range(16):
             four = rows[4 * group : 4 * group + 4]
             out_ref[pl.ds(pl.multiple_of(pair * LANES + 8 * group, 8), 8), :] = jnp.concatenate(
@@ -647,19 +658,13 @@
     )
     lane = jnp.arange(LANES, dtype=jnp.int32)
     lane_ri = lane // (LANES // 2)
-    lane_q = lane // planes % chunk
     lane_x = lane % planes + tile * planes
     unit = 2.0 * math.pi / length
     angle = unit * (off_x.reshape(-1, 1) * lane_x[None] % length).astype(jnp.float32)
     phases = (jnp.cos(angle), jnp.sin(angle) * jnp.where(lane_ri == 0, 1.0, -1.0)[None])
-    row = jnp.arange(32, dtype=jnp.int32)[:, None]
-    row_q, row_ri, row_i = row // 8, row // 4 % 2, row % 4
-    angle = unit * (row_i * lane_x[None] % length).astype(jnp.float32)
-    sine = jnp.where(row_ri == 0, 1.0, -1.0) * jnp.sin(angle)
-    shift = jnp.where(row_ri == lane_ri[None], jnp.cos(angle), sine)
-    shift = jnp.where(lane_q[None] % 4 == row_q, shift / math.sqrt(length), 0.0)
-    p_far, far_rows, info, phases, shift = lax.optimization_barrier(
-        (p_same[1:], far_rows, info, phases, shift)
+    shift = shift_tables(length, planes, chunk)
+    p_far, far_rows, info, phases = lax.optimization_barrier(
+        (p_same[1:], far_rows, info, phases)
     )
     p_other += [other_core(piece) for piece in p_far]
     far_maps = [from_chip(rows, by) for by, rows in enumerate(far_rows, 1)]

time: 74.5 us -> 74.4 us (level)
  waiting for transfers between devices: 19.1 us -> 20.8 us
  Pallas kernels: 23.7 us -> 22.8 us
  other arithmetic: 3.73 us -> 2.97 us
    all_to_all x1, waiting for transfers between devices: 3.51 us -> 5.2 us  [shards(): lax.all_to_all(message(block_owner, owner_list), 'tile', 0, 0, tiled=True)]
    pallas_call x7, Pallas kernels: 22.3 us -> 21.4 us  [call(): pl.pallas_call(kernel, out_shape=[spaces[at](shape, jnp.float32) if at in...]
    select_n x5 -> x0, other arithmetic: 0.78 us -> none  [the longest x2 0.76 us: shards(): shift = jnp.where(lane_q[None] % 4 == row_q, shift / math.sqrt(length), 0.0)]
  transfers between devices with their start and end apart: 8 -> 8, of which waited for: 6 -> 6; matrix products, arithmetic and copies ran while one was open for 6% -> 5% of each run, Pallas kernels for 21% -> 20%
where the time goes in v6:
time: 74.4 us; the launch traced here: 73.9 us
  Pallas kernels  22.8 us (31%)
  waiting for transfers between devices  20.8 us (28%)
  starting transfers between devices  16.6 us (22%)
  blocking collectives  9.29 us (12%)
  other arithmetic  2.97 us (4%)
  between operations  0.85 us (1%)
    pallas_call x7, Pallas kernels, call(): pl.pallas_call(kernel, out_shape=[spaces[at](shape, jnp.float32) if at in...  21.4 us
    all_to_all x1, blocking collectives, shards(): total = lax.all_to_all(found, ('coil', 'tile'), 0, 0, tiled=True)  9.29 us
    all_to_all x1, waiting for transfers between devices, shards(): lax.all_to_all(done, ('coil', 'tile'), 0, 0, axis_index_groups=groups, ti...  7.12 us
    all_to_all x1, starting transfers between devices, shards(): lax.all_to_all(message(block_owner, owner_list), 'tile', 0, 0, tiled=True)  5.83 us
    all_to_all x1, waiting for transfers between devices, shards(): lax.all_to_all(message(block_owner, owner_list), 'tile', 0, 0, tiled=True)  5.2 us
    all_to_all x1, starting transfers between devices, shards(): lax.all_to_all(done, ('coil', 'tile'), 0, 0, axis_index_groups=groups, ti...  3.53 us
    all_to_all x1, starting transfers between devices, shards(): parts = lax.all_to_all(partial, 'tile', 0, 0, tiled=True)  3.38 us
    all_to_all x1, waiting for transfers between devices, shards(): parts = lax.all_to_all(partial, 'tile', 0, 0, tiled=True)  3.24 us
  transfers between devices with their start and end apart: 8, of which 6 were waited for; matrix products, arithmetic and copies ran while one was open for 5% of the time, Pallas kernels for 20%

profile of v6, /device:TPU:0, one launch (start us, length us, event | category | flops | bytes accessed | tf_op | source)
XLA Modules:
  0.0 73.9 jit_solution(13659002691620676191)
XLA Ops:
  0.6 0.5 collective-permute-start.1
  1.1 2.6 %collective-permute-start = (f32[2,16,32,128]{3,2,1,0:T(8,128)}, f32[2,16,32,128]{3,2,1,0:T(8,128)S(1)}, u32[]{:S(2)}, u32[]{:S(2)}) collective-permute-start(f32[2,16,32,128]{3,2,1,0:T(8,128)} %p_ref.1), channel_id=1, source_target_pairs={{0,16},{8,24},{16,0},{24,8},{1,17},{9,25},{17,1},{25,9},{2,18},{10... | collective-permute-start | bytes 1572872 | tf_op jit(solution)/shard_map/ppermute | solution.py:645
  3.7 1.4 %message.1 = s32[8,8,128]{2,1,0:T(8,128)} custom-call(s32[1,32]{1,0:T(1,128)} %bitcast.20, s32[3,1,8,16]{3,2,1,0:T(8,128)} %list_ref.1), custom_call_target="tpu_custom_call" | custom-call | tf_op jit(solution)/shard_map/message/pallas_call | solution.py:178
  5.1 5.8 %all-to-all-start = ((s32[8,8,128]{2,1,0:T(8,128)}), s32[8,8,128]{2,1,0:T(8,128)S(1)}, u32[]{:S(2)}, u32[]{:S(2)}) async-start(s32[8,8,128]{2,1,0:T(8,128)} %message.1), calls=%async_computation | async-start | bytes 65536 | tf_op jit(solution)/shard_map/all_to_all | solution.py:653
  11.0 0.0 copy-start
  11.0 0.1 fusion.4
  11.1 1.4 %map_rows.1 = f32[2,16,64,128]{3,2,1,0:T(8,128)S(1)} custom-call(f32[2,16,128,128]{3,2,1,0:T(8,128)} %bitcast.13), custom_call_target="tpu_custom_call" | custom-call | bytes 2097152 | tf_op jit(solution)/shard_map/map_rows/pallas_call | solution.py:95
  12.5 5.2 %all-to-all-done = s32[8,8,128]{2,1,0:T(8,128)S(1)} async-done(((s32[8,8,128]{2,1,0:T(8,128)}), s32[8,8,128]{2,1,0:T(8,128)S(1)}, u32[]{:S(2)}, u32[]{:S(2)}) %all-to-all-start) | async-done | bytes 32800 | tf_op jit(solution)/shard_map/all_to_all | solution.py:653
  17.7 0.1 multiply_reduce_fusion
  17.8 0.1 mul.81
  17.8 0.3 select_reduce_fusion.1
  18.1 0.1 iota_compare_fusion
  18.3 0.1 reshape.172
  18.4 0.1 copy.15
  18.4 0.1 broadcast_in_dim.50
  18.5 0.5 select_reduce_fusion
  19.0 0.1 mul.84
  19.1 0.1 squeeze.15
  19.2 0.1 squeeze.14
  19.3 0.6 pad_add_fusion.refs_6_.info_hbm.refs_1_
  19.9 1.3 %sine_multiply_fusion = (f32[256,128]{1,0:T(8,128)}, f32[256,128]{1,0:T(8,128)}) fusion(f32[128]{0:T(128)S(1)} %compare_select_fusion.3, s32[128]{0:T(128)S(1)} %fusion.5, s32[256]{0:T(256)S(1)} %mul.84), kind=kLoop, calls=%fused_computation.9 | loop fusion | flops 491520 | bytes 264192 | tf_op jit(solution)/shard_map/mul | solution.py:664
  21.2 0.0 collective-permute-done.refs_1_
  21.2 0.0 copy-start.3
  21.2 0.0 copy-start.4
  21.2 0.1 collective-permute-start.2
  21.3 0.6 collective-permute-start.3
  21.9 0.0 collective-permute-done.1.refs_2_
  21.9 1.3 %collective-permute-done.2.refs_3_ = f32[2,16,32,128]{3,2,1,0:T(8,128)S(1)} collective-permute-done((f32[2,16,32,128]{3,2,1,0:T(8,128)S(1)}, f32[2,16,32,128]{3,2,1,0:T(8,128)S(1)}, u32[]{:S(2)}, u32[]{:S(2)}) %collective-permute-start.2) | collective-permute-done | bytes 524320 | tf_op jit(solution)/shard_map/ppermute | solution.py:649
  23.2 0.0 copy-done
  23.2 6.6 %forward.1 = f32[8,32,128]{2,1,0:T(8,128)} custom-call(f32[2,16,32,128]{3,2,1,0:T(8,128)S(1)} %copy-done, f32[2,16,32,128]{3,2,1,0:T(8,128)S(1)} %collective-permute-done.refs_1_, f32[2,16,32,128]{3,2,1,0:T(8,128)S(1)} %collective-permute-done.1.refs_2_, f32[2,16,32,128]{3,2,1,0:T(8,128)S(1)} %collective-permute-done.2.refs_3_, ...), custom_call_target="tpu_custom_call" | custom-call | flops 1610612736 | bytes 5113856 | tf_op jit(solution)/shard_map/forward/pallas_call | solution.py:95
  29.8 3.4 %all-to-all-start.1 = ((f32[8,32,128]{2,1,0:T(8,128)}), f32[8,32,128]{2,1,0:T(8,128)S(1)}, u32[]{:S(2)}, u32[]{:S(2)}) async-start(f32[8,32,128]{2,1,0:T(8,128)} %forward.1), calls=%async_computation.1 | async-start | bytes 262144 | tf_op jit(solution)/shard_map/all_to_all | solution.py:673
  33.2 0.0 copy-done.3
  33.2 0.0 copy-done.4
  33.2 4.2 %matrices.1.matrix_ref = f32[2048,128]{1,0:T(8,128)S(1)} custom-call(s32[2,256]{1,0:T(2,128)S(1)} %copy-done.3, f32[32,3,4,128]{3,2,1,0:T(4,128)S(1)} %copy-done.4), custom_call_target="tpu_custom_call" | custom-call | flops 1000000000 | bytes 198656 | tf_op jit(solution)/shard_map/matrices/pallas_call | solution.py:95
  37.4 3.2 %all-to-all-done.1.parts_ref = f32[8,32,128]{2,1,0:T(8,128)S(1)} async-done(((f32[8,32,128]{2,1,0:T(8,128)}), f32[8,32,128]{2,1,0:T(8,128)S(1)}, u32[]{:S(2)}, u32[]{:S(2)}) %all-to-all-start.1) | async-done | bytes 131104 | tf_op jit(solution)/shard_map/all_to_all | solution.py:673
  40.7 0.9 %regrid.1 = f32[16,32,128]{2,1,0:T(8,128)} custom-call(f32[8,32,128]{2,1,0:T(8,128)S(1)} %all-to-all-done.1.parts_ref, f32[2048,128]{1,0:T(8,128)S(1)} %matrices.1.matrix_ref), custom_call_target="tpu_custom_call" | custom-call | flops 10000000 | bytes 1179648 | tf_op jit(solution)/shard_map/regrid/pallas_call | solution.py:95
  41.5 3.5 %all-to-all-start.2 = ((f32[16,32,128]{2,1,0:T(8,128)}), f32[16,32,128]{2,1,0:T(8,128)S(1)}, u32[]{:S(2)}, u32[]{:S(2)}) async-start(f32[16,32,128]{2,1,0:T(8,128)} %regrid.1), calls=%async_computation.2 | async-start | bytes 524288 | tf_op jit(solution)/shard_map/all_to_all | solution.py:679
  45.1 0.0 copy-start.1
  45.1 2.0 %collective-permute-done.3.refs_7_ = f32[2,16,64,128]{3,2,1,0:T(8,128)} collective-permute-done((f32[2,16,64,128]{3,2,1,0:T(8,128)S(1)}, f32[2,16,64,128]{3,2,1,0:T(8,128)}, u32[]{:S(2)}, u32[]{:S(2)}) %collective-permute-start.3) | collective-permute-done | bytes 1048608 | tf_op jit(solution)/shard_map/ppermute | solution.py:645
  47.1 7.1 %all-to-all-done.2.refs_0_ = f32[16,32,128]{2,1,0:T(8,128)S(1)} async-done(((f32[16,32,128]{2,1,0:T(8,128)}), f32[16,32,128]{2,1,0:T(8,128)S(1)}, u32[]{:S(2)}, u32[]{:S(2)}) %all-to-all-start.2) | async-done | bytes 262176 | tf_op jit(solution)/shard_map/all_to_all | solution.py:679
  54.2 6.7 %inverse.1 = (f32[2,16,32,128]{3,2,1,0:T(8,128)S(1)}, f32[2,16,32,128]{3,2,1,0:T(8,128)S(1)}) custom-call(f32[16,32,128]{2,1,0:T(8,128)S(1)} %all-to-all-done.2.refs_0_, s32[2,256]{1,0:T(2,128)} %pad_add_fusion.refs_6_.info_hbm.refs_1_, f32[256,128]{1,0:T(8,128)} %get-tuple-element.16.refs_7_.refs_2_, f32[256,128]{1,0:T(8,128)} %get-tuple-element.17.refs_8_.refs_3_, ...), custom_call_target="tpu_custom_call" | custom-call | flops 1610612736 | bytes 4327424 | tf_op jit(solution)/shard_map/inverse/pallas_call | solution.py:95
  61.0 0.0 copy-start.2
  61.0 0.1 collective-permute-start.4
  61.1 1.9 %collective-permute-done.4.refs_1_ = f32[2,16,32,128]{3,2,1,0:T(8,128)S(1)} collective-permute-done((f32[2,16,32,128]{3,2,1,0:T(8,128)S(1)}, f32[2,16,32,128]{3,2,1,0:T(8,128)S(1)}, u32[]{:S(2)}, u32[]{:S(2)}) %collective-permute-start.4) | collective-permute-done | bytes 524320 | tf_op jit(solution)/shard_map/ppermute | solution.py:649
  63.0 0.0 copy-done.1
  63.0 0.3 sums.1
  63.3 9.3 %all_to_all.26 = f32[32,1,128]{2,1,0:T(1,128)S(1)} all-to-all(f32[32,1,128]{2,1,0:T(1,128)S(1)} %bitcast.12), channel_id=1, replica_groups=mesh['coil'=4,'tile'=8] {'coil','tile'}, dimensions={0} | all-to-all | bytes 32768 | tf_op jit(solution)/shard_map/all_to_all | solution.py:686
  72.6 0.0 copy-done.2
  72.6 1.3 %finish.1 = (f32[2,16,32,128]{3,2,1,0:T(8,128)}, f32[2,16,32,128]{3,2,1,0:T(8,128)}, f32[2,16,32,128]{3,2,1,0:T(8,128)}) custom-call(f32[32,128]{1,0:T(8,128)S(1)} %bitcast.11, f32[2,16,32,128]{3,2,1,0:T(8,128)S(1)} %copy-done.2, f32[2,16,32,128]{3,2,1,0:T(8,128)S(1)} %copy-done.1, f32[2,16,32,128]{3,2,1,0:T(8,128)S(1)} %copy-done, ...), custom_call_target="tpu_custom_call" | custom-call | flops 10000000 | bytes 2113536 | tf_op jit(solution)/shard_map/finish/pallas_call | solution.py:95
  (7 shorter events, 0.0 us)
Async XLA Ops:
  0.6 21.3 %collective-permute-start.1 = (f32[2,16,32,128]{3,2,1,0:T(8,128)}, f32[2,16,32,128]{3,2,1,0:T(8,128)S(1)}, u32[]{:S(2)}, u32[]{:S(2)}) collective-permute-start(f32[2,16,32,128]{3,2,1,0:T(8,128)} %p_ref.1), channel_id=1, source_target_pairs={{0,8},{8,0},{16,24},{24,16},{1,9},{9,1},{17,25},{25,17},{2,10},{10... | collective-permute-start | bytes 1572872 | tf_op jit(solution)/shard_map/ppermute | solution.py:649
  1.1 20.0 %collective-permute-start = (f32[2,16,32,128]{3,2,1,0:T(8,128)}, f32[2,16,32,128]{3,2,1,0:T(8,128)S(1)}, u32[]{:S(2)}, u32[]{:S(2)}) collective-permute-start(f32[2,16,32,128]{3,2,1,0:T(8,128)} %p_ref.1), channel_id=1, source_target_pairs={{0,16},{8,24},{16,0},{24,8},{1,17},{9,25},{17,1},{25,9},{2,18},{10... | collective-permute-start | bytes 1572872 | tf_op jit(solution)/shard_map/ppermute | solution.py:645
  5.1 12.5 %all-to-all-start = ((s32[8,8,128]{2,1,0:T(8,128)}), s32[8,8,128]{2,1,0:T(8,128)S(1)}, u32[]{:S(2)}, u32[]{:S(2)}) async-start(s32[8,8,128]{2,1,0:T(8,128)} %message.1), calls=%async_computation | async-start | bytes 65536 | tf_op jit(solution)/shard_map/all_to_all | solution.py:653
  11.0 12.2 %copy-start = (f32[2,16,32,128]{3,2,1,0:T(8,128)S(1)}, f32[2,16,32,128]{3,2,1,0:T(8,128)}, u32[]{:S(2)}) copy-start(f32[2,16,32,128]{3,2,1,0:T(8,128)} %p_ref.1) | copy-start | bytes 1572868
  21.2 12.0 %copy-start.3 = (s32[2,256]{1,0:T(2,128)S(1)}, s32[2,256]{1,0:T(2,128)}, u32[]{:S(2)}) copy-start(s32[2,256]{1,0:T(2,128)} %pad_add_fusion.refs_6_.info_hbm.refs_1_) | copy-start | bytes 6148
  21.2 12.0 %copy-start.4 = (f32[32,3,4,128]{3,2,1,0:T(4,128)S(1)}, f32[32,3,4,128]{3,2,1,0:T(4,128)}, u32[]{:S(2)}) copy-start(f32[32,3,4,128]{3,2,1,0:T(4,128)} %weights_ref) | copy-start | bytes 589828
  21.2 2.0 %collective-permute-start.2 = (f32[2,16,32,128]{3,2,1,0:T(8,128)S(1)}, f32[2,16,32,128]{3,2,1,0:T(8,128)S(1)}, u32[]{:S(2)}, u32[]{:S(2)}) collective-permute-start(f32[2,16,32,128]{3,2,1,0:T(8,128)S(1)} %collective-permute-done.refs_1_), channel_id=1, source_target_pairs={{0,8},{8,0},{16,24},{24,16},{1,9},{9,1},{17,25},{25,17},{2,10},{10... | collective-permute-start | bytes 1572872 | tf_op jit(solution)/shard_map/ppermute | solution.py:649
  21.3 25.8 %collective-permute-start.3 = (f32[2,16,64,128]{3,2,1,0:T(8,128)S(1)}, f32[2,16,64,128]{3,2,1,0:T(8,128)}, u32[]{:S(2)}, u32[]{:S(2)}) collective-permute-start(f32[2,16,64,128]{3,2,1,0:T(8,128)S(1)} %map_rows.1), channel_id=1, source_target_pairs={{0,16},{8,24},{16,0},{24,8},{1,17},{9,25},{17,1},{25,9},{2,18},{10... | collective-permute-start | bytes 3145736 | tf_op jit(solution)/shard_map/ppermute | solution.py:645
  29.8 10.9 %all-to-all-start.1 = ((f32[8,32,128]{2,1,0:T(8,128)}), f32[8,32,128]{2,1,0:T(8,128)S(1)}, u32[]{:S(2)}, u32[]{:S(2)}) async-start(f32[8,32,128]{2,1,0:T(8,128)} %forward.1), calls=%async_computation.1 | async-start | bytes 262144 | tf_op jit(solution)/shard_map/all_to_all | solution.py:673
  41.5 12.7 %all-to-all-start.2 = ((f32[16,32,128]{2,1,0:T(8,128)}), f32[16,32,128]{2,1,0:T(8,128)S(1)}, u32[]{:S(2)}, u32[]{:S(2)}) async-start(f32[16,32,128]{2,1,0:T(8,128)} %regrid.1), calls=%async_computation.2 | async-start | bytes 524288 | tf_op jit(solution)/shard_map/all_to_all | solution.py:679
  45.1 17.9 %copy-start.1 = (f32[2,16,32,128]{3,2,1,0:T(8,128)S(1)}, f32[2,16,32,128]{3,2,1,0:T(8,128)}, u32[]{:S(2)}) copy-start(f32[2,16,32,128]{3,2,1,0:T(8,128)} %r_ref.1) | copy-start | bytes 1572868
  61.0 11.6 %copy-start.2 = (f32[2,16,32,128]{3,2,1,0:T(8,128)S(1)}, f32[2,16,32,128]{3,2,1,0:T(8,128)}, u32[]{:S(2)}) copy-start(f32[2,16,32,128]{3,2,1,0:T(8,128)} %x_ref.1) | copy-start | bytes 1572868
  61.0 2.0 %collective-permute-start.4 = (f32[2,16,32,128]{3,2,1,0:T(8,128)S(1)}, f32[2,16,32,128]{3,2,1,0:T(8,128)S(1)}, u32[]{:S(2)}, u32[]{:S(2)}) collective-permute-start(f32[2,16,32,128]{3,2,1,0:T(8,128)S(1)} %get-tuple-element.22), channel_id=1, source_target_pairs={{0,8},{8,0},{16,24},{24,16},{1,9},{9,1},{17,25},{25,17},{2,10},{10... | collective-permute-start | bytes 1572872 | tf_op jit(solution)/shard_map/ppermute | solution.py:649

commit v7 on v6

--- a/solution.py
+++ b/solution.py
@@ -220,18 +220,19 @@
 
 
 def forward_kernel(*refs, pieces, chunk, slots):
-    p_hbm = refs[:pieces]
-    s_hbm, table_hbm, info_hbm, cos_hbm, sin_hbm, shift_hbm, out_ref = refs[pieces : pieces + 7]
-    pbuf, sbuf, tables, info, cos_ref, sin_ref, shift_ref = refs[pieces + 7 : pieces + 14]
-    natural, ybuf, grid, gbuf, sems = refs[pieces + 14 :]
-    _, planes, part, length = p_hbm[0].shape
+    p_refs = refs[:pieces]
+    s_hbm, table_hbm, info_hbm, cos_hbm, sin_hbm, shift_hbm, weights_ref = refs[pieces : pieces + 7]
+    out_ref, turned_ref = refs[pieces + 7 : pieces + 9]
+    sbuf, tables, info, cos_ref, sin_ref, shift_ref = refs[pieces + 9 : pieces + 15]
+    natural, ybuf, grid, gbuf, sems = refs[pieces + 15 :]
+    _, planes, part, length = p_refs[0].shape
     rows = length * planes
     starts = quarters_of(pieces // 2, part)
     order = [0, pieces // 2]
     order += [at for at in range(pieces) if at not in order]
     first = [(table_hbm.at[0:2], tables.at[0:2])]
     for at in order:
-        first += [(p_hbm[at], pbuf.at[at]), (s_hbm.at[:, :, pl.ds(starts[at], part), :], sbuf.at[at])]
+        first.append((s_hbm.at[:, :, pl.ds(starts[at], part), :], sbuf.at[at]))
     last = [
         (table_hbm.at[2:4], tables.at[2:4]),
         (info_hbm, info),
@@ -244,15 +245,14 @@
     batch = min(planes, 256 // part)
     table = (tables[0], tables[1])
     for turn, at in enumerate(order):
-        copies[1 + 2 * turn].wait()
-        copies[2 + 2 * turn].wait()
+        copies[1 + turn].wait()
         for base in range(0, planes, batch):
             bands = []
             for plane in range(base, base + batch):
                 s_re = sbuf[at, 0, plane]
                 s_im = sbuf[at, 1, plane]
-                p_re = pbuf[at, 0, plane]
-                p_im = pbuf[at, 1, plane]
+                p_re = p_refs[at][0, plane]
+                p_im = p_refs[at][1, plane]
                 bands.append(
                     jnp.concatenate([s_re * p_re - s_im * p_im, s_re * p_im + s_im * p_re], axis=1)
                 )
@@ -262,8 +262,14 @@
                 natural[ri, base : base + batch, pl.ds(starts[at], part), :] = half.reshape(
                     batch, part, length
                 )
-    for copy in copies[1 + 2 * pieces :]:
+    for copy in copies[1 + pieces :]:
         copy.wait()
+    own = lax.axis_index("tile") * slots
+    for block in range(slots):
+        w_y = weights_ref[block, 1]
+        turned_ref[block] = pltpu.roll(
+            jnp.concatenate([w_y, w_y], axis=0), info[1, own + block] % 4, 0
+        )
     table = (tables[2], tables[3])
     for pair in range(planes // 2):
         columns = [
@@ -283,16 +289,15 @@
     cut_boxes(info, grid, cos_ref, sin_ref, shift_ref, out_ref, gbuf, planes, chunk, slots)
 
 
-def forward(pieces, smap, tables, info, phases, shift, chunk, slots):
+def forward(pieces, smap, tables, info, phases, shift, weights, chunk, slots):
     _, planes, part, length = pieces[0].shape
     count = len(pieces)
     blocks = info.shape[1]
-    operands = [*pieces, smap, tables, info, *phases, shift]
+    operands = [*pieces, smap, tables, info, *phases, shift, weights]
     return call(
         functools.partial(forward_kernel, pieces=count, chunk=chunk, slots=slots),
-        [(blocks // slots, 32, LANES)],
+        [(blocks // slots, 32, LANES), (slots, 8, LANES)],
         [
-            (count, 2, planes, part, length),
             (count, 2, planes, part, length),
             pltpu.VMEM(tables.shape, tables.dtype),
             pltpu.SMEM(info.shape, info.dtype),
@@ -303,14 +308,14 @@
             (2 * length * planes, length),
             (length * (length // chunk + 1), LANES),
             (blocks * 4, LANES),
-            pltpu.SemaphoreType.DMA((2 * count + 6,)),
+            pltpu.SemaphoreType.DMA((count + 6,)),
         ],
         operands,
         48 * planes * length**3,
         "forward",
-        hbm=range(len(operands)),
-        fixed=range(count, len(operands)),
-    )[0]
+        hbm=range(count, len(operands) - 1),
+        fixed=range(count, len(operands) - 1),
+    )
 
 
 def regrid_kernel(parts_ref, matrix_ref, out_ref):
@@ -551,15 +556,9 @@
     return call(finish_kernel, [x.shape] * 3, [], [total, x, r, p, normal], 10**7, "finish")
 
 
-def matrices_kernel(info_hbm, weights_ref, out_ref, held, info, sem, *, slots):
-    base = lax.axis_index("tile") * slots
-    copy = pltpu.make_async_copy(info_hbm, info, sem)
-    copy.start()
-    copy.wait()
-
+def matrices_kernel(weights_ref, turned_ref, out_ref, held, *, slots):
     def one(block, carry):
         w_x = weights_ref[block, 0]
-        w_y = weights_ref[block, 1]
         w_z = weights_ref[block, 2]
         twice = jnp.concatenate([w_x, w_x], axis=0)
         rolled = [twice] + [pltpu.roll(twice, 8 - d, 0) for d in range(1, 4)]
@@ -571,9 +570,7 @@
                 other = (f + d_z) % 4
                 along_z = w_z[f : f + 1] * w_z[other : other + 1]
                 right += [along * along_z for along in along_x]
-        turned = pltpu.roll(
-            jnp.concatenate([w_y, w_y], axis=0), info[1, base + block] % 4, 0
-        )[:4]
+        turned = turned_ref[block, 0:4]
         left = halves(jnp.concatenate([turned * turned[e : e + 1] for e in range(4)], axis=0))
         high, low = halves(jnp.concatenate(right, axis=0))
         both = dot_bf16(jnp.concatenate(left, axis=0), high, ((1,), (1,)))
@@ -600,15 +597,14 @@
     lax.fori_loop(0, 16, turn, 0, unroll=2)
 
 
-def block_matrices(info, weights):
+def block_matrices(weights, turned):
     return call(
         functools.partial(matrices_kernel, slots=weights.shape[0]),
         [(16 * LANES, LANES)],
-        [(16 * LANES, LANES), pltpu.SMEM(info.shape, info.dtype), pltpu.SemaphoreType.DMA],
-        [info, weights],
+        [(16 * LANES, LANES)],
+        [weights, turned],
         10**9,
         "matrices",
-        hbm=[0],
     )[0]
 
 
@@ -668,10 +664,12 @@
     )
     p_other += [other_core(piece) for piece in p_far]
     far_maps = [from_chip(rows, by) for by, rows in enumerate(far_rows, 1)]
-    partial = forward([image_p, *p_far, *p_other], smap, tables, info, phases, shift, chunk, slots)
-    partial, weights = lax.optimization_barrier((partial, kb_weights))
+    partial, turned = forward(
+        [image_p, *p_far, *p_other], smap, tables, info, phases, shift, kb_weights, chunk, slots
+    )
+    partial, turned = lax.optimization_barrier((partial, turned))
     parts = lax.all_to_all(partial, "tile", 0, 0, tiled=True)
-    done = regrid(parts, block_matrices(info, weights), chips * ntile)
+    done = regrid(parts, block_matrices(kb_weights, turned), chips * ntile)
     groups = [
         [at * ntile + t for at in range(ncoil) if at % 2 == k for t in range(ntile)]
         for k in range(2)

time: 74.4 us -> 74.2 us (level)
  transfers between devices with their start and end apart: 8 -> 8, of which waited for: 6 -> 6; matrix products, arithmetic and copies ran while one was open for 5% -> 5% of each run, Pallas kernels for 20% -> 19%
where the time goes in v7:
time: 74.2 us; the launch traced here: 73.7 us
  Pallas kernels  22.2 us (30%)
  waiting for transfers between devices  21.4 us (29%)
  starting transfers between devices  16.5 us (22%)
  blocking collectives  9.25 us (12%)
  other arithmetic  2.97 us (4%)
  between operations  0.83 us (1%)
    pallas_call x7, Pallas kernels, call(): pl.pallas_call(kernel, out_shape=[spaces[at](shape, jnp.float32) if at in...  20.7 us
    all_to_all x1, blocking collectives, shards(): total = lax.all_to_all(found, ('coil', 'tile'), 0, 0, tiled=True)  9.25 us
    all_to_all x1, waiting for transfers between devices, shards(): lax.all_to_all(done, ('coil', 'tile'), 0, 0, axis_index_groups=groups, ti...  6.96 us
    all_to_all x1, starting transfers between devices, shards(): lax.all_to_all(message(block_owner, owner_list), 'tile', 0, 0, tiled=True)  5.83 us
    all_to_all x1, waiting for transfers between devices, shards(): lax.all_to_all(message(block_owner, owner_list), 'tile', 0, 0, tiled=True)  5.18 us
    all_to_all x1, waiting for transfers between devices, shards(): parts = lax.all_to_all(partial, 'tile', 0, 0, tiled=True)  3.87 us
    all_to_all x1, starting transfers between devices, shards(): lax.all_to_all(done, ('coil', 'tile'), 0, 0, axis_index_groups=groups, ti...  3.53 us
    all_to_all x1, starting transfers between devices, shards(): parts = lax.all_to_all(partial, 'tile', 0, 0, tiled=True)  3.38 us
  transfers between devices with their start and end apart: 8, of which 6 were waited for; matrix products, arithmetic and copies ran while one was open for 5% of the time, Pallas kernels for 19%

profile of v7, /device:TPU:0, one launch (start us, length us, event | category | flops | bytes accessed | tf_op | source)
XLA Modules:
  0.0 73.7 jit_solution(17543375781806588937)
XLA Ops:
  0.6 0.5 collective-permute-start.1
  1.1 2.6 %collective-permute-start = (f32[2,16,32,128]{3,2,1,0:T(8,128)}, f32[2,16,32,128]{3,2,1,0:T(8,128)S(1)}, u32[]{:S(2)}, u32[]{:S(2)}) collective-permute-start(f32[2,16,32,128]{3,2,1,0:T(8,128)} %p_ref.1), channel_id=1, source_target_pairs={{0,16},{8,24},{16,0},{24,8},{1,17},{9,25},{17,1},{25,9},{2,18},{10... | collective-permute-start | bytes 1572872 | tf_op jit(solution)/shard_map/ppermute | solution.py:641
  3.7 1.4 %message.1 = s32[8,8,128]{2,1,0:T(8,128)} custom-call(s32[1,32]{1,0:T(1,128)} %bitcast.20, s32[3,1,8,16]{3,2,1,0:T(8,128)} %list_ref.1), custom_call_target="tpu_custom_call" | custom-call | tf_op jit(solution)/shard_map/message/pallas_call | solution.py:178
  5.1 5.8 %all-to-all-start = ((s32[8,8,128]{2,1,0:T(8,128)}), s32[8,8,128]{2,1,0:T(8,128)S(1)}, u32[]{:S(2)}, u32[]{:S(2)}) async-start(s32[8,8,128]{2,1,0:T(8,128)} %message.1), calls=%async_computation | async-start | bytes 65536 | tf_op jit(solution)/shard_map/all_to_all | solution.py:649
  11.0 0.0 copy-start
  11.0 0.0 copy-start.3
  11.0 0.1 fusion.4
  11.1 1.4 %map_rows.1 = f32[2,16,64,128]{3,2,1,0:T(8,128)S(1)} custom-call(f32[2,16,128,128]{3,2,1,0:T(8,128)} %bitcast.13), custom_call_target="tpu_custom_call" | custom-call | bytes 2097152 | tf_op jit(solution)/shard_map/map_rows/pallas_call | solution.py:95
  12.5 5.2 %all-to-all-done = s32[8,8,128]{2,1,0:T(8,128)S(1)} async-done(((s32[8,8,128]{2,1,0:T(8,128)}), s32[8,8,128]{2,1,0:T(8,128)S(1)}, u32[]{:S(2)}, u32[]{:S(2)}) %all-to-all-start) | async-done | bytes 32800 | tf_op jit(solution)/shard_map/all_to_all | solution.py:649
  17.7 0.1 multiply_reduce_fusion
  17.8 0.1 mul.81
  17.8 0.3 select_reduce_fusion.1
  18.1 0.1 iota_compare_fusion
  18.3 0.1 reshape.172
  18.4 0.1 copy.15
  18.4 0.1 broadcast_in_dim.50
  18.5 0.5 select_reduce_fusion
  19.0 0.1 mul.84
  19.1 0.1 squeeze.15
  19.2 0.1 squeeze.14
  19.3 0.6 pad_add_fusion.refs_6_.refs_1_
  19.9 1.3 %sine_multiply_fusion = (f32[256,128]{1,0:T(8,128)}, f32[256,128]{1,0:T(8,128)}) fusion(f32[128]{0:T(128)S(1)} %compare_select_fusion.3, s32[128]{0:T(128)S(1)} %fusion.5, s32[256]{0:T(256)S(1)} %mul.84), kind=kLoop, calls=%fused_computation.9 | loop fusion | flops 491520 | bytes 264192 | tf_op jit(solution)/shard_map/mul | solution.py:660
  21.2 0.0 collective-permute-done.refs_1_
  21.2 0.0 collective-permute-start.2
  21.2 0.6 collective-permute-start.3
  21.8 0.0 collective-permute-done.1.refs_2_
  21.8 1.3 %collective-permute-done.2.refs_3_ = f32[2,16,32,128]{3,2,1,0:T(8,128)S(1)} collective-permute-done((f32[2,16,32,128]{3,2,1,0:T(8,128)S(1)}, f32[2,16,32,128]{3,2,1,0:T(8,128)S(1)}, u32[]{:S(2)}, u32[]{:S(2)}) %collective-permute-start.2) | collective-permute-done | bytes 524320 | tf_op jit(solution)/shard_map/ppermute | solution.py:645
  23.1 0.0 copy-done
  23.1 0.0 copy-done.3
  23.1 6.6 %forward.1 = (f32[8,32,128]{2,1,0:T(8,128)}, f32[32,8,128]{2,1,0:T(8,128)S(1)}) custom-call(f32[2,16,32,128]{3,2,1,0:T(8,128)S(1)} %copy-done, f32[2,16,32,128]{3,2,1,0:T(8,128)S(1)} %collective-permute-done.refs_1_, f32[2,16,32,128]{3,2,1,0:T(8,128)S(1)} %collective-permute-done.1.refs_2_, f32[2,16,32,128]{3,2,1,0:T(8,128)S(1)} %collective-permute-done.2.refs_3_, ...), custom_call_target="tpu_custom_call" | custom-call | flops 1610612736 | bytes 5310464 | tf_op jit(solution)/shard_map/forward/pallas_call | solution.py:95
  29.7 3.4 %all-to-all-start.1 = ((f32[8,32,128]{2,1,0:T(8,128)}), f32[8,32,128]{2,1,0:T(8,128)S(1)}, u32[]{:S(2)}, u32[]{:S(2)}) async-start(f32[8,32,128]{2,1,0:T(8,128)} %get-tuple-element.18), calls=%async_computation.1 | async-start | bytes 262144 | tf_op jit(solution)/shard_map/all_to_all | solution.py:671
  33.1 3.6 %matrices.1.matrix_ref = f32[2048,128]{1,0:T(8,128)S(1)} custom-call(f32[32,3,4,128]{3,2,1,0:T(4,128)S(1)} %copy-done.3, f32[32,8,128]{2,1,0:T(8,128)S(1)} %get-tuple-element.19.turned_ref), custom_call_target="tpu_custom_call" | custom-call | flops 1000000000 | bytes 327680 | tf_op jit(solution)/shard_map/matrices/pallas_call | solution.py:95
  36.7 3.9 %all-to-all-done.1.parts_ref = f32[8,32,128]{2,1,0:T(8,128)S(1)} async-done(((f32[8,32,128]{2,1,0:T(8,128)}), f32[8,32,128]{2,1,0:T(8,128)S(1)}, u32[]{:S(2)}, u32[]{:S(2)}) %all-to-all-start.1) | async-done | bytes 131104 | tf_op jit(solution)/shard_map/all_to_all | solution.py:671
  40.6 0.9 %regrid.1 = f32[16,32,128]{2,1,0:T(8,128)} custom-call(f32[8,32,128]{2,1,0:T(8,128)S(1)} %all-to-all-done.1.parts_ref, f32[2048,128]{1,0:T(8,128)S(1)} %matrices.1.matrix_ref), custom_call_target="tpu_custom_call" | custom-call | flops 10000000 | bytes 1179648 | tf_op jit(solution)/shard_map/regrid/pallas_call | solution.py:95
  41.4 3.5 %all-to-all-start.2 = ((f32[16,32,128]{2,1,0:T(8,128)}), f32[16,32,128]{2,1,0:T(8,128)S(1)}, u32[]{:S(2)}, u32[]{:S(2)}) async-start(f32[16,32,128]{2,1,0:T(8,128)} %regrid.1), calls=%async_computation.2 | async-start | bytes 524288 | tf_op jit(solution)/shard_map/all_to_all | solution.py:677
  45.0 0.0 copy-start.1
  45.0 2.1 %collective-permute-done.3.refs_7_ = f32[2,16,64,128]{3,2,1,0:T(8,128)} collective-permute-done((f32[2,16,64,128]{3,2,1,0:T(8,128)S(1)}, f32[2,16,64,128]{3,2,1,0:T(8,128)}, u32[]{:S(2)}, u32[]{:S(2)}) %collective-permute-start.3) | collective-permute-done | bytes 1048608 | tf_op jit(solution)/shard_map/ppermute | solution.py:641
  47.1 7.0 %all-to-all-done.2.refs_0_ = f32[16,32,128]{2,1,0:T(8,128)S(1)} async-done(((f32[16,32,128]{2,1,0:T(8,128)}), f32[16,32,128]{2,1,0:T(8,128)S(1)}, u32[]{:S(2)}, u32[]{:S(2)}) %all-to-all-start.2) | async-done | bytes 262176 | tf_op jit(solution)/shard_map/all_to_all | solution.py:677
  54.1 6.7 %inverse.1 = (f32[2,16,32,128]{3,2,1,0:T(8,128)S(1)}, f32[2,16,32,128]{3,2,1,0:T(8,128)S(1)}) custom-call(f32[16,32,128]{2,1,0:T(8,128)S(1)} %all-to-all-done.2.refs_0_, s32[2,256]{1,0:T(2,128)} %pad_add_fusion.refs_6_.refs_1_, f32[256,128]{1,0:T(8,128)} %get-tuple-element.16.refs_7_.refs_2_, f32[256,128]{1,0:T(8,128)} %get-tuple-element.17.refs_8_.refs_3_, ...), custom_call_target="tpu_custom_call" | custom-call | flops 1610612736 | bytes 4327424 | tf_op jit(solution)/shard_map/inverse/pallas_call | solution.py:95
  60.8 0.0 copy-start.2
  60.8 0.1 collective-permute-start.4
  60.9 1.9 %collective-permute-done.4.refs_1_ = f32[2,16,32,128]{3,2,1,0:T(8,128)S(1)} collective-permute-done((f32[2,16,32,128]{3,2,1,0:T(8,128)S(1)}, f32[2,16,32,128]{3,2,1,0:T(8,128)S(1)}, u32[]{:S(2)}, u32[]{:S(2)}) %collective-permute-start.4) | collective-permute-done | bytes 524320 | tf_op jit(solution)/shard_map/ppermute | solution.py:645
  62.8 0.0 copy-done.1
  62.8 0.3 sums.1
  63.1 9.3 %all_to_all.26 = f32[32,1,128]{2,1,0:T(1,128)S(1)} all-to-all(f32[32,1,128]{2,1,0:T(1,128)S(1)} %bitcast.12), channel_id=1, replica_groups=mesh['coil'=4,'tile'=8] {'coil','tile'}, dimensions={0} | all-to-all | bytes 32768 | tf_op jit(solution)/shard_map/all_to_all | solution.py:684
  72.4 0.0 copy-done.2
  72.4 1.3 %finish.1 = (f32[2,16,32,128]{3,2,1,0:T(8,128)}, f32[2,16,32,128]{3,2,1,0:T(8,128)}, f32[2,16,32,128]{3,2,1,0:T(8,128)}) custom-call(f32[32,128]{1,0:T(8,128)S(1)} %bitcast.11, f32[2,16,32,128]{3,2,1,0:T(8,128)S(1)} %copy-done.2, f32[2,16,32,128]{3,2,1,0:T(8,128)S(1)} %copy-done.1, f32[2,16,32,128]{3,2,1,0:T(8,128)S(1)} %copy-done, ...), custom_call_target="tpu_custom_call" | custom-call | flops 10000000 | bytes 2113536 | tf_op jit(solution)/shard_map/finish/pallas_call | solution.py:95
  (7 shorter events, 0.0 us)
Async XLA Ops:
  0.6 21.2 %collective-permute-start.1 = (f32[2,16,32,128]{3,2,1,0:T(8,128)}, f32[2,16,32,128]{3,2,1,0:T(8,128)S(1)}, u32[]{:S(2)}, u32[]{:S(2)}) collective-permute-start(f32[2,16,32,128]{3,2,1,0:T(8,128)} %p_ref.1), channel_id=1, source_target_pairs={{0,8},{8,0},{16,24},{24,16},{1,9},{9,1},{17,25},{25,17},{2,10},{10... | collective-permute-start | bytes 1572872 | tf_op jit(solution)/shard_map/ppermute | solution.py:645
  1.1 20.0 %collective-permute-start = (f32[2,16,32,128]{3,2,1,0:T(8,128)}, f32[2,16,32,128]{3,2,1,0:T(8,128)S(1)}, u32[]{:S(2)}, u32[]{:S(2)}) collective-permute-start(f32[2,16,32,128]{3,2,1,0:T(8,128)} %p_ref.1), channel_id=1, source_target_pairs={{0,16},{8,24},{16,0},{24,8},{1,17},{9,25},{17,1},{25,9},{2,18},{10... | collective-permute-start | bytes 1572872 | tf_op jit(solution)/shard_map/ppermute | solution.py:641
  5.1 12.5 %all-to-all-start = ((s32[8,8,128]{2,1,0:T(8,128)}), s32[8,8,128]{2,1,0:T(8,128)S(1)}, u32[]{:S(2)}, u32[]{:S(2)}) async-start(s32[8,8,128]{2,1,0:T(8,128)} %message.1), calls=%async_computation | async-start | bytes 65536 | tf_op jit(solution)/shard_map/all_to_all | solution.py:649
  11.0 12.1 %copy-start = (f32[2,16,32,128]{3,2,1,0:T(8,128)S(1)}, f32[2,16,32,128]{3,2,1,0:T(8,128)}, u32[]{:S(2)}) copy-start(f32[2,16,32,128]{3,2,1,0:T(8,128)} %p_ref.1) | copy-start | bytes 1572868
  11.0 12.1 %copy-start.3 = (f32[32,3,4,128]{3,2,1,0:T(4,128)S(1)}, f32[32,3,4,128]{3,2,1,0:T(4,128)}, u32[]{:S(2)}) copy-start(f32[32,3,4,128]{3,2,1,0:T(4,128)} %weights_ref.1) | copy-start | bytes 589828
  21.2 1.9 %collective-permute-start.2 = (f32[2,16,32,128]{3,2,1,0:T(8,128)S(1)}, f32[2,16,32,128]{3,2,1,0:T(8,128)S(1)}, u32[]{:S(2)}, u32[]{:S(2)}) collective-permute-start(f32[2,16,32,128]{3,2,1,0:T(8,128)S(1)} %collective-permute-done.refs_1_), channel_id=1, source_target_pairs={{0,8},{8,0},{16,24},{24,16},{1,9},{9,1},{17,25},{25,17},{2,10},{10... | collective-permute-start | bytes 1572872 | tf_op jit(solution)/shard_map/ppermute | solution.py:645
  21.2 25.9 %collective-permute-start.3 = (f32[2,16,64,128]{3,2,1,0:T(8,128)S(1)}, f32[2,16,64,128]{3,2,1,0:T(8,128)}, u32[]{:S(2)}, u32[]{:S(2)}) collective-permute-start(f32[2,16,64,128]{3,2,1,0:T(8,128)S(1)} %map_rows.1), channel_id=1, source_target_pairs={{0,16},{8,24},{16,0},{24,8},{1,17},{9,25},{17,1},{25,9},{2,18},{10... | collective-permute-start | bytes 3145736 | tf_op jit(solution)/shard_map/ppermute | solution.py:641
  29.7 10.9 %all-to-all-start.1 = ((f32[8,32,128]{2,1,0:T(8,128)}), f32[8,32,128]{2,1,0:T(8,128)S(1)}, u32[]{:S(2)}, u32[]{:S(2)}) async-start(f32[8,32,128]{2,1,0:T(8,128)} %get-tuple-element.18), calls=%async_computation.1 | async-start | bytes 262144 | tf_op jit(solution)/shard_map/all_to_all | solution.py:671
  41.4 12.7 %all-to-all-start.2 = ((f32[16,32,128]{2,1,0:T(8,128)}), f32[16,32,128]{2,1,0:T(8,128)S(1)}, u32[]{:S(2)}, u32[]{:S(2)}) async-start(f32[16,32,128]{2,1,0:T(8,128)} %regrid.1), calls=%async_computation.2 | async-start | bytes 524288 | tf_op jit(solution)/shard_map/all_to_all | solution.py:677
  45.0 17.8 %copy-start.1 = (f32[2,16,32,128]{3,2,1,0:T(8,128)S(1)}, f32[2,16,32,128]{3,2,1,0:T(8,128)}, u32[]{:S(2)}) copy-start(f32[2,16,32,128]{3,2,1,0:T(8,128)} %r_ref.1) | copy-start | bytes 1572868
  60.8 11.5 %copy-start.2 = (f32[2,16,32,128]{3,2,1,0:T(8,128)S(1)}, f32[2,16,32,128]{3,2,1,0:T(8,128)}, u32[]{:S(2)}) copy-start(f32[2,16,32,128]{3,2,1,0:T(8,128)} %x_ref.1) | copy-start | bytes 1572868
  60.8 2.0 %collective-permute-start.4 = (f32[2,16,32,128]{3,2,1,0:T(8,128)S(1)}, f32[2,16,32,128]{3,2,1,0:T(8,128)S(1)}, u32[]{:S(2)}, u32[]{:S(2)}) collective-permute-start(f32[2,16,32,128]{3,2,1,0:T(8,128)S(1)} %get-tuple-element.22), channel_id=1, source_target_pairs={{0,8},{8,0},{16,24},{24,16},{1,9},{9,1},{17,25},{25,17},{2,10},{10... | collective-permute-start | bytes 1572872 | tf_op jit(solution)/shard_map/ppermute | solution.py:645

commit v8 on v7

--- a/solution.py
+++ b/solution.py
@@ -645,8 +645,9 @@
         return lax.ppermute(values, "coil", pairs)
 
     p_same = [image_p] + [from_chip(image_p, by) for by in range(1, chips)]
-    p_other = [other_core(image_p)]
-    gathered = lax.all_to_all(message(block_owner, owner_list), "tile", 0, 0, tiled=True)
+    sent, p_later = lax.optimization_barrier((message(block_owner, owner_list), image_p))
+    p_other = [other_core(p_later)]
+    gathered = lax.all_to_all(sent, "tile", 0, 0, tiled=True)
     far_rows = map_rows(smap, chips)
     off_x, off_y, off_z = block_offsets(gathered, slots, ntile, capacity)
     info = jnp.stack(

time: 74.2 us -> 74.1 us (level)
  no operation moved by 1% of the time
where the time goes in v8:
time: 74.1 us; the launch traced here: 73.6 us
  Pallas kernels  22.1 us (30%)
  waiting for transfers between devices  21.3 us (29%)
  starting transfers between devices  16.5 us (22%)
  blocking collectives  9.25 us (12%)
  other arithmetic  2.97 us (4%)
  between operations  0.84 us (1%)
    pallas_call x7, Pallas kernels, call(): pl.pallas_call(kernel, out_shape=[spaces[at](shape, jnp.float32) if at in...  20.7 us
    all_to_all x1, blocking collectives, shards(): total = lax.all_to_all(found, ('coil', 'tile'), 0, 0, tiled=True)  9.25 us
    all_to_all x1, waiting for transfers between devices, shards(): lax.all_to_all(done, ('coil', 'tile'), 0, 0, axis_index_groups=groups, ti...  6.95 us
    all_to_all x1, starting transfers between devices, shards(): gathered = lax.all_to_all(sent, 'tile', 0, 0, tiled=True)  5.83 us
    all_to_all x1, waiting for transfers between devices, shards(): gathered = lax.all_to_all(sent, 'tile', 0, 0, tiled=True)  5.13 us
    all_to_all x1, waiting for transfers between devices, shards(): parts = lax.all_to_all(partial, 'tile', 0, 0, tiled=True)  3.87 us
    ppermute x2, starting transfers between devices, from_chip(): return lax.ppermute(values, 'coil', pairs)  3.6 us
    all_to_all x1, starting transfers between devices, shards(): lax.all_to_all(done, ('coil', 'tile'), 0, 0, axis_index_groups=groups, ti...  3.53 us
  transfers between devices with their start and end apart: 8, of which 6 were waited for; matrix products, arithmetic and copies ran while one was open for 5% of the time, Pallas kernels for 19%

profile of v8, /device:TPU:0, one launch (start us, length us, event | category | flops | bytes accessed | tf_op | source)
XLA Modules:
  0.0 73.6 jit_solution(11242403620553557916)
XLA Ops:
  0.6 3.0 %collective-permute-start = (f32[2,16,32,128]{3,2,1,0:T(8,128)}, f32[2,16,32,128]{3,2,1,0:T(8,128)S(1)}, u32[]{:S(2)}, u32[]{:S(2)}) collective-permute-start(f32[2,16,32,128]{3,2,1,0:T(8,128)} %p_ref.1), channel_id=1, source_target_pairs={{0,16},{8,24},{16,0},{24,8},{1,17},{9,25},{17,1},{25,9},{2,18},{10... | collective-permute-start | bytes 1572872 | tf_op jit(solution)/shard_map/ppermute | solution.py:641
  3.6 1.4 %message.1 = s32[8,8,128]{2,1,0:T(8,128)} custom-call(s32[1,32]{1,0:T(1,128)} %bitcast.20, s32[3,1,8,16]{3,2,1,0:T(8,128)} %list_ref.1), custom_call_target="tpu_custom_call" | custom-call | tf_op jit(solution)/shard_map/message/pallas_call | solution.py:178
  5.1 5.8 %all-to-all-start = ((s32[8,8,128]{2,1,0:T(8,128)}), s32[8,8,128]{2,1,0:T(8,128)S(1)}, u32[]{:S(2)}, u32[]{:S(2)}) async-start(s32[8,8,128]{2,1,0:T(8,128)} %message.1), calls=%async_computation | async-start | bytes 65536 | tf_op jit(solution)/shard_map/all_to_all | solution.py:650
  10.9 0.0 copy-start
  10.9 0.0 copy-start.3
  10.9 0.1 collective-permute-start.1
  11.0 0.1 fusion.4
  11.1 1.3 %map_rows.1 = f32[2,16,64,128]{3,2,1,0:T(8,128)S(1)} custom-call(f32[2,16,128,128]{3,2,1,0:T(8,128)} %bitcast.13), custom_call_target="tpu_custom_call" | custom-call | bytes 2097152 | tf_op jit(solution)/shard_map/map_rows/pallas_call | solution.py:95
  12.5 5.1 %all-to-all-done = s32[8,8,128]{2,1,0:T(8,128)S(1)} async-done(((s32[8,8,128]{2,1,0:T(8,128)}), s32[8,8,128]{2,1,0:T(8,128)S(1)}, u32[]{:S(2)}, u32[]{:S(2)}) %all-to-all-start) | async-done | bytes 32800 | tf_op jit(solution)/shard_map/all_to_all | solution.py:650
  17.6 0.1 multiply_reduce_fusion
  17.7 0.1 mul.81
  17.8 0.3 select_reduce_fusion.1
  18.1 0.1 iota_compare_fusion
  18.2 0.1 reshape.172
  18.3 0.1 copy.15
  18.4 0.1 broadcast_in_dim.50
  18.5 0.5 select_reduce_fusion
  18.9 0.1 mul.84
  19.0 0.1 squeeze.15
  19.1 0.1 squeeze.14
  19.2 0.6 pad_add_fusion.refs_6_.refs_1_
  19.8 1.3 %sine_multiply_fusion = (f32[256,128]{1,0:T(8,128)}, f32[256,128]{1,0:T(8,128)}) fusion(f32[128]{0:T(128)S(1)} %compare_select_fusion.3, s32[128]{0:T(128)S(1)} %fusion.5, s32[256]{0:T(256)S(1)} %mul.84), kind=kLoop, calls=%fused_computation.9 | loop fusion | flops 491520 | bytes 264192 | tf_op jit(solution)/shard_map/mul | solution.py:661
  21.1 0.0 collective-permute-done.refs_1_
  21.1 0.0 collective-permute-start.2
  21.1 0.6 collective-permute-start.3
  21.7 0.0 collective-permute-done.1.refs_2_
  21.7 1.3 %collective-permute-done.2.refs_3_ = f32[2,16,32,128]{3,2,1,0:T(8,128)S(1)} collective-permute-done((f32[2,16,32,128]{3,2,1,0:T(8,128)S(1)}, f32[2,16,32,128]{3,2,1,0:T(8,128)S(1)}, u32[]{:S(2)}, u32[]{:S(2)}) %collective-permute-start.2) | collective-permute-done | bytes 524320 | tf_op jit(solution)/shard_map/ppermute | solution.py:645
  23.0 0.0 copy-done
  23.0 0.0 copy-done.3
  23.0 6.5 %forward.1 = (f32[8,32,128]{2,1,0:T(8,128)}, f32[32,8,128]{2,1,0:T(8,128)S(1)}) custom-call(f32[2,16,32,128]{3,2,1,0:T(8,128)S(1)} %copy-done, f32[2,16,32,128]{3,2,1,0:T(8,128)S(1)} %collective-permute-done.refs_1_, f32[2,16,32,128]{3,2,1,0:T(8,128)S(1)} %collective-permute-done.1.refs_2_, f32[2,16,32,128]{3,2,1,0:T(8,128)S(1)} %collective-permute-done.2.refs_3_, ...), custom_call_target="tpu_custom_call" | custom-call | flops 1610612736 | bytes 5310464 | tf_op jit(solution)/shard_map/forward/pallas_call | solution.py:95
  29.6 3.4 %all-to-all-start.1 = ((f32[8,32,128]{2,1,0:T(8,128)}), f32[8,32,128]{2,1,0:T(8,128)S(1)}, u32[]{:S(2)}, u32[]{:S(2)}) async-start(f32[8,32,128]{2,1,0:T(8,128)} %get-tuple-element.22), calls=%async_computation.1 | async-start | bytes 262144 | tf_op jit(solution)/shard_map/all_to_all | solution.py:672
  33.0 3.6 %matrices.1.matrix_ref = f32[2048,128]{1,0:T(8,128)S(1)} custom-call(f32[32,3,4,128]{3,2,1,0:T(4,128)S(1)} %copy-done.3, f32[32,8,128]{2,1,0:T(8,128)S(1)} %get-tuple-element.23.turned_ref), custom_call_target="tpu_custom_call" | custom-call | flops 1000000000 | bytes 327680 | tf_op jit(solution)/shard_map/matrices/pallas_call | solution.py:95
  36.6 3.9 %all-to-all-done.1.parts_ref = f32[8,32,128]{2,1,0:T(8,128)S(1)} async-done(((f32[8,32,128]{2,1,0:T(8,128)}), f32[8,32,128]{2,1,0:T(8,128)S(1)}, u32[]{:S(2)}, u32[]{:S(2)}) %all-to-all-start.1) | async-done | bytes 131104 | tf_op jit(solution)/shard_map/all_to_all | solution.py:672
  40.5 0.9 %regrid.1 = f32[16,32,128]{2,1,0:T(8,128)} custom-call(f32[8,32,128]{2,1,0:T(8,128)S(1)} %all-to-all-done.1.parts_ref, f32[2048,128]{1,0:T(8,128)S(1)} %matrices.1.matrix_ref), custom_call_target="tpu_custom_call" | custom-call | flops 10000000 | bytes 1179648 | tf_op jit(solution)/shard_map/regrid/pallas_call | solution.py:95
  41.4 3.5 %all-to-all-start.2 = ((f32[16,32,128]{2,1,0:T(8,128)}), f32[16,32,128]{2,1,0:T(8,128)S(1)}, u32[]{:S(2)}, u32[]{:S(2)}) async-start(f32[16,32,128]{2,1,0:T(8,128)} %regrid.1), calls=%async_computation.2 | async-start | bytes 524288 | tf_op jit(solution)/shard_map/all_to_all | solution.py:678
  44.9 0.0 copy-start.1
  44.9 2.1 %collective-permute-done.3.refs_7_ = f32[2,16,64,128]{3,2,1,0:T(8,128)} collective-permute-done((f32[2,16,64,128]{3,2,1,0:T(8,128)S(1)}, f32[2,16,64,128]{3,2,1,0:T(8,128)}, u32[]{:S(2)}, u32[]{:S(2)}) %collective-permute-start.3) | collective-permute-done | bytes 1048608 | tf_op jit(solution)/shard_map/ppermute | solution.py:641
  47.1 6.9 %all-to-all-done.2.refs_0_ = f32[16,32,128]{2,1,0:T(8,128)S(1)} async-done(((f32[16,32,128]{2,1,0:T(8,128)}), f32[16,32,128]{2,1,0:T(8,128)S(1)}, u32[]{:S(2)}, u32[]{:S(2)}) %all-to-all-start.2) | async-done | bytes 262176 | tf_op jit(solution)/shard_map/all_to_all | solution.py:678
  54.0 6.7 %inverse.1 = (f32[2,16,32,128]{3,2,1,0:T(8,128)S(1)}, f32[2,16,32,128]{3,2,1,0:T(8,128)S(1)}) custom-call(f32[16,32,128]{2,1,0:T(8,128)S(1)} %all-to-all-done.2.refs_0_, s32[2,256]{1,0:T(2,128)} %pad_add_fusion.refs_6_.refs_1_, f32[256,128]{1,0:T(8,128)} %get-tuple-element.20.refs_7_.refs_2_, f32[256,128]{1,0:T(8,128)} %get-tuple-element.21.refs_8_.refs_3_, ...), custom_call_target="tpu_custom_call" | custom-call | flops 1610612736 | bytes 4327424 | tf_op jit(solution)/shard_map/inverse/pallas_call | solution.py:95
  60.7 0.0 copy-start.2
  60.8 0.1 collective-permute-start.4
  60.8 1.9 %collective-permute-done.4.refs_1_ = f32[2,16,32,128]{3,2,1,0:T(8,128)S(1)} collective-permute-done((f32[2,16,32,128]{3,2,1,0:T(8,128)S(1)}, f32[2,16,32,128]{3,2,1,0:T(8,128)S(1)}, u32[]{:S(2)}, u32[]{:S(2)}) %collective-permute-start.4) | collective-permute-done | bytes 524320 | tf_op jit(solution)/shard_map/ppermute | solution.py:645
  62.7 0.0 copy-done.1
  62.7 0.3 sums.1
  63.0 9.3 %all_to_all.26 = f32[32,1,128]{2,1,0:T(1,128)S(1)} all-to-all(f32[32,1,128]{2,1,0:T(1,128)S(1)} %bitcast.12), channel_id=1, replica_groups=mesh['coil'=4,'tile'=8] {'coil','tile'}, dimensions={0} | all-to-all | bytes 32768 | tf_op jit(solution)/shard_map/all_to_all | solution.py:685
  72.3 0.0 copy-done.2
  72.3 1.3 %finish.1 = (f32[2,16,32,128]{3,2,1,0:T(8,128)}, f32[2,16,32,128]{3,2,1,0:T(8,128)}, f32[2,16,32,128]{3,2,1,0:T(8,128)}) custom-call(f32[32,128]{1,0:T(8,128)S(1)} %bitcast.11, f32[2,16,32,128]{3,2,1,0:T(8,128)S(1)} %copy-done.2, f32[2,16,32,128]{3,2,1,0:T(8,128)S(1)} %copy-done.1, f32[2,16,32,128]{3,2,1,0:T(8,128)S(1)} %copy-done, ...), custom_call_target="tpu_custom_call" | custom-call | flops 10000000 | bytes 2113536 | tf_op jit(solution)/shard_map/finish/pallas_call | solution.py:95
  (7 shorter events, 0.0 us)
Async XLA Ops:
  0.6 20.5 %collective-permute-start = (f32[2,16,32,128]{3,2,1,0:T(8,128)}, f32[2,16,32,128]{3,2,1,0:T(8,128)S(1)}, u32[]{:S(2)}, u32[]{:S(2)}) collective-permute-start(f32[2,16,32,128]{3,2,1,0:T(8,128)} %p_ref.1), channel_id=1, source_target_pairs={{0,16},{8,24},{16,0},{24,8},{1,17},{9,25},{17,1},{25,9},{2,18},{10... | collective-permute-start | bytes 1572872 | tf_op jit(solution)/shard_map/ppermute | solution.py:641
  5.1 12.5 %all-to-all-start = ((s32[8,8,128]{2,1,0:T(8,128)}), s32[8,8,128]{2,1,0:T(8,128)S(1)}, u32[]{:S(2)}, u32[]{:S(2)}) async-start(s32[8,8,128]{2,1,0:T(8,128)} %message.1), calls=%async_computation | async-start | bytes 65536 | tf_op jit(solution)/shard_map/all_to_all | solution.py:650
  10.9 12.1 %copy-start = (f32[2,16,32,128]{3,2,1,0:T(8,128)S(1)}, f32[2,16,32,128]{3,2,1,0:T(8,128)}, u32[]{:S(2)}) copy-start(f32[2,16,32,128]{3,2,1,0:T(8,128)} %p_ref.1) | copy-start | bytes 1572868
  10.9 12.1 %copy-start.3 = (f32[32,3,4,128]{3,2,1,0:T(4,128)S(1)}, f32[32,3,4,128]{3,2,1,0:T(4,128)}, u32[]{:S(2)}) copy-start(f32[32,3,4,128]{3,2,1,0:T(4,128)} %weights_ref.1) | copy-start | bytes 589828
  10.9 10.8 %collective-permute-start.1 = (f32[2,16,32,128]{3,2,1,0:T(8,128)}, f32[2,16,32,128]{3,2,1,0:T(8,128)S(1)}, u32[]{:S(2)}, u32[]{:S(2)}) collective-permute-start(f32[2,16,32,128]{3,2,1,0:T(8,128)} %p_ref.1), channel_id=1, source_target_pairs={{0,8},{8,0},{16,24},{24,16},{1,9},{9,1},{17,25},{25,17},{2,10},{10... | collective-permute-start | bytes 1572872 | tf_op jit(solution)/shard_map/ppermute | solution.py:645
  21.1 1.9 %collective-permute-start.2 = (f32[2,16,32,128]{3,2,1,0:T(8,128)S(1)}, f32[2,16,32,128]{3,2,1,0:T(8,128)S(1)}, u32[]{:S(2)}, u32[]{:S(2)}) collective-permute-start(f32[2,16,32,128]{3,2,1,0:T(8,128)S(1)} %collective-permute-done.refs_1_), channel_id=1, source_target_pairs={{0,8},{8,0},{16,24},{24,16},{1,9},{9,1},{17,25},{25,17},{2,10},{10... | collective-permute-start | bytes 1572872 | tf_op jit(solution)/shard_map/ppermute | solution.py:645
  21.1 25.9 %collective-permute-start.3 = (f32[2,16,64,128]{3,2,1,0:T(8,128)S(1)}, f32[2,16,64,128]{3,2,1,0:T(8,128)}, u32[]{:S(2)}, u32[]{:S(2)}) collective-permute-start(f32[2,16,64,128]{3,2,1,0:T(8,128)S(1)} %map_rows.1), channel_id=1, source_target_pairs={{0,16},{8,24},{16,0},{24,8},{1,17},{9,25},{17,1},{25,9},{2,18},{10... | collective-permute-start | bytes 3145736 | tf_op jit(solution)/shard_map/ppermute | solution.py:641
  29.6 10.9 %all-to-all-start.1 = ((f32[8,32,128]{2,1,0:T(8,128)}), f32[8,32,128]{2,1,0:T(8,128)S(1)}, u32[]{:S(2)}, u32[]{:S(2)}) async-start(f32[8,32,128]{2,1,0:T(8,128)} %get-tuple-element.22), calls=%async_computation.1 | async-start | bytes 262144 | tf_op jit(solution)/shard_map/all_to_all | solution.py:672
  41.4 12.7 %all-to-all-start.2 = ((f32[16,32,128]{2,1,0:T(8,128)}), f32[16,32,128]{2,1,0:T(8,128)S(1)}, u32[]{:S(2)}, u32[]{:S(2)}) async-start(f32[16,32,128]{2,1,0:T(8,128)} %regrid.1), calls=%async_computation.2 | async-start | bytes 524288 | tf_op jit(solution)/shard_map/all_to_all | solution.py:678
  44.9 17.8 %copy-start.1 = (f32[2,16,32,128]{3,2,1,0:T(8,128)S(1)}, f32[2,16,32,128]{3,2,1,0:T(8,128)}, u32[]{:S(2)}) copy-start(f32[2,16,32,128]{3,2,1,0:T(8,128)} %r_ref.1) | copy-start | bytes 1572868
  60.7 11.5 %copy-start.2 = (f32[2,16,32,128]{3,2,1,0:T(8,128)S(1)}, f32[2,16,32,128]{3,2,1,0:T(8,128)}, u32[]{:S(2)}) copy-start(f32[2,16,32,128]{3,2,1,0:T(8,128)} %x_ref.1) | copy-start | bytes 1572868
  60.8 2.0 %collective-permute-start.4 = (f32[2,16,32,128]{3,2,1,0:T(8,128)S(1)}, f32[2,16,32,128]{3,2,1,0:T(8,128)S(1)}, u32[]{:S(2)}, u32[]{:S(2)}) collective-permute-start(f32[2,16,32,128]{3,2,1,0:T(8,128)S(1)} %get-tuple-element.26), channel_id=1, source_target_pairs={{0,8},{8,0},{16,24},{24,16},{1,9},{9,1},{17,25},{25,17},{2,10},{10... | collective-permute-start | bytes 1572872 | tf_op jit(solution)/shard_map/ppermute | solution.py:645
